TPU v7x, 32 devices: a whole 2x2x4 slice. The times are simulated.
32 devices in a mesh: group: 2 (over y), dev: 16 (over z, x, core).
Axes of the slice: x: 2, y: 2, z: 4, core: 2. Of those that a mesh axis runs over, the one named last changes fastest.
Arguments:
- forces: float32 [3, 65536], P(None, ('group', 'dev')), may hold values from -4 to 4
- stencil_start: int32 [3, 65536], P(None, ('group', 'dev')), may hold values from 0 to 1023, as said below
- fraction: float32 [3, 65536], P(None, ('group', 'dev')), may hold values from 0 to 1
- tile_pairs: int32 [1536, 2], P(('group', 'dev')), may hold values from 0 to 15, as said below
- pair_count: int32 [32], P(('group', 'dev')), may hold values from 1 to 48, as said below
Outputs:
- velocity: float32 [3, 65536], P(None, ('group', 'dev'))
Inputs may be any that keep to these rules, and one draw needn't show every extreme that they name: `stencil_start`: along the first dimension, a point of block b = p // 2048 starts in planes b * 32 to (b + 1) * 32 - 1; along the others it lies in 0 to 127 and 0 to 127. `tile_pairs`: tile numbers are local to the device's block of 2048 points. `pair_count`: the live slots are the first ones of each device's list; some device has all 48 live.
All inputs are finite; a program needn't handle non-finite values.
Results may differ from a plain program's by a relative error of at most 0.0003.
Values sent between devices are 32-bit elements; how exact they have to be, the bound alone decides.
No kernel may reach another device: no remote copies, remote signals or barrier semaphores. Data moves between devices by JAX's collectives and lax.ppermute only.
A program may use at most 128 MiB of HBM per device.

v0:
```python
import functools

import jax
import jax.numpy as jnp
import ml_dtypes
import numpy as np
from jax import lax
from jax.experimental import pallas as pl
from jax.experimental.pallas import tpu as pltpu
from jax.sharding import PartitionSpec as P

NX = 1024
NY = 128
NZ = 128

TWO_PI = 6.283185307179586
EPS_SQ = 1.0
RANGE_SQ = 16.0
NEAR_SCALE = 0.25

LANES = 128
SPREAD_LIMIT = 24 * 2**20
SOLVE_LIMIT = 20 * 2**20
GATHER_LIMIT = 20 * 2**20
KEEP_BYTES = 32 * 2**20
KZ = 16
BF16 = jnp.bfloat16
F32 = jnp.float32


def wrapped(gap, length):
    gap = jnp.where(gap > length / 2, gap - length, gap)
    return jnp.where(gap < -length / 2, gap + length, gap)


def near_kernel(pairs_ref, count_ref, forces_ref, start_ref, fraction_ref, out_ref, columns):
    tiles = out_ref.shape[1] // LANES
    out_ref[...] = jnp.zeros_like(out_ref)
    for tile in range(tiles):
        at = slice(tile * LANES, (tile + 1) * LANES)
        nine = jnp.concatenate(
            [
                start_ref[:, at].astype(F32),
                fraction_ref[:, at],
                forces_ref[:, at],
                jnp.zeros((7, LANES), F32),
            ],
            axis=0,
        )
        columns[at] = nine.T

    @pl.loop(0, count_ref[0])
    def _(slot):
        target = pl.ds(pl.multiple_of(pairs_ref[2 * slot] * LANES, LANES), LANES)
        base = pl.multiple_of(pairs_ref[2 * slot + 1] * LANES, LANES)
        start = start_ref[:, target].astype(F32)
        fraction = fraction_ref[:, target]
        sums = [jnp.zeros((8, LANES), F32) for _ in range(3)]
        for row in range(0, LANES, 8):
            source = columns[pl.ds(base + row, 8)]
            gaps = []
            for axis, length in enumerate((None, NY, NZ)):
                gap = start[axis : axis + 1] - source[:, axis : axis + 1]
                if length is not None:
                    gap = wrapped(gap, float(length))
                gaps.append(gap + (fraction[axis : axis + 1] - source[:, 3 + axis : 4 + axis]))
            pulled = [source[:, 6 + axis : 7 + axis] for axis in range(3)]
            distance = gaps[0] * gaps[0] + gaps[1] * gaps[1] + gaps[2] * gaps[2]
            inverse = lax.rsqrt(distance + EPS_SQ)
            fall = NEAR_SCALE * jnp.exp(distance * (-1.0 / RANGE_SQ)) * (inverse * inverse * inverse)
            diagonal = (distance + 2.0 * EPS_SQ) * fall
            along = fall * (gaps[0] * pulled[0] + gaps[1] * pulled[1] + gaps[2] * pulled[2])
            sums = [sums[i] + (diagonal * pulled[i] + gaps[i] * along) for i in range(3)]
        out_ref[:, target] += jnp.concatenate(
            [jnp.sum(value, axis=0, keepdims=True) for value in sums], axis=0
        )


def near_field(forces, stencil_start, fraction, tile_pairs, pair_count):
    smem = pl.BlockSpec(memory_space=pltpu.SMEM)
    vmem = pl.BlockSpec(memory_space=pltpu.VMEM)
    points = forces.shape[1]
    slots = tile_pairs.shape[0]
    return pl.pallas_call(
        near_kernel,
        in_specs=[smem, smem, vmem, vmem, vmem],
        out_specs=vmem,
        out_shape=jax.ShapeDtypeStruct((3, points), F32),
        scratch_shapes=[pltpu.VMEM((points, 16), F32)],
        compiler_params=pltpu.CompilerParams(vmem_limit_bytes=8 * 2**20),
        cost_estimate=pl.CostEstimate(
            flops=slots * LANES * LANES * 6000, bytes_accessed=points * 48, transcendentals=0
        ),
        name="near",
    )(tile_pairs.reshape(-1), pair_count, forces, stencil_start, fraction)


def pack_kernel(first_ref, forces_ref, start_ref, fraction_ref, out_ref):
    points = forces_ref.shape[1]
    piece = points // 8
    start = start_ref[...]
    out_ref[0, 0:3, 0:points] = forces_ref[...]
    out_ref[0, 3:4, 0:points] = (start[0:1] - first_ref[0]).astype(F32)
    out_ref[0, 4:6, 0:points] = start[1:3].astype(F32)
    out_ref[0, 6:8, 0:points] = fraction_ref[0:2]
    for row in range(8):
        out_ref[0, row : row + 1, points:] = fraction_ref[2:3, row * piece : (row + 1) * piece]


def pack(first, forces, stencil_start, fraction):
    vmem = pl.BlockSpec(memory_space=pltpu.VMEM)
    points = forces.shape[1]
    return pl.pallas_call(
        pack_kernel,
        in_specs=[pl.BlockSpec(memory_space=pltpu.SMEM), vmem, vmem, vmem],
        out_specs=vmem,
        out_shape=jax.ShapeDtypeStruct((1, 8, points + points // 8), F32),
        name="pack",
    )(first, forces, stencil_start, fraction)


def unpack(values):
    points = values.shape[1] // 9 * 8
    pieces = [values[row : row + 1, points:] for row in range(8)]
    return values[:, :points], jnp.concatenate(pieces, axis=1)


def split(value):
    high = value.astype(BF16)
    low = (value - high.astype(F32)).astype(BF16)
    return high, low


def spline_weights(fraction):
    square = fraction * fraction
    cube = square * fraction
    rest = 1.0 - fraction
    return [
        rest * rest * rest * (1.0 / 6.0),
        (3.0 * cube - 6.0 * square + 4.0) * (1.0 / 6.0),
        (-3.0 * cube + 3.0 * square + 3.0 * fraction + 1.0) * (1.0 / 6.0),
        cube * (1.0 / 6.0),
    ]


def cos_sin_turns(turns):
    part = turns - jnp.floor(turns + 0.5)
    half = part * (0.5 * TWO_PI)
    square = half * half
    sine = half * (
        1.0
        + square
        * (
            -1.0 / 6.0
            + square
            * (1.0 / 120.0 + square * (-1.0 / 5040.0 + square * (1.0 / 362880.0 + square * (-1.0 / 39916800.0))))
        )
    )
    cosine = 1.0 + square * (
        -0.5
        + square
        * (
            1.0 / 24.0
            + square
            * (-1.0 / 720.0 + square * (1.0 / 40320.0 + square * (-1.0 / 3628800.0 + square * (1.0 / 479001600.0))))
        )
    )
    return 1.0 - 2.0 * sine * sine, 2.0 * sine * cosine


def widen(table, width):
    return jnp.concatenate([table] * (width // LANES), axis=1)


def mode_rows(start, weights, modes, length):
    width = start.shape[1]
    cosine, sine = cos_sin_turns(widen(modes[0], width) * start * (1.0 / length))
    sum_cos = weights[0] + weights[1] * widen(modes[1], width)
    sum_sin = weights[1] * widen(modes[2], width)
    sum_cos = sum_cos + weights[2] * widen(modes[3], width) + weights[3] * widen(modes[5], width)
    sum_sin = sum_sin + weights[2] * widen(modes[4], width) + weights[3] * widen(modes[6], width)
    return cosine * sum_cos - sine * sum_sin, sine * sum_cos + cosine * sum_sin


def basis_rows(main, last, modes_y, modes_z):
    weights_y = [w[1:2] for w in spline_weights(main[6:8])]
    rows_y = mode_rows(main[4:5], weights_y, modes_y, NY)
    rows_z = mode_rows(main[5:6], spline_weights(last), modes_z, NZ)
    return rows_y, rows_z


def column_values(rows_y, rows_z):
    values = []
    for ty in range(2):
        for tz in range(2):
            for iy in range(rows_y[0].shape[0]):
                values.append(rows_y[ty][iy : iy + 1] * rows_z[tz])
    return values


def plane_rows(start, weights, rows):
    iota = lax.broadcasted_iota(jnp.int32, (rows, start.shape[1]), 0).astype(F32)
    away = iota - start
    result = jnp.where(away == 0.0, weights[0], 0.0)
    for stencil in range(1, 4):
        result = jnp.where(away == float(stencil), weights[stencil], result)
    return result


def first_plane(block, planes):
    joined = max(1, 8 // planes)
    return lax.div(block, joined) * (joined * planes)


def spread_kernel(rows, points_ref, modes_y_ref, modes_z_ref, out_ref, *kept_refs):
    main, last = unpack(points_ref[0])
    count = main.shape[1]
    modes_y = [modes_y_ref[i] for i in range(7)]
    modes_z = [modes_z_ref[i] for i in range(7)]
    rows_y, rows_z = basis_rows(main, last, modes_y, modes_z)
    for kept_ref in kept_refs:
        kept_ref[0] = jnp.concatenate([*rows_y, *rows_z], axis=0)
    values = column_values(rows_y, rows_z)
    weights_x = spline_weights(main[6:7])
    weight = plane_rows(main[3:4], weights_x, rows)
    stack = jnp.concatenate([weight * main[c : c + 1] for c in range(3)], axis=0)
    if 3 * rows < LANES:
        stack = jnp.concatenate([stack, jnp.zeros((LANES - 3 * rows, count), F32)], axis=0)
    both = jnp.concatenate(split(stack), axis=0)
    parts = [split(value) for value in values]
    left = jnp.concatenate(
        [jnp.concatenate([p[i] for p in parts], axis=0) for i in range(2)], axis=1
    )
    right = jnp.concatenate([both, both], axis=1)
    acc = lax.dot_general(left, right, (((1,), (1,)), ((), ())), preferred_element_type=F32)
    total = (acc[:, :LANES] + acc[:, LANES:]).T
    out_ref[0] = total[: 3 * rows]


def keeps(points, modes_y):
    blocks_rows = 2 * (modes_y.shape[1] + KZ)
    return modes_y.shape[1] % 8 == 0 and lax.axis_size(("group", "dev")) * blocks_rows * (
        points.shape[2] // 9 * 8
    ) * 4 <= KEEP_BYTES


def spread(points, modes_y, modes_z, rows, keep):
    blocks, _, width = points.shape
    count = width // 9 * 8
    own_y = modes_y.shape[1]
    cols = 4 * own_y * KZ
    kept = 2 * (own_y + KZ)
    out_specs = [pl.BlockSpec((1, 3 * rows, cols), lambda i: (i, 0, 0))]
    out_shape = [jax.ShapeDtypeStruct((blocks, 3 * rows, cols), F32)]
    if keep:
        out_specs.append(pl.BlockSpec((1, kept, count), lambda i: (i, 0, 0)))
        out_shape.append(jax.ShapeDtypeStruct((blocks, kept, count), F32))
    return pl.pallas_call(
        functools.partial(spread_kernel, rows),
        grid=(blocks,),
        in_specs=[
            pl.BlockSpec((1, 8, width), lambda i: (i, 0, 0)),
            pl.BlockSpec(modes_y.shape, lambda i: (0, 0, 0)),
            pl.BlockSpec(modes_z.shape, lambda i: (0, 0, 0)),
        ],
        out_specs=out_specs,
        out_shape=out_shape,
        compiler_params=pltpu.CompilerParams(vmem_limit_bytes=SPREAD_LIMIT),
        cost_estimate=pl.CostEstimate(
            flops=blocks * count * cols * LANES * 14,
            bytes_accessed=blocks * (9 * count + 3 * rows * cols) * 4,
            transcendentals=0,
        ),
        name="spread",
    )(points, modes_y, modes_z)


def solve_kernel(planes, rows, parts, ids_ref, *refs):
    piece_refs = refs[:parts]
    forward_ref, back_ref, waves_ref, out_ref, modes, stacked = refs[parts:]
    extra = 8
    out_ref[...] = jnp.zeros_like(out_ref)
    before = 0
    for piece_ref in piece_refs:

        @pl.loop(0, piece_ref.shape[0])
        def _(index):
            first = pl.multiple_of(first_plane(ids_ref[before + index], planes), 8)
            for c in range(3):
                out_ref[c, pl.ds(first, rows)] += piece_ref[index, c * rows : (c + 1) * rows]

        before += piece_ref.shape[0]
    for c in range(3):
        out_ref[c, 0:extra] += out_ref[c, NX : NX + extra]
    half = NX // 2
    quarter = NX // 4
    lanes = waves_ref.shape[1]

    def fill(value):
        high, low = split(value)
        stacked[0:half] = high
        stacked[half : 2 * half] = high
        stacked[2 * half : 3 * half] = low

    for parity in range(2):

        @pl.loop(0, 3)
        def _(c):
            first = out_ref[c, 0:half]
            second = out_ref[c, half:NX]
            fill(first + second if parity == 0 else first - second)
            modes[parity, c] = jnp.dot(forward_ref[parity], stacked[...], preferred_element_type=F32)

    wave_y = waves_ref[0:1]
    wave_z = waves_ref[1:2]
    mult = waves_ref[2:3]
    flat = wave_y * wave_y + wave_z * wave_z
    group = 8

    for parity in range(2):

        @pl.loop(0, quarter // group)
        def _(index):
            row = pl.multiple_of(index * group, group)
            number = lax.broadcasted_iota(jnp.int32, (group, lanes), 0) + row
            number = (2 * number + parity).astype(F32)
            wave_x = number * (TWO_PI / NX)
            squared = wave_x * wave_x + flat
            anchor = squared == 0.0
            inverse = jnp.where(anchor, 0.0, 1.0 / jnp.where(anchor, 1.0, squared))
            factor = inverse * mult * jnp.where(number == 0.0, 1.0, 2.0)
            waves = (wave_x, wave_y, wave_z)
            values = {}
            for c in range(3):
                for tx in range(2):
                    for tyz in range(4):
                        values[c, tx, tyz // 2, tyz % 2] = modes[
                            parity,
                            c,
                            pl.ds(pl.multiple_of(tx * quarter + row, group), group),
                            tyz * lanes : (tyz + 1) * lanes,
                        ]

            def flip(state, axis):
                return tuple(1 - t if i == axis else t for i, t in enumerate(state))

            states = [(a, b, d) for a in range(2) for b in range(2) for d in range(2)]
            divergence = {}
            for state in states:
                total = None
                for axis in range(3):
                    term = waves[axis] * values[(axis,) + flip(state, axis)]
                    if state[axis]:
                        term = -term
                    total = term if total is None else total + term
                divergence[state] = total * inverse
            for state in states:
                for axis in range(3):
                    term = waves[axis] * divergence[flip(state, axis)]
                    value = values[(axis,) + state]
                    value = value - term if state[axis] else value + term
                    tyz = 2 * state[1] + state[2]
                    modes[
                        parity,
                        axis,
                        pl.ds(pl.multiple_of(state[0] * quarter + row, group), group),
                        tyz * lanes : (tyz + 1) * lanes,
                    ] = value * factor

    @pl.loop(0, 3)
    def _(c):
        fill(modes[0, c])
        even = jnp.dot(back_ref[0], stacked[...], preferred_element_type=F32)
        out_ref[c, 0:half] = even
        fill(modes[1, c])
        odd = jnp.dot(back_ref[1], stacked[...], preferred_element_type=F32)
        even = out_ref[c, 0:half]
        out_ref[c, 0:half] = even + odd
        out_ref[c, half:NX] = even - odd
        out_ref[c, NX : NX + extra] = out_ref[c, 0:extra]


def solve(pieces, ids, waves, forward, back, planes, rows):
    full = pl.BlockSpec(memory_space=pltpu.VMEM)
    cols = pieces[0].shape[2]
    return pl.pallas_call(
        functools.partial(solve_kernel, planes, rows, len(pieces)),
        in_specs=[pl.BlockSpec(memory_space=pltpu.SMEM)] + [full] * (len(pieces) + 3),
        out_specs=full,
        out_shape=jax.ShapeDtypeStruct((3, NX + 8, cols), F32),
        scratch_shapes=[
            pltpu.VMEM((2, 3, NX // 2, cols), F32),
            pltpu.VMEM((3 * NX // 2, cols), BF16),
        ],
        compiler_params=pltpu.CompilerParams(vmem_limit_bytes=SOLVE_LIMIT),
        cost_estimate=pl.CostEstimate(
            flops=36 * NX // 2 * NX // 2 * cols,
            bytes_accessed=6 * NX * cols * 4,
            transcendentals=0,
        ),
        name="solve",
    )(ids, *pieces, forward, back, waves)


def gather_kernel(planes, rows, before, kept, ids_ref, points_ref, *refs):
    basis_refs, (lines_ref, out_ref, plane) = refs[:-3], refs[-3:]
    step = pl.program_id(0)
    first = pl.multiple_of(first_plane(ids_ref[before + step], planes), 8)
    stack = jnp.concatenate([lines_ref[c, pl.ds(first, rows)] for c in range(3)], axis=0)
    if 3 * rows < LANES:
        stack = jnp.concatenate([stack, jnp.zeros((LANES - 3 * rows, lines_ref.shape[2]), F32)], axis=0)
    high, low = split(stack)
    plane[0:LANES] = high
    plane[LANES:] = low
    main, last = unpack(points_ref[0])
    count = main.shape[1]
    chunk = count // 4
    if kept:
        own_y = basis_refs[0].shape[1] // 2 - KZ
    else:
        modes_y, modes_z = [[ref[i] for i in range(7)] for ref in basis_refs]
    for index in range(4):
        at = slice(index * chunk, (index + 1) * chunk)
        if kept:
            rows_y = [basis_refs[0][0, i * own_y : (i + 1) * own_y, at] for i in range(2)]
            rows_z = [
                basis_refs[0][0, 2 * own_y + i * KZ : 2 * own_y + (i + 1) * KZ, at] for i in range(2)
            ]
        else:
            rows_y, rows_z = basis_rows(main[:, at], last[:, at], modes_y, modes_z)
        pairs = [split(value) for value in column_values(rows_y, rows_z)]
        highs = jnp.concatenate([p[0] for p in pairs], axis=0)
        lows = jnp.concatenate([p[1] for p in pairs], axis=0)
        result = jnp.dot(plane[...], highs, preferred_element_type=F32)
        small = jnp.dot(plane[0:LANES], lows, preferred_element_type=F32)
        result = result[:LANES] + result[LANES:] + small
        weight = plane_rows(main[3:4, at], spline_weights(main[6:7, at]), rows)
        out_ref[0, :, at] = jnp.concatenate(
            [
                jnp.sum(weight * result[c * rows : (c + 1) * rows], axis=0, keepdims=True)
                for c in range(3)
            ],
            axis=0,
        )


def gather(points, before, ids, basis, lines, planes, rows):
    blocks, _, width = points.shape
    count = width // 9 * 8
    cols = lines.shape[2]
    kept = len(basis) == 1
    if kept:
        basis_specs = [pl.BlockSpec((1,) + basis[0].shape[1:], lambda i: (i, 0, 0))]
    else:
        basis_specs = [pl.BlockSpec(table.shape, lambda i: (0, 0, 0)) for table in basis]
    return pl.pallas_call(
        functools.partial(gather_kernel, planes, rows, before, kept),
        grid=(blocks,),
        in_specs=[
            pl.BlockSpec(memory_space=pltpu.SMEM),
            pl.BlockSpec((1, 8, width), lambda i: (i, 0, 0)),
            *basis_specs,
            pl.BlockSpec(memory_space=pltpu.VMEM),
        ],
        out_specs=pl.BlockSpec((1, 3, count), lambda i: (i, 0, 0)),
        out_shape=jax.ShapeDtypeStruct((blocks, 3, count), F32),
        scratch_shapes=[pltpu.VMEM((2 * LANES, cols), BF16)],
        compiler_params=pltpu.CompilerParams(vmem_limit_bytes=GATHER_LIMIT),
        cost_estimate=pl.CostEstimate(
            flops=blocks * count * cols * LANES * 14,
            bytes_accessed=blocks * 12 * count * 4,
            transcendentals=0,
        ),
        name="interpolate",
    )(ids, points, *basis, lines)


def line_tables():
    half = NX // 2
    place = np.arange(half)
    forward, back = [], []
    for parity in range(2):
        number = 2 * np.arange(NX // 4) + parity
        angle = (number[:, None] * place[None, :] % NX) * (2.0 * np.pi / NX)
        table = np.concatenate([np.cos(angle), np.sin(angle)], axis=0)
        for tables, value in ((forward, table), (back, table.T)):
            high = value.astype(ml_dtypes.bfloat16)
            low = (value - high.astype(np.float64)).astype(ml_dtypes.bfloat16)
            tables.append(np.concatenate([high, low, high], axis=1))
    return np.stack(forward), np.stack(back)


def mode_table(numbers, length):
    angle = numbers * (2.0 * np.pi / length)
    rows = [numbers]
    for stencil in range(1, 4):
        rows += [np.cos(stencil * angle), np.sin(stencil * angle)]
    table = np.stack(rows, axis=1)[..., None].astype(np.float32)
    return np.broadcast_to(table, table.shape[:3] + (LANES,))


def far_tables(device, devices):
    own_y = (NY // 2) * (NZ // 2) // devices // KZ
    parts_z = NZ // 2 // KZ
    number_y = np.arange(NY // 2).reshape(-1, own_y).astype(np.float64)
    number_z = np.arange(NZ // 2).reshape(-1, KZ).astype(np.float64)
    mult_y = np.where(number_y == 0, 1.0, 2.0)
    mult_z = np.where(number_z == 0, 1.0, 2.0) / float(NX * NY * NZ)
    shape = (number_y.shape[0], parts_z, own_y, KZ)
    waves = [
        np.broadcast_to(number_y[:, None, :, None] * (TWO_PI / NY), shape),
        np.broadcast_to(number_z[None, :, None, :] * (TWO_PI / NZ), shape),
        mult_y[:, None, :, None] * mult_z[None, :, None, :],
    ]
    waves = np.stack([w.reshape(devices, own_y * KZ) for w in waves], axis=1)
    waves = np.concatenate([waves, np.zeros((devices, 5, own_y * KZ))], axis=1)

    def own(table, index):
        return lax.dynamic_index_in_dim(jnp.asarray(table, F32), index, 0, keepdims=False)

    return (
        own(mode_table(number_y, NY), device // parts_z),
        own(mode_table(number_z, NZ), device % parts_z),
        own(waves, device),
    )


def per_device(forces, stencil_start, fraction, tile_pairs, pair_count):
    groups = lax.axis_size("group")
    members = lax.axis_size("dev")
    devices = groups * members
    planes = NX // devices
    device = lax.axis_index("group") * members + lax.axis_index("dev")
    rows = max(8, planes) + 8
    first = first_plane(device, planes).reshape(1)
    own = pack(first, forces, stencil_start, fraction)

    def from_flipped(values, mask):
        pairs = [(i, i ^ mask) for i in range(devices)]
        return lax.ppermute(values, ("group", "dev"), pairs)

    near_masks = (4, 8, 12)
    parts = [own, jnp.concatenate([from_flipped(own, mask) for mask in near_masks], axis=0)]
    masks = [0, *near_masks]
    own_half = jnp.concatenate(parts, axis=0)
    last_bit = devices.bit_length() - 2
    bits = [1] + list(range(4, last_bit))
    for bit in bits:
        parts.append(from_flipped(own_half, 1 << bit))
        own_half = jnp.concatenate([own_half, parts[-1]], axis=0)
        masks = masks + [m ^ 1 << bit for m in masks]
    top = 1 << last_bit
    parts.append(from_flipped(own_half, 1))
    other = from_flipped(own_half, top)
    parts += [other, from_flipped(other, 1)]
    masks = np.array([m ^ flip for flip in (0, 1, top, top ^ 1) for m in masks], np.int32)
    ids = device ^ jnp.asarray(masks)
    modes_y, modes_z, waves = far_tables(device, devices)
    forward, back = line_tables()
    keep = keeps(own, modes_y)
    spreads = [spread(points, modes_y, modes_z, rows, keep) for points in parts]
    pieces = [result[0] for result in spreads]
    lines = solve(pieces, ids, waves, jnp.asarray(forward), jnp.asarray(back), planes, rows)
    firsts = np.cumsum([0] + [points.shape[0] for points in parts])

    def sums(part):
        basis = spreads[part][1:] if keep else [modes_y, modes_z]
        return gather(parts[part], int(firsts[part]), ids, basis, lines, planes, rows)

    count = len(parts)
    across = from_flipped(sums(count - 1), 1)
    across = from_flipped(sums(count - 2) + across, top)
    total = across + from_flipped(sums(count - 3), 1)
    for part in range(count - 4, 1, -1):
        half = total.shape[0] // 2
        total = total[:half] + from_flipped(sums(part) + total[half:], 1 << bits[part - 2])
    beside = sums(1) + total[1:]
    far = (sums(0) + total[:1])[0]
    for index, mask in enumerate(near_masks):
        far = far + from_flipped(beside[index], mask)
    return far + near_field(forces, stencil_start, fraction, tile_pairs, pair_count)


def solution(mesh):
    in_specs = (
        P(None, ("group", "dev")),
        P(None, ("group", "dev")),
        P(None, ("group", "dev")),
        P(("group", "dev"), None),
        P(("group", "dev")),
    )
    out_specs = P(None, ("group", "dev"))
    return jax.shard_map(
        per_device, mesh=mesh, in_specs=in_specs, out_specs=out_specs, check_vma=False
    )
```

profile of v0, /device:TPU:0, one launch (start us, length us, event | category | flops | bytes accessed | tf_op | source)
XLA Modules:
  0.0 165.2 jit_solution(15122422323077956004)
XLA Ops:
  0.0 1.4 pack.1.points_ref
  1.4 3.0 %collective-permute-start = (f32[1,8,2304]{2,1,0:T(8,128)}, f32[1,8,2304]{2,1,0:T(8,128)S(1)}, u32[]{:S(2)}, u32[]{:S(2)}) collective-permute-start(f32[1,8,2304]{2,1,0:T(8,128)} %pack.1.points_ref), channel_id=1, source_target_pairs={{0,4},{1,5},{2,6},{3,7},{4,0},{5,1},{6,2},{7,3},{8,12},{9,13},{10,... | collective-permute-start | bytes 221192 | tf_op jit(solution)/shard_map/ppermute | solution.py:540
  4.5 2.6 %collective-permute-start.1 = (f32[1,8,2304]{2,1,0:T(8,128)}, f32[1,8,2304]{2,1,0:T(8,128)S(1)}, u32[]{:S(2)}, u32[]{:S(2)}) collective-permute-start(f32[1,8,2304]{2,1,0:T(8,128)} %pack.1.points_ref), channel_id=1, source_target_pairs={{0,8},{1,9},{2,10},{3,11},{4,12},{5,13},{6,14},{7,15},{8,0},{9,1},... | collective-permute-start | bytes 221192 | tf_op jit(solution)/shard_map/ppermute | solution.py:540
  12.6 1.7 %spread.6 = (f32[1,120,512]{2,1,0:T(8,128)S(1)}, f32[1,48,2048]{2,1,0:T(8,128)S(1)}) custom-call(f32[1,8,2304]{2,1,0:T(8,128)S(1)} %copy-done.2, f32[7,8,128]{2,1,0:T(8,128)S(1)} %broadcast.5.modes_y_ref, f32[7,16,128]{2,1,0:T(8,128)S(1)} %broadcast.7.modes_z_ref), custom_call_target="tpu_custom_call" | custom-call | flops 1879048192 | bytes 319488 | tf_op jit(solution)/shard_map/spread/pallas_call | solution.py:258
  16.5 3.4 %collective-permute-start.3 = (f32[4,8,2304]{2,1,0:T(8,128)S(1)}, f32[4,8,2304]{2,1,0:T(8,128)S(1)}, u32[]{:S(2)}, u32[]{:S(2)}) collective-permute-start(f32[4,8,2304]{2,1,0:T(8,128)S(1)} %pad_maximum_fusion), channel_id=1, source_target_pairs={{0,2},{1,3},{2,0},{3,1},{4,6},{5,7},{6,4},{7,5},{8,10},{9,11},{10,... | collective-permute-start | bytes 884744 | tf_op jit(solution)/shard_map/ppermute | solution.py:540
  20.0 5.1 %spread.7 = (f32[3,120,512]{2,1,0:T(8,128)S(1)}, f32[3,48,2048]{2,1,0:T(8,128)S(1)}) custom-call(f32[3,8,2304]{2,1,0:T(8,128)S(1)} %get-tuple-element.33.points_ref, f32[7,8,128]{2,1,0:T(8,128)S(1)} %broadcast.5.modes_y_ref, f32[7,16,128]{2,1,0:T(8,128)S(1)} %broadcast.7.modes_z_ref), custom_call_target="tpu_custom_call" | custom-call | flops 5637144576 | bytes 958464 | tf_op jit(solution)/shard_map/spread/pallas_call | solution.py:258
  25.1 11.8 %collective-permute-start.5 = (f32[8,8,2304]{2,1,0:T(8,128)S(1)}, f32[8,8,2304]{2,1,0:T(8,128)S(1)}, u32[]{:S(2)}, u32[]{:S(2)}) collective-permute-start(f32[8,8,2304]{2,1,0:T(8,128)S(1)} %constant_dynamic-update-slice_fusion.3), channel_id=1, source_target_pairs={{0,16},{1,17},{2,18},{3,19},{4,20},{5,21},{6,22},{7,23},{8,24},{9,... | collective-permute-start | bytes 1769480 | tf_op jit(solution)/shard_map/ppermute | solution.py:540
  36.9 6.8 %spread.8 = (f32[4,120,512]{2,1,0:T(8,128)S(1)}, f32[4,48,2048]{2,1,0:T(8,128)S(1)}) custom-call(f32[4,8,2304]{2,1,0:T(8,128)S(1)} %collective-permute-done.3.points_ref, f32[7,8,128]{2,1,0:T(8,128)S(1)} %broadcast.5.modes_y_ref, f32[7,16,128]{2,1,0:T(8,128)S(1)} %broadcast.7.modes_z_ref), custom_call_target="tpu_custom_call" | custom-call | flops 7516192768 | bytes 1277952 | tf_op jit(solution)/shard_map/spread/pallas_call | solution.py:258
  43.7 2.3 %collective-permute-done.5.points_ref = f32[8,8,2304]{2,1,0:T(8,128)S(1)} collective-permute-done((f32[8,8,2304]{2,1,0:T(8,128)S(1)}, f32[8,8,2304]{2,1,0:T(8,128)S(1)}, u32[]{:S(2)}, u32[]{:S(2)}) %collective-permute-start.5) | collective-permute-done | bytes 589856 | tf_op jit(solution)/shard_map/ppermute | solution.py:540
  46.0 13.5 %spread.10 = (f32[8,120,512]{2,1,0:T(8,128)S(1)}, f32[8,48,2048]{2,1,0:T(8,128)S(1)}) custom-call(f32[8,8,2304]{2,1,0:T(8,128)S(1)} %collective-permute-done.5.points_ref, f32[7,8,128]{2,1,0:T(8,128)S(1)} %broadcast.5.modes_y_ref, f32[7,16,128]{2,1,0:T(8,128)S(1)} %broadcast.7.modes_z_ref), custom_call_target="tpu_custom_call" | custom-call | flops 15032385536 | bytes 2555904 | tf_op jit(solution)/shard_map/spread/pallas_call | solution.py:258
  59.5 13.6 %spread.9 = (f32[8,120,512]{2,1,0:T(8,128)S(1)}, f32[8,48,2048]{2,1,0:T(8,128)S(1)}) custom-call(f32[8,8,2304]{2,1,0:T(8,128)S(1)} %collective-permute-done.4.points_ref, f32[7,8,128]{2,1,0:T(8,128)S(1)} %broadcast.5.modes_y_ref, f32[7,16,128]{2,1,0:T(8,128)S(1)} %broadcast.7.modes_z_ref), custom_call_target="tpu_custom_call" | custom-call | flops 15032385536 | bytes 2555904 | tf_op jit(solution)/shard_map/spread/pallas_call | solution.py:258
  73.1 13.5 %spread.11 = (f32[8,120,512]{2,1,0:T(8,128)S(1)}, f32[8,48,2048]{2,1,0:T(8,128)S(1)}) custom-call(f32[8,8,2304]{2,1,0:T(8,128)S(1)} %collective-permute-done.6.points_ref, f32[7,8,128]{2,1,0:T(8,128)S(1)} %broadcast.5.modes_y_ref, f32[7,16,128]{2,1,0:T(8,128)S(1)} %broadcast.7.modes_z_ref), custom_call_target="tpu_custom_call" | custom-call | flops 15032385536 | bytes 2555904 | tf_op jit(solution)/shard_map/spread/pallas_call | solution.py:258
  86.6 15.8 %solve.1.refs_1_ = f32[3,1032,512]{2,1,0:T(8,128)S(1)} custom-call(s32[32]{0:T(128)S(1)} %broadcast_xor_fusion.ids_ref, f32[1,120,512]{2,1,0:T(8,128)S(1)} %get-tuple-element.18.refs_0_, f32[3,120,512]{2,1,0:T(8,128)S(1)} %get-tuple-element.19.refs_1_, f32[4,120,512]{2,1,0:T(8,128)S(1)} %get-tuple-element.20.refs_2_, ...), custom_call_target="tpu_custom_call" | custom-call | flops 4831838208 | bytes 12582912 | tf_op jit(solution)/shard_map/solve/pallas_call | solution.py:386
  102.4 11.1 %interpolate.9 = f32[8,3,2048]{2,1,0:T(4,128)S(1)} custom-call(s32[32]{0:T(128)S(1)} %broadcast_xor_fusion.ids_ref, f32[8,8,2304]{2,1,0:T(8,128)S(1)} %collective-permute-done.4.points_ref, f32[8,48,2048]{2,1,0:T(8,128)S(1)} %get-tuple-element.26.refs_0_, f32[3,1032,512]{2,1,0:T(8,128)S(1)} %solve.1.refs_1_), custom_call_target="tpu_custom_call" | custom-call | flops 15032385536 | bytes 786432 | tf_op jit(solution)/shard_map/interpolate/pallas_call | solution.py:456
  114.2 10.9 %interpolate.8 = f32[8,3,2048]{2,1,0:T(4,128)S(1)} custom-call(s32[32]{0:T(128)S(1)} %broadcast_xor_fusion.ids_ref, f32[8,8,2304]{2,1,0:T(8,128)S(1)} %collective-permute-done.6.points_ref, f32[8,48,2048]{2,1,0:T(8,128)S(1)} %get-tuple-element.25.refs_0_, f32[3,1032,512]{2,1,0:T(8,128)S(1)} %solve.1.refs_1_), custom_call_target="tpu_custom_call" | custom-call | flops 15032385536 | bytes 786432 | tf_op jit(solution)/shard_map/interpolate/pallas_call | solution.py:456
  125.2 11.1 %interpolate.7 = f32[8,3,2048]{2,1,0:T(4,128)S(1)} custom-call(s32[32]{0:T(128)S(1)} %broadcast_xor_fusion.ids_ref, f32[8,8,2304]{2,1,0:T(8,128)S(1)} %collective-permute-done.5.points_ref, f32[8,48,2048]{2,1,0:T(8,128)S(1)} %get-tuple-element.24.refs_0_, f32[3,1032,512]{2,1,0:T(8,128)S(1)} %solve.1.refs_1_), custom_call_target="tpu_custom_call" | custom-call | flops 15032385536 | bytes 786432 | tf_op jit(solution)/shard_map/interpolate/pallas_call | solution.py:456
  137.3 5.8 %interpolate.10 = f32[4,3,2048]{2,1,0:T(4,128)S(1)} custom-call(s32[32]{0:T(128)S(1)} %broadcast_xor_fusion.ids_ref, f32[4,8,2304]{2,1,0:T(8,128)S(1)} %collective-permute-done.3.points_ref, f32[4,48,2048]{2,1,0:T(8,128)S(1)} %get-tuple-element.27.refs_0_, f32[3,1032,512]{2,1,0:T(8,128)S(1)} %solve.1.refs_1_), custom_call_target="tpu_custom_call" | custom-call | flops 7516192768 | bytes 393216 | tf_op jit(solution)/shard_map/interpolate/pallas_call | solution.py:456
  143.1 2.0 %collective-permute-done.8 = f32[8,3,2048]{2,1,0:T(4,128)S(1)} collective-permute-done((f32[8,3,2048]{2,1,0:T(4,128)S(1)}, f32[8,3,2048]{2,1,0:T(4,128)S(1)}, u32[]{:S(2)}, u32[]{:S(2)}) %collective-permute-start.8) | collective-permute-done | bytes 196640 | tf_op jit(solution)/shard_map/ppermute | solution.py:540
  145.3 1.4 collective-permute-start.10
  146.7 4.5 %interpolate.11 = f32[3,3,2048]{2,1,0:T(4,128)S(1)} custom-call(s32[32]{0:T(128)S(1)} %broadcast_xor_fusion.ids_ref, f32[3,8,2304]{2,1,0:T(8,128)S(1)} %get-tuple-element.33.points_ref, f32[3,48,2048]{2,1,0:T(8,128)S(1)} %get-tuple-element.28.refs_0_, f32[3,1032,512]{2,1,0:T(8,128)S(1)} %solve.1.refs_1_), custom_call_target="tpu_custom_call" | custom-call | flops 5637144576 | bytes 294912 | tf_op jit(solution)/shard_map/interpolate/pallas_call | solution.py:456
  151.3 3.6 %collective-permute-start.11 = (f32[3,2048]{1,0:T(4,128)S(1)}, f32[3,2048]{1,0:T(4,128)S(1)}, u32[]{:S(2)}, u32[]{:S(2)}) collective-permute-start(f32[3,2048]{1,0:T(4,128)S(1)} %get-tuple-element.29), channel_id=1, source_target_pairs={{0,4},{1,5},{2,6},{3,7},{4,0},{5,1},{6,2},{7,3},{8,12},{9,13},{10,... | collective-permute-start | bytes 73736 | tf_op jit(solution)/shard_map/ppermute | solution.py:540
  154.9 3.9 %collective-permute-start.12 = (f32[3,2048]{1,0:T(4,128)S(1)}, f32[3,2048]{1,0:T(4,128)S(1)}, u32[]{:S(2)}, u32[]{:S(2)}) collective-permute-start(f32[3,2048]{1,0:T(4,128)S(1)} %get-tuple-element.31), channel_id=1, source_target_pairs={{0,8},{1,9},{2,10},{3,11},{4,12},{5,13},{6,14},{7,15},{8,0},{9,1},... | collective-permute-start | bytes 73736 | tf_op jit(solution)/shard_map/ppermute | solution.py:540
  158.9 1.8 %interpolate.6 = f32[1,3,2048]{2,1,0:T(4,128)S(1)} custom-call(s32[32]{0:T(128)S(1)} %broadcast_xor_fusion.ids_ref, f32[1,8,2304]{2,1,0:T(8,128)S(1)} %copy-done.3, f32[1,48,2048]{2,1,0:T(8,128)S(1)} %get-tuple-element.17.refs_0_, f32[3,1032,512]{2,1,0:T(8,128)S(1)} %solve.1.refs_1_), custom_call_target="tpu_custom_call" | custom-call | flops 1879048192 | bytes 98304 | tf_op jit(solution)/shard_map/interpolate/pallas_call | solution.py:456
  161.2 3.4 %collective-permute-done.13 = f32[3,2048]{1,0:T(4,128)S(1)} collective-permute-done((f32[3,2048]{1,0:T(4,128)S(1)}, f32[3,2048]{1,0:T(4,128)S(1)}, u32[]{:S(2)}, u32[]{:S(2)}) %collective-permute-start.13) | collective-permute-done | bytes 24608 | tf_op jit(solution)/shard_map/ppermute | solution.py:540
  (54 shorter events, 10.1 us)
Async XLA Ops:
  1.4 15.0 %collective-permute-start = (f32[1,8,2304]{2,1,0:T(8,128)}, f32[1,8,2304]{2,1,0:T(8,128)S(1)}, u32[]{:S(2)}, u32[]{:S(2)}) collective-permute-start(f32[1,8,2304]{2,1,0:T(8,128)} %pack.1.points_ref), channel_id=1, source_target_pairs={{0,4},{1,5},{2,6},{3,7},{4,0},{5,1},{6,2},{7,3},{8,12},{9,13},{10,... | collective-permute-start | bytes 221192 | tf_op jit(solution)/shard_map/ppermute | solution.py:540
  4.5 12.0 %collective-permute-start.1 = (f32[1,8,2304]{2,1,0:T(8,128)}, f32[1,8,2304]{2,1,0:T(8,128)S(1)}, u32[]{:S(2)}, u32[]{:S(2)}) collective-permute-start(f32[1,8,2304]{2,1,0:T(8,128)} %pack.1.points_ref), channel_id=1, source_target_pairs={{0,8},{1,9},{2,10},{3,11},{4,12},{5,13},{6,14},{7,15},{8,0},{9,1},... | collective-permute-start | bytes 221192 | tf_op jit(solution)/shard_map/ppermute | solution.py:540
  7.0 9.4 %collective-permute-start.2 = (f32[1,8,2304]{2,1,0:T(8,128)}, f32[1,8,2304]{2,1,0:T(8,128)S(1)}, u32[]{:S(2)}, u32[]{:S(2)}) collective-permute-start(f32[1,8,2304]{2,1,0:T(8,128)} %pack.1.points_ref), channel_id=1, source_target_pairs={{0,12},{1,13},{2,14},{3,15},{4,8},{5,9},{6,10},{7,11},{8,4},{9,5},... | collective-permute-start | bytes 221192 | tf_op jit(solution)/shard_map/ppermute | solution.py:540
  11.7 0.9 copy-start.2
  12.6 1.7 %copy-start.4 = (f32[3,2048]{1,0:T(4,128)S(1)}, f32[3,2048]{1,0:T(4,128)}, u32[]{:S(2)}) copy-start(f32[3,2048]{1,0:T(4,128)} %forces_ref.3) | copy-start | bytes 73732
  12.6 1.7 %copy-start.5 = (s32[3,2048]{1,0:T(4,128)S(1)}, s32[3,2048]{1,0:T(4,128)}, u32[]{:S(2)}) copy-start(s32[3,2048]{1,0:T(4,128)} %start_ref.3) | copy-start | bytes 73732
  12.6 1.7 %copy-start.6 = (f32[3,2048]{1,0:T(4,128)S(1)}, f32[3,2048]{1,0:T(4,128)}, u32[]{:S(2)}) copy-start(f32[3,2048]{1,0:T(4,128)} %fraction_ref.3) | copy-start | bytes 73732
  16.5 8.6 %collective-permute-start.3 = (f32[4,8,2304]{2,1,0:T(8,128)S(1)}, f32[4,8,2304]{2,1,0:T(8,128)S(1)}, u32[]{:S(2)}, u32[]{:S(2)}) collective-permute-start(f32[4,8,2304]{2,1,0:T(8,128)S(1)} %pad_maximum_fusion), channel_id=1, source_target_pairs={{0,2},{1,3},{2,0},{3,1},{4,6},{5,7},{6,4},{7,5},{8,10},{9,11},{10,... | collective-permute-start | bytes 884744 | tf_op jit(solution)/shard_map/ppermute | solution.py:540
  25.1 20.9 %collective-permute-start.5 = (f32[8,8,2304]{2,1,0:T(8,128)S(1)}, f32[8,8,2304]{2,1,0:T(8,128)S(1)}, u32[]{:S(2)}, u32[]{:S(2)}) collective-permute-start(f32[8,8,2304]{2,1,0:T(8,128)S(1)} %constant_dynamic-update-slice_fusion.3), channel_id=1, source_target_pairs={{0,16},{1,17},{2,18},{3,19},{4,20},{5,21},{6,22},{7,23},{8,24},{9,... | collective-permute-start | bytes 1769480 | tf_op jit(solution)/shard_map/ppermute | solution.py:540
  36.9 22.6 %collective-permute-start.4 = (f32[8,8,2304]{2,1,0:T(8,128)S(1)}, f32[8,8,2304]{2,1,0:T(8,128)S(1)}, u32[]{:S(2)}, u32[]{:S(2)}) collective-permute-start(f32[8,8,2304]{2,1,0:T(8,128)S(1)} %constant_dynamic-update-slice_fusion.3), channel_id=1, source_target_pairs={{0,1},{1,0},{2,3},{3,2},{4,5},{5,4},{6,7},{7,6},{8,9},{9,8},{10,11... | collective-permute-start | bytes 1769480 | tf_op jit(solution)/shard_map/ppermute | solution.py:540
  46.0 27.2 %collective-permute-start.6 = (f32[8,8,2304]{2,1,0:T(8,128)S(1)}, f32[8,8,2304]{2,1,0:T(8,128)S(1)}, u32[]{:S(2)}, u32[]{:S(2)}) collective-permute-start(f32[8,8,2304]{2,1,0:T(8,128)S(1)} %collective-permute-done.5.points_ref), channel_id=1, source_target_pairs={{0,1},{1,0},{2,3},{3,2},{4,5},{5,4},{6,7},{7,6},{8,9},{9,8},{10,11... | collective-permute-start | bytes 1769480 | tf_op jit(solution)/shard_map/ppermute | solution.py:540
  73.1 13.5 %copy-start = (bf16[2,512,1536]{2,1,0:T(8,128)(2,1)S(1)}, bf16[2,512,1536]{2,1,0:T(8,128)(2,1)}, u32[]{:S(2)}) copy-start(bf16[2,512,1536]{2,1,0:T(8,128)(2,1)} %constant.69.clone.refs_6_) | copy-start | bytes 9437188
  73.1 13.5 %copy-start.1 = (bf16[2,512,1536]{2,1,0:T(8,128)(2,1)S(1)}, bf16[2,512,1536]{2,1,0:T(8,128)(2,1)}, u32[]{:S(2)}) copy-start(bf16[2,512,1536]{2,1,0:T(8,128)(2,1)} %constant.70.clone.refs_7_) | copy-start | bytes 9437188
  113.6 29.5 %collective-permute-start.9 = (f32[8,3,2048]{2,1,0:T(4,128)S(1)}, f32[8,3,2048]{2,1,0:T(4,128)S(1)}, u32[]{:S(2)}, u32[]{:S(2)}) collective-permute-start(f32[8,3,2048]{2,1,0:T(4,128)S(1)} %interpolate.9), channel_id=1, source_target_pairs={{0,1},{1,0},{2,3},{3,2},{4,5},{5,4},{6,7},{7,6},{8,9},{9,8},{10,11... | collective-permute-start | bytes 589832 | tf_op jit(solution)/shard_map/ppermute | solution.py:540
  125.1 11.2 %collective-permute-start.7 = (f32[8,3,2048]{2,1,0:T(4,128)S(1)}, f32[8,3,2048]{2,1,0:T(4,128)S(1)}, u32[]{:S(2)}, u32[]{:S(2)}) collective-permute-start(f32[8,3,2048]{2,1,0:T(4,128)S(1)} %interpolate.8), channel_id=1, source_target_pairs={{0,1},{1,0},{2,3},{3,2},{4,5},{5,4},{6,7},{7,6},{8,9},{9,8},{10,11... | collective-permute-start | bytes 589832 | tf_op jit(solution)/shard_map/ppermute | solution.py:540
  136.4 8.7 %collective-permute-start.8 = (f32[8,3,2048]{2,1,0:T(4,128)S(1)}, f32[8,3,2048]{2,1,0:T(4,128)S(1)}, u32[]{:S(2)}, u32[]{:S(2)}) collective-permute-start(f32[8,3,2048]{2,1,0:T(4,128)S(1)} %add.55), channel_id=1, source_target_pairs={{0,16},{1,17},{2,18},{3,19},{4,20},{5,21},{6,22},{7,23},{8,24},{9,... | collective-permute-start | bytes 589832 | tf_op jit(solution)/shard_map/ppermute | solution.py:540
  145.3 6.0 %collective-permute-start.10 = (f32[4,3,2048]{2,1,0:T(4,128)S(1)}, f32[4,3,2048]{2,1,0:T(4,128)S(1)}, u32[]{:S(2)}, u32[]{:S(2)}) collective-permute-start(f32[4,3,2048]{2,1,0:T(4,128)S(1)} %slice_add_fusion), channel_id=1, source_target_pairs={{0,2},{1,3},{2,0},{3,1},{4,6},{5,7},{6,4},{7,5},{8,10},{9,11},{10,... | collective-permute-start | bytes 294920 | tf_op jit(solution)/shard_map/ppermute | solution.py:540
  146.7 12.2 %copy-start.3 = (f32[1,8,2304]{2,1,0:T(8,128)S(1)}, f32[1,8,2304]{2,1,0:T(8,128)}, u32[]{:S(2)}) copy-start(f32[1,8,2304]{2,1,0:T(8,128)} %pack.1.points_ref) | copy-start | bytes 221188
  151.3 9.4 %collective-permute-start.11 = (f32[3,2048]{1,0:T(4,128)S(1)}, f32[3,2048]{1,0:T(4,128)S(1)}, u32[]{:S(2)}, u32[]{:S(2)}) collective-permute-start(f32[3,2048]{1,0:T(4,128)S(1)} %get-tuple-element.29), channel_id=1, source_target_pairs={{0,4},{1,5},{2,6},{3,7},{4,0},{5,1},{6,2},{7,3},{8,12},{9,13},{10,... | collective-permute-start | bytes 73736 | tf_op jit(solution)/shard_map/ppermute | solution.py:540
  154.9 6.2 %collective-permute-start.12 = (f32[3,2048]{1,0:T(4,128)S(1)}, f32[3,2048]{1,0:T(4,128)S(1)}, u32[]{:S(2)}, u32[]{:S(2)}) collective-permute-start(f32[3,2048]{1,0:T(4,128)S(1)} %get-tuple-element.31), channel_id=1, source_target_pairs={{0,8},{1,9},{2,10},{3,11},{4,12},{5,13},{6,14},{7,15},{8,0},{9,1},... | collective-permute-start | bytes 73736 | tf_op jit(solution)/shard_map/ppermute | solution.py:540
  158.9 5.7 %collective-permute-start.13 = (f32[3,2048]{1,0:T(4,128)S(1)}, f32[3,2048]{1,0:T(4,128)S(1)}, u32[]{:S(2)}, u32[]{:S(2)}) collective-permute-start(f32[3,2048]{1,0:T(4,128)S(1)} %get-tuple-element.30), channel_id=1, source_target_pairs={{0,12},{1,13},{2,14},{3,15},{4,8},{5,9},{6,10},{7,11},{8,4},{9,5},... | collective-permute-start | bytes 73736 | tf_op jit(solution)/shard_map/ppermute | solution.py:540
where the time goes:
time: 164 us; the launch traced here: 165 us
  Pallas kernels  118 us (72%)
  starting transfers between devices  31.3 us (19%)
  waiting for transfers between devices  8.16 us (5%)
  local copies, waits for them, and re-layouts  5.06 us (3%)
    pallas_call x6, Pallas kernels, spread(): pl.pallas_call(functools.partial(spread_kernel, rows), grid=(blocks,), in...  54.2 us
    pallas_call x6, Pallas kernels, gather(): pl.pallas_call(functools.partial(gather_kernel, planes, rows, before, kep...  45.3 us
    ppermute x14, starting transfers between devices, from_flipped(): return lax.ppermute(values, ('group', 'dev'), pairs)  31.3 us
    pallas_call x1, Pallas kernels, solve(): pl.pallas_call(functools.partial(solve_kernel, planes, rows, len(pieces))...  15.8 us
    ppermute x14, waiting for transfers between devices, from_flipped(): return lax.ppermute(values, ('group', 'dev'), pairs)  8.16 us
  transfers between devices with their start and end apart: 14, of which 4 were waited for; matrix products, arithmetic and copies ran while one was open for 3% of the time, Pallas kernels for 46%

commit v1 on v0

--- a/solution.py
+++ b/solution.py
@@ -36,18 +36,16 @@
 def near_kernel(pairs_ref, count_ref, forces_ref, start_ref, fraction_ref, out_ref, columns):
     tiles = out_ref.shape[1] // LANES
     out_ref[...] = jnp.zeros_like(out_ref)
-    for tile in range(tiles):
-        at = slice(tile * LANES, (tile + 1) * LANES)
+
+    @pl.loop(0, tiles)
+    def _(tile):
+        at = pl.ds(pl.multiple_of(tile * LANES, LANES), LANES)
         nine = jnp.concatenate(
-            [
-                start_ref[:, at].astype(F32),
-                fraction_ref[:, at],
-                forces_ref[:, at],
-                jnp.zeros((7, LANES), F32),
-            ],
-            axis=0,
+            [start_ref[:, at].astype(F32), fraction_ref[:, at], forces_ref[:, at]], axis=0
         )
-        columns[at] = nine.T
+        for value in range(9):
+            wide = jnp.broadcast_to(nine[value : value + 1], (LANES, LANES))
+            columns[value, at] = wide.T
 
     @pl.loop(0, count_ref[0])
     def _(slot):
@@ -57,14 +55,14 @@
         fraction = fraction_ref[:, target]
         sums = [jnp.zeros((8, LANES), F32) for _ in range(3)]
         for row in range(0, LANES, 8):
-            source = columns[pl.ds(base + row, 8)]
+            source = [columns[value, pl.ds(base + row, 8)] for value in range(9)]
             gaps = []
             for axis, length in enumerate((None, NY, NZ)):
-                gap = start[axis : axis + 1] - source[:, axis : axis + 1]
+                gap = start[axis : axis + 1] - source[axis]
                 if length is not None:
                     gap = wrapped(gap, float(length))
-                gaps.append(gap + (fraction[axis : axis + 1] - source[:, 3 + axis : 4 + axis]))
-            pulled = [source[:, 6 + axis : 7 + axis] for axis in range(3)]
+                gaps.append(gap + (fraction[axis : axis + 1] - source[3 + axis]))
+            pulled = source[6:9]
             distance = gaps[0] * gaps[0] + gaps[1] * gaps[1] + gaps[2] * gaps[2]
             inverse = lax.rsqrt(distance + EPS_SQ)
             fall = NEAR_SCALE * jnp.exp(distance * (-1.0 / RANGE_SQ)) * (inverse * inverse * inverse)
@@ -86,8 +84,8 @@
         in_specs=[smem, smem, vmem, vmem, vmem],
         out_specs=vmem,
         out_shape=jax.ShapeDtypeStruct((3, points), F32),
-        scratch_shapes=[pltpu.VMEM((points, 16), F32)],
-        compiler_params=pltpu.CompilerParams(vmem_limit_bytes=8 * 2**20),
+        scratch_shapes=[pltpu.VMEM((9, points, LANES), F32)],
+        compiler_params=pltpu.CompilerParams(vmem_limit_bytes=16 * 2**20),
         cost_estimate=pl.CostEstimate(
             flops=slots * LANES * LANES * 6000, bytes_accessed=points * 48, transcendentals=0
         ),
@@ -277,7 +275,8 @@
 
 def solve_kernel(planes, rows, parts, ids_ref, *refs):
     piece_refs = refs[:parts]
-    forward_ref, back_ref, waves_ref, out_ref, modes, stacked = refs[parts:]
+    forward_half_ref, forward_ref, back_half_ref, back_ref = refs[parts : parts + 4]
+    waves_ref, out_ref, modes, stacked = refs[parts + 4 :]
     extra = 8
     out_ref[...] = jnp.zeros_like(out_ref)
     before = 0
@@ -292,24 +291,26 @@
         before += piece_ref.shape[0]
     for c in range(3):
         out_ref[c, 0:extra] += out_ref[c, NX : NX + extra]
-    half = NX // 2
     quarter = NX // 4
     lanes = waves_ref.shape[1]
-
-    def fill(value):
+    families = ((0, quarter // 2, 4, 0), (quarter, quarter // 2, 4, 2), (2 * quarter, quarter, 2, 1))
+
+    def transform(table, value):
         high, low = split(value)
-        stacked[0:half] = high
-        stacked[half : 2 * half] = high
-        stacked[2 * half : 3 * half] = low
-
-    for parity in range(2):
-
-        @pl.loop(0, 3)
-        def _(c):
-            first = out_ref[c, 0:half]
-            second = out_ref[c, half:NX]
-            fill(first + second if parity == 0 else first - second)
-            modes[parity, c] = jnp.dot(forward_ref[parity], stacked[...], preferred_element_type=F32)
+        size = value.shape[0]
+        stacked[0:size] = high
+        stacked[size : 2 * size] = high
+        stacked[2 * size : 3 * size] = low
+        return jnp.dot(table, stacked[0 : 3 * size], preferred_element_type=F32)
+
+    @pl.loop(0, 3)
+    def _(c):
+        cuts = [out_ref[c, i * quarter : (i + 1) * quarter] for i in range(4)]
+        first, second = cuts[0] + cuts[2], cuts[1] + cuts[3]
+        modes[c, 0:quarter] = transform(forward_half_ref[0], first + second)
+        modes[c, quarter : 2 * quarter] = transform(forward_half_ref[1], first - second)
+        odd = jnp.concatenate([cuts[0] - cuts[2], cuts[1] - cuts[3]], axis=0)
+        modes[c, 2 * quarter :] = transform(forward_ref[...], odd)
 
     wave_y = waves_ref[0:1]
     wave_z = waves_ref[1:2]
@@ -317,34 +318,30 @@
     flat = wave_y * wave_y + wave_z * wave_z
     group = 8
 
-    for parity in range(2):
-
-        @pl.loop(0, quarter // group)
+    for base, count, stride, offset in families:
+
+        @pl.loop(0, count // group)
         def _(index):
             row = pl.multiple_of(index * group, group)
             number = lax.broadcasted_iota(jnp.int32, (group, lanes), 0) + row
-            number = (2 * number + parity).astype(F32)
+            number = (stride * number + offset).astype(F32)
             wave_x = number * (TWO_PI / NX)
             squared = wave_x * wave_x + flat
             anchor = squared == 0.0
             inverse = jnp.where(anchor, 0.0, 1.0 / jnp.where(anchor, 1.0, squared))
             factor = inverse * mult * jnp.where(number == 0.0, 1.0, 2.0)
             waves = (wave_x, wave_y, wave_z)
-            values = {}
-            for c in range(3):
-                for tx in range(2):
-                    for tyz in range(4):
-                        values[c, tx, tyz // 2, tyz % 2] = modes[
-                            parity,
-                            c,
-                            pl.ds(pl.multiple_of(tx * quarter + row, group), group),
-                            tyz * lanes : (tyz + 1) * lanes,
-                        ]
+
+            def place(axis, state):
+                first = pl.multiple_of(base + state[0] * count + row, group)
+                tyz = 2 * state[1] + state[2]
+                return axis, pl.ds(first, group), slice(tyz * lanes, (tyz + 1) * lanes)
 
             def flip(state, axis):
                 return tuple(1 - t if i == axis else t for i, t in enumerate(state))
 
             states = [(a, b, d) for a in range(2) for b in range(2) for d in range(2)]
+            values = {(c,) + state: modes[place(c, state)] for c in range(3) for state in states}
             divergence = {}
             for state in states:
                 total = None
@@ -359,47 +356,43 @@
                     term = waves[axis] * divergence[flip(state, axis)]
                     value = values[(axis,) + state]
                     value = value - term if state[axis] else value + term
-                    tyz = 2 * state[1] + state[2]
-                    modes[
-                        parity,
-                        axis,
-                        pl.ds(pl.multiple_of(state[0] * quarter + row, group), group),
-                        tyz * lanes : (tyz + 1) * lanes,
-                    ] = value * factor
+                    modes[place(axis, state)] = value * factor
 
     @pl.loop(0, 3)
     def _(c):
-        fill(modes[0, c])
-        even = jnp.dot(back_ref[0], stacked[...], preferred_element_type=F32)
-        out_ref[c, 0:half] = even
-        fill(modes[1, c])
-        odd = jnp.dot(back_ref[1], stacked[...], preferred_element_type=F32)
-        even = out_ref[c, 0:half]
-        out_ref[c, 0:half] = even + odd
-        out_ref[c, half:NX] = even - odd
+        even = transform(back_half_ref[0], modes[c, 0:quarter])
+        out_ref[c, 0:quarter] = even
+        even = transform(back_half_ref[1], modes[c, quarter : 2 * quarter])
+        first = out_ref[c, 0:quarter]
+        out_ref[c, 0:quarter] = first + even
+        out_ref[c, quarter : 2 * quarter] = first - even
+        odd = transform(back_ref[...], modes[c, 2 * quarter :])
+        even = out_ref[c, 0 : 2 * quarter]
+        out_ref[c, 0 : 2 * quarter] = even + odd
+        out_ref[c, 2 * quarter : NX] = even - odd
         out_ref[c, NX : NX + extra] = out_ref[c, 0:extra]
 
 
-def solve(pieces, ids, waves, forward, back, planes, rows):
+def solve(pieces, ids, waves, tables, planes, rows):
     full = pl.BlockSpec(memory_space=pltpu.VMEM)
     cols = pieces[0].shape[2]
     return pl.pallas_call(
         functools.partial(solve_kernel, planes, rows, len(pieces)),
-        in_specs=[pl.BlockSpec(memory_space=pltpu.SMEM)] + [full] * (len(pieces) + 3),
+        in_specs=[pl.BlockSpec(memory_space=pltpu.SMEM)] + [full] * (len(pieces) + 5),
         out_specs=full,
         out_shape=jax.ShapeDtypeStruct((3, NX + 8, cols), F32),
         scratch_shapes=[
-            pltpu.VMEM((2, 3, NX // 2, cols), F32),
+            pltpu.VMEM((3, NX, cols), F32),
             pltpu.VMEM((3 * NX // 2, cols), BF16),
         ],
         compiler_params=pltpu.CompilerParams(vmem_limit_bytes=SOLVE_LIMIT),
         cost_estimate=pl.CostEstimate(
-            flops=36 * NX // 2 * NX // 2 * cols,
+            flops=27 * NX // 2 * NX // 2 * cols,
             bytes_accessed=6 * NX * cols * 4,
             transcendentals=0,
         ),
         name="solve",
-    )(ids, *pieces, forward, back, waves)
+    )(ids, *pieces, *tables, waves)
 
 
 def gather_kernel(planes, rows, before, kept, ids_ref, points_ref, *refs):
@@ -444,13 +437,13 @@
         )
 
 
-def gather(points, before, ids, basis, lines, planes, rows):
-    blocks, _, width = points.shape
+def gather(points, skip, blocks, before, ids, basis, lines, planes, rows):
+    width = points.shape[2]
     count = width // 9 * 8
     cols = lines.shape[2]
     kept = len(basis) == 1
     if kept:
-        basis_specs = [pl.BlockSpec((1,) + basis[0].shape[1:], lambda i: (i, 0, 0))]
+        basis_specs = [pl.BlockSpec((1,) + basis[0].shape[1:], lambda i: (i + skip, 0, 0))]
     else:
         basis_specs = [pl.BlockSpec(table.shape, lambda i: (0, 0, 0)) for table in basis]
     return pl.pallas_call(
@@ -458,7 +451,7 @@
         grid=(blocks,),
         in_specs=[
             pl.BlockSpec(memory_space=pltpu.SMEM),
-            pl.BlockSpec((1, 8, width), lambda i: (i, 0, 0)),
+            pl.BlockSpec((1, 8, width), lambda i: (i + skip, 0, 0)),
             *basis_specs,
             pl.BlockSpec(memory_space=pltpu.VMEM),
         ],
@@ -476,18 +469,24 @@
 
 
 def line_tables():
-    half = NX // 2
-    place = np.arange(half)
-    forward, back = [], []
-    for parity in range(2):
-        number = 2 * np.arange(NX // 4) + parity
-        angle = (number[:, None] * place[None, :] % NX) * (2.0 * np.pi / NX)
-        table = np.concatenate([np.cos(angle), np.sin(angle)], axis=0)
-        for tables, value in ((forward, table), (back, table.T)):
-            high = value.astype(ml_dtypes.bfloat16)
-            low = (value - high.astype(np.float64)).astype(ml_dtypes.bfloat16)
-            tables.append(np.concatenate([high, low, high], axis=1))
-    return np.stack(forward), np.stack(back)
+    def table(numbers, length):
+        angle = (numbers[:, None] * np.arange(length)[None, :] % NX) * (2.0 * np.pi / NX)
+        return np.concatenate([np.cos(angle), np.sin(angle)], axis=0)
+
+    def stacked(value):
+        high = value.astype(ml_dtypes.bfloat16)
+        low = (value - high.astype(np.float64)).astype(ml_dtypes.bfloat16)
+        return np.concatenate([high, low, high], axis=1)
+
+    quarter = NX // 4
+    even = [table(4 * np.arange(quarter // 2) + first, quarter) for first in (0, 2)]
+    odd = table(2 * np.arange(quarter) + 1, 2 * quarter)
+    return (
+        np.stack([stacked(value) for value in even]),
+        stacked(odd),
+        np.stack([stacked(value.T) for value in even]),
+        stacked(odd.T),
+    )
 
 
 def mode_table(numbers, length):
@@ -556,29 +555,54 @@
     masks = np.array([m ^ flip for flip in (0, 1, top, top ^ 1) for m in masks], np.int32)
     ids = device ^ jnp.asarray(masks)
     modes_y, modes_z, waves = far_tables(device, devices)
-    forward, back = line_tables()
+    tables = [jnp.asarray(table) for table in line_tables()]
     keep = keeps(own, modes_y)
     spreads = [spread(points, modes_y, modes_z, rows, keep) for points in parts]
     pieces = [result[0] for result in spreads]
-    lines = solve(pieces, ids, waves, jnp.asarray(forward), jnp.asarray(back), planes, rows)
+    lines = solve(pieces, ids, waves, tables, planes, rows)
     firsts = np.cumsum([0] + [points.shape[0] for points in parts])
 
-    def sums(part):
+    def sums(part, after, skip=0, blocks=None):
         basis = spreads[part][1:] if keep else [modes_y, modes_z]
-        return gather(parts[part], int(firsts[part]), ids, basis, lines, planes, rows)
+        blocks = blocks or parts[part].shape[0]
+        return gather(
+            parts[part], skip, blocks, int(firsts[part]) + skip, after, basis, lines, planes, rows
+        )
+
+    def then(value):
+        return lax.optimization_barrier((value, ids))
 
     count = len(parts)
-    across = from_flipped(sums(count - 1), 1)
-    across = from_flipped(sums(count - 2) + across, top)
-    total = across + from_flipped(sums(count - 3), 1)
+    across, after = then(sums(count - 1, ids))
+    across = sums(count - 2, after) + from_flipped(across, 1)
+    across, after = then(across)
+    across, beside = from_flipped(across, top), sums(count - 3, after)
+    (across, beside), after = then((across, beside))
+    beside = from_flipped(beside, 1)
+    total = None
     for part in range(count - 4, 1, -1):
+        given = sums(part, after)
+        if total is None:
+            (beside, given), after = then((beside, given))
+            total = across + beside
         half = total.shape[0] // 2
-        total = total[:half] + from_flipped(sums(part) + total[half:], 1 << bits[part - 2])
-    beside = sums(1) + total[1:]
-    far = (sums(0) + total[:1])[0]
-    for index, mask in enumerate(near_masks):
-        far = far + from_flipped(beside[index], mask)
-    return far + near_field(forces, stencil_start, fraction, tile_pairs, pair_count)
+        given = given + total[half:]
+        if part == 2:
+            given, after = then(given)
+            far_pair = sums(1, after, 1, 2)
+        given = from_flipped(given, 1 << bits[part - 2])
+        if part == 2:
+            (given, far_pair), after = then((given, far_pair))
+        total = total[:half] + given
+    far_pair, after = then(far_pair + total[2:])
+    far_pair = from_flipped(far_pair, 8)
+    last, far = sums(1, after, 0, 1), sums(0, after)
+    (far_pair, last, far), after = then((far_pair, last, far))
+    last = last + total[1:2] + far_pair[1:]
+    far = far + total[:1] + far_pair[:1]
+    forces, count_late, last = lax.optimization_barrier((forces, pair_count, last))
+    near = near_field(forces, stencil_start, fraction, tile_pairs, count_late)
+    return far[0] + from_flipped(last, 4)[0] + near
 
 
 def solution(mesh):

time: 164 us -> 155 us (0.945)
  the two profiles are of different devices: /device:TPU:0 before, /device:TPU:2 now
where the time goes in v1:
time: 155 us; the launch traced here: 153 us
  Pallas kernels  122 us (79%)
  starting transfers between devices  12.5 us (8%)
  waiting for transfers between devices  10.7 us (7%)
  local copies, waits for them, and re-layouts  5.03 us (3%)
  other arithmetic  1.57 us (1%)
    pallas_call x6, Pallas kernels, spread(): pl.pallas_call(functools.partial(spread_kernel, rows), grid=(blocks,), in...  54.3 us
    pallas_call x7, Pallas kernels, gather(): pl.pallas_call(functools.partial(gather_kernel, planes, rows, before, kep...  46.2 us
    pallas_call x1, Pallas kernels, solve(): pl.pallas_call(functools.partial(solve_kernel, planes, rows, len(pieces))...  12.9 us
    ppermute x13, starting transfers between devices, from_flipped(): return lax.ppermute(values, ('group', 'dev'), pairs)  12.5 us
    ppermute x13, waiting for transfers between devices, from_flipped(): return lax.ppermute(values, ('group', 'dev'), pairs)  10.7 us
    pallas_call x1, Pallas kernels, near_field(): pl.pallas_call(near_kernel, in_specs=[smem, smem, vmem, vmem, vmem], out_...  7.32 us
  transfers between devices with their start and end apart: 13, of which 4 were waited for; matrix products, arithmetic and copies ran while one was open for 3% of the time, Pallas kernels for 54%

profile of v1, /device:TPU:2, one launch (start us, length us, event | category | flops | bytes accessed | tf_op | source)
XLA Modules:
  0.0 153.0 jit_solution(362559453202782361)
XLA Ops:
  1.4 1.6 %collective-permute-start = (f32[1,8,2304]{2,1,0:T(8,128)}, f32[1,8,2304]{2,1,0:T(8,128)S(1)}, u32[]{:S(2)}, u32[]{:S(2)}) collective-permute-start(f32[1,8,2304]{2,1,0:T(8,128)} %pack.1.points_ref), channel_id=1, source_target_pairs={{0,4},{1,5},{2,6},{3,7},{4,0},{5,1},{6,2},{7,3},{8,12},{9,13},{10,... | collective-permute-start | bytes 221192 | tf_op jit(solution)/shard_map/ppermute | solution.py:539
  3.0 2.6 %collective-permute-start.1 = (f32[1,8,2304]{2,1,0:T(8,128)}, f32[1,8,2304]{2,1,0:T(8,128)S(1)}, u32[]{:S(2)}, u32[]{:S(2)}) collective-permute-start(f32[1,8,2304]{2,1,0:T(8,128)} %pack.1.points_ref), channel_id=1, source_target_pairs={{0,8},{1,9},{2,10},{3,11},{4,12},{5,13},{6,14},{7,15},{8,0},{9,1},... | collective-permute-start | bytes 221192 | tf_op jit(solution)/shard_map/ppermute | solution.py:539
  11.4 1.7 %spread.7 = (f32[1,120,512]{2,1,0:T(8,128)S(1)}, f32[1,48,2048]{2,1,0:T(8,128)S(1)}) custom-call(f32[1,8,2304]{2,1,0:T(8,128)S(1)} %copy-done.4, f32[7,8,128]{2,1,0:T(8,128)S(1)} %broadcast.5.modes_y_ref, f32[7,16,128]{2,1,0:T(8,128)S(1)} %broadcast.7.modes_z_ref), custom_call_target="tpu_custom_call" | custom-call | flops 1879048192 | bytes 319488 | tf_op jit(solution)/shard_map/spread/pallas_call | solution.py:256
  14.3 5.1 %spread.8 = (f32[3,120,512]{2,1,0:T(8,128)S(1)}, f32[3,48,2048]{2,1,0:T(8,128)S(1)}) custom-call(f32[3,8,2304]{2,1,0:T(8,128)S(1)} %get-tuple-element.71.points_ref, f32[7,8,128]{2,1,0:T(8,128)S(1)} %broadcast.5.modes_y_ref, f32[7,16,128]{2,1,0:T(8,128)S(1)} %broadcast.7.modes_z_ref), custom_call_target="tpu_custom_call" | custom-call | flops 5637144576 | bytes 958464 | tf_op jit(solution)/shard_map/spread/pallas_call | solution.py:256
  19.4 2.5 %collective-permute-done.3.points_ref = f32[4,8,2304]{2,1,0:T(8,128)S(1)} collective-permute-done((f32[4,8,2304]{2,1,0:T(8,128)S(1)}, f32[4,8,2304]{2,1,0:T(8,128)S(1)}, u32[]{:S(2)}, u32[]{:S(2)}) %collective-permute-start.3) | collective-permute-done | bytes 294944 | tf_op jit(solution)/shard_map/ppermute | solution.py:539
  21.9 1.6 %collective-permute-start.4 = (f32[8,8,2304]{2,1,0:T(8,128)S(1)}, f32[8,8,2304]{2,1,0:T(8,128)S(1)}, u32[]{:S(2)}, u32[]{:S(2)}) collective-permute-start(f32[8,8,2304]{2,1,0:T(8,128)S(1)} %constant_dynamic-update-slice_fusion), channel_id=1, source_target_pairs={{0,16},{1,17},{2,18},{3,19},{4,20},{5,21},{6,22},{7,23},{8,24},{9,... | collective-permute-start | bytes 1769480 | tf_op jit(solution)/shard_map/ppermute | solution.py:539
  23.5 6.8 %spread.9 = (f32[4,120,512]{2,1,0:T(8,128)S(1)}, f32[4,48,2048]{2,1,0:T(8,128)S(1)}) custom-call(f32[4,8,2304]{2,1,0:T(8,128)S(1)} %collective-permute-done.3.points_ref, f32[7,8,128]{2,1,0:T(8,128)S(1)} %broadcast.5.modes_y_ref, f32[7,16,128]{2,1,0:T(8,128)S(1)} %broadcast.7.modes_z_ref), custom_call_target="tpu_custom_call" | custom-call | flops 7516192768 | bytes 1277952 | tf_op jit(solution)/shard_map/spread/pallas_call | solution.py:256
  30.3 5.1 %collective-permute-done.4.points_ref = f32[8,8,2304]{2,1,0:T(8,128)S(1)} collective-permute-done((f32[8,8,2304]{2,1,0:T(8,128)S(1)}, f32[8,8,2304]{2,1,0:T(8,128)S(1)}, u32[]{:S(2)}, u32[]{:S(2)}) %collective-permute-start.4) | collective-permute-done | bytes 589856 | tf_op jit(solution)/shard_map/ppermute | solution.py:539
  35.4 13.5 %spread.11 = (f32[8,120,512]{2,1,0:T(8,128)S(1)}, f32[8,48,2048]{2,1,0:T(8,128)S(1)}) custom-call(f32[8,8,2304]{2,1,0:T(8,128)S(1)} %collective-permute-done.4.points_ref, f32[7,8,128]{2,1,0:T(8,128)S(1)} %broadcast.5.modes_y_ref, f32[7,16,128]{2,1,0:T(8,128)S(1)} %broadcast.7.modes_z_ref), custom_call_target="tpu_custom_call" | custom-call | flops 15032385536 | bytes 2555904 | tf_op jit(solution)/shard_map/spread/pallas_call | solution.py:256
  48.9 13.6 %spread.10 = (f32[8,120,512]{2,1,0:T(8,128)S(1)}, f32[8,48,2048]{2,1,0:T(8,128)S(1)}) custom-call(f32[8,8,2304]{2,1,0:T(8,128)S(1)} %collective-permute-done.6.points_ref, f32[7,8,128]{2,1,0:T(8,128)S(1)} %broadcast.5.modes_y_ref, f32[7,16,128]{2,1,0:T(8,128)S(1)} %broadcast.7.modes_z_ref), custom_call_target="tpu_custom_call" | custom-call | flops 15032385536 | bytes 2555904 | tf_op jit(solution)/shard_map/spread/pallas_call | solution.py:256
  62.6 13.6 %spread.6 = (f32[8,120,512]{2,1,0:T(8,128)S(1)}, f32[8,48,2048]{2,1,0:T(8,128)S(1)}) custom-call(f32[8,8,2304]{2,1,0:T(8,128)S(1)} %collective-permute-done.5.points_ref, f32[7,8,128]{2,1,0:T(8,128)S(1)} %broadcast.5.modes_y_ref, f32[7,16,128]{2,1,0:T(8,128)S(1)} %broadcast.7.modes_z_ref), custom_call_target="tpu_custom_call" | custom-call | flops 15032385536 | bytes 2555904 | tf_op jit(solution)/shard_map/spread/pallas_call | solution.py:256
  76.2 12.9 %solve.1.refs_1_ = f32[3,1032,512]{2,1,0:T(8,128)S(1)} custom-call(s32[32]{0:T(128)S(1)} %broadcast_xor_fusion.ids_ref, f32[1,120,512]{2,1,0:T(8,128)S(1)} %get-tuple-element.39.refs_0_, f32[3,120,512]{2,1,0:T(8,128)S(1)} %get-tuple-element.40.refs_1_, f32[4,120,512]{2,1,0:T(8,128)S(1)} %get-tuple-element.41.refs_2_, ...), custom_call_target="tpu_custom_call" | custom-call | flops 3623878656 | bytes 12582912 | tf_op jit(solution)/shard_map/solve/pallas_call | solution.py:379
  89.2 11.3 %interpolate.7 = f32[8,3,2048]{2,1,0:T(4,128)S(1)} custom-call(s32[32]{0:T(128)S(1)} %broadcast_xor_fusion.ids_ref, f32[8,8,2304]{2,1,0:T(8,128)S(1)} %collective-permute-done.5.points_ref, f32[8,48,2048]{2,1,0:T(8,128)S(1)} %get-tuple-element.38.refs_0_, f32[3,1032,512]{2,1,0:T(8,128)S(1)} %solve.1.refs_1_), custom_call_target="tpu_custom_call" | custom-call | flops 15032385536 | bytes 786432 | tf_op jit(solution)/shard_map/interpolate/pallas_call | solution.py:449
  101.1 11.1 %interpolate.8 = f32[8,3,2048]{2,1,0:T(4,128)S(1)} custom-call(s32[32]{0:T(128)S(1)} %broadcast_xor_fusion.ids_ref, f32[8,8,2304]{2,1,0:T(8,128)S(1)} %collective-permute-done.4.points_ref, f32[8,48,2048]{2,1,0:T(8,128)S(1)} %get-tuple-element.46.refs_0_, f32[3,1032,512]{2,1,0:T(8,128)S(1)} %solve.1.refs_1_), custom_call_target="tpu_custom_call" | custom-call | flops 15032385536 | bytes 786432 | tf_op jit(solution)/shard_map/interpolate/pallas_call | solution.py:449
  112.3 1.6 %collective-permute-start.8 = (f32[8,3,2048]{2,1,0:T(4,128)S(1)}, f32[8,3,2048]{2,1,0:T(4,128)S(1)}, u32[]{:S(2)}, u32[]{:S(2)}) collective-permute-start(f32[8,3,2048]{2,1,0:T(4,128)S(1)} %add.61), channel_id=1, source_target_pairs={{0,16},{1,17},{2,18},{3,19},{4,20},{5,21},{6,22},{7,23},{8,24},{9,... | collective-permute-start | bytes 589832 | tf_op jit(solution)/shard_map/ppermute | solution.py:539
  113.9 11.1 %interpolate.9 = f32[8,3,2048]{2,1,0:T(4,128)S(1)} custom-call(s32[32]{0:T(128)S(1)} %broadcast_xor_fusion.ids_ref, f32[8,8,2304]{2,1,0:T(8,128)S(1)} %collective-permute-done.6.points_ref, f32[8,48,2048]{2,1,0:T(8,128)S(1)} %get-tuple-element.50.refs_0_, f32[3,1032,512]{2,1,0:T(8,128)S(1)} %solve.1.refs_1_), custom_call_target="tpu_custom_call" | custom-call | flops 15032385536 | bytes 786432 | tf_op jit(solution)/shard_map/interpolate/pallas_call | solution.py:449
  125.1 5.8 %interpolate.10 = f32[4,3,2048]{2,1,0:T(4,128)S(1)} custom-call(s32[32]{0:T(128)S(1)} %broadcast_xor_fusion.ids_ref, f32[4,8,2304]{2,1,0:T(8,128)S(1)} %collective-permute-done.3.points_ref, f32[4,48,2048]{2,1,0:T(8,128)S(1)} %get-tuple-element.53.refs_0_, f32[3,1032,512]{2,1,0:T(8,128)S(1)} %solve.1.refs_1_), custom_call_target="tpu_custom_call" | custom-call | flops 7516192768 | bytes 393216 | tf_op jit(solution)/shard_map/interpolate/pallas_call | solution.py:449
  131.7 3.1 %interpolate.11 = f32[2,3,2048]{2,1,0:T(4,128)S(1)} custom-call(s32[32]{0:T(128)S(1)} %broadcast_xor_fusion.ids_ref, f32[3,8,2304]{2,1,0:T(8,128)S(1)} %get-tuple-element.71.points_ref, f32[3,48,2048]{2,1,0:T(8,128)S(1)} %get-tuple-element.59.refs_0_, f32[3,1032,512]{2,1,0:T(8,128)S(1)} %solve.1.refs_1_), custom_call_target="tpu_custom_call" | custom-call | flops 3758096384 | bytes 196608 | tf_op jit(solution)/shard_map/interpolate/pallas_call | solution.py:449
  134.8 2.2 %collective-permute-done.10 = f32[4,3,2048]{2,1,0:T(4,128)S(1)} collective-permute-done((f32[4,3,2048]{2,1,0:T(4,128)S(1)}, f32[4,3,2048]{2,1,0:T(4,128)S(1)}, u32[]{:S(2)}, u32[]{:S(2)}) %collective-permute-start.10) | collective-permute-done | bytes 98336 | tf_op jit(solution)/shard_map/ppermute | solution.py:539
  137.1 1.6 %collective-permute-start.11 = (f32[2,3,2048]{2,1,0:T(4,128)S(1)}, f32[2,3,2048]{2,1,0:T(4,128)S(1)}, u32[]{:S(2)}, u32[]{:S(2)}) collective-permute-start(f32[2,3,2048]{2,1,0:T(4,128)S(1)} %slice_add_fusion.2), channel_id=1, source_target_pairs={{0,8},{1,9},{2,10},{3,11},{4,12},{5,13},{6,14},{7,15},{8,0},{9,1},... | collective-permute-start | bytes 147464 | tf_op jit(solution)/shard_map/ppermute | solution.py:539
  138.7 1.8 %interpolate.12 = f32[1,3,2048]{2,1,0:T(4,128)S(1)} custom-call(s32[32]{0:T(128)S(1)} %broadcast_xor_fusion.ids_ref, f32[3,8,2304]{2,1,0:T(8,128)S(1)} %get-tuple-element.71.points_ref, f32[3,48,2048]{2,1,0:T(8,128)S(1)} %get-tuple-element.59.refs_0_, f32[3,1032,512]{2,1,0:T(8,128)S(1)} %solve.1.refs_1_), custom_call_target="tpu_custom_call" | custom-call | flops 1879048192 | bytes 98304 | tf_op jit(solution)/shard_map/interpolate/pallas_call | solution.py:449
  140.6 1.8 %interpolate.13 = f32[1,3,2048]{2,1,0:T(4,128)S(1)} custom-call(s32[32]{0:T(128)S(1)} %broadcast_xor_fusion.ids_ref, f32[1,8,2304]{2,1,0:T(8,128)S(1)} %copy-done.5, f32[1,48,2048]{2,1,0:T(8,128)S(1)} %get-tuple-element.64.refs_0_, f32[3,1032,512]{2,1,0:T(8,128)S(1)} %solve.1.refs_1_), custom_call_target="tpu_custom_call" | custom-call | flops 1879048192 | bytes 98304 | tf_op jit(solution)/shard_map/interpolate/pallas_call | solution.py:449
  143.3 1.7 %collective-permute-start.12 = (f32[1,3,2048]{2,1,0:T(4,128)S(1)}, f32[1,3,2048]{2,1,0:T(4,128)S(1)}, u32[]{:S(2)}, u32[]{:S(2)}) collective-permute-start(f32[1,3,2048]{2,1,0:T(4,128)S(1)} %fusion), channel_id=1, source_target_pairs={{0,4},{1,5},{2,6},{3,7},{4,0},{5,1},{6,2},{7,3},{8,12},{9,13},{10,... | collective-permute-start | bytes 73736 | tf_op jit(solution)/shard_map/ppermute | solution.py:539
  145.0 7.3 %near.1 = f32[3,2048]{1,0:T(4,128)S(1)} custom-call(s32[96]{0:T(128)S(1)} %reshape.8.pairs_ref, s32[1]{0:T(128)S(6)} %copy.22.count_ref, f32[3,2048]{1,0:T(4,128)S(1)} %copy-done.6, s32[3,2048]{1,0:T(4,128)S(1)} %copy-done.7, f32[3,2048]{1,0:T(4,128)S(1)} %copy-done.8), custom_call_target="tpu_custom_call" | custom-call | flops 4718592000 | bytes 98304 | tf_op jit(solution)/shard_map/near/pallas_call | solution.py:82
  (57 shorter events, 10.8 us)
Async XLA Ops:
  1.4 12.3 %collective-permute-start = (f32[1,8,2304]{2,1,0:T(8,128)}, f32[1,8,2304]{2,1,0:T(8,128)S(1)}, u32[]{:S(2)}, u32[]{:S(2)}) collective-permute-start(f32[1,8,2304]{2,1,0:T(8,128)} %pack.1.points_ref), channel_id=1, source_target_pairs={{0,4},{1,5},{2,6},{3,7},{4,0},{5,1},{6,2},{7,3},{8,12},{9,13},{10,... | collective-permute-start | bytes 221192 | tf_op jit(solution)/shard_map/ppermute | solution.py:539
  3.0 10.8 %collective-permute-start.1 = (f32[1,8,2304]{2,1,0:T(8,128)}, f32[1,8,2304]{2,1,0:T(8,128)S(1)}, u32[]{:S(2)}, u32[]{:S(2)}) collective-permute-start(f32[1,8,2304]{2,1,0:T(8,128)} %pack.1.points_ref), channel_id=1, source_target_pairs={{0,8},{1,9},{2,10},{3,11},{4,12},{5,13},{6,14},{7,15},{8,0},{9,1},... | collective-permute-start | bytes 221192 | tf_op jit(solution)/shard_map/ppermute | solution.py:539
  5.6 8.2 %collective-permute-start.2 = (f32[1,8,2304]{2,1,0:T(8,128)}, f32[1,8,2304]{2,1,0:T(8,128)S(1)}, u32[]{:S(2)}, u32[]{:S(2)}) collective-permute-start(f32[1,8,2304]{2,1,0:T(8,128)} %pack.1.points_ref), channel_id=1, source_target_pairs={{0,12},{1,13},{2,14},{3,15},{4,8},{5,9},{6,10},{7,11},{8,4},{9,5},... | collective-permute-start | bytes 221192 | tf_op jit(solution)/shard_map/ppermute | solution.py:539
  10.5 0.9 copy-start.4
  13.8 8.1 %collective-permute-start.3 = (f32[4,8,2304]{2,1,0:T(8,128)S(1)}, f32[4,8,2304]{2,1,0:T(8,128)S(1)}, u32[]{:S(2)}, u32[]{:S(2)}) collective-permute-start(f32[4,8,2304]{2,1,0:T(8,128)S(1)} %pad_maximum_fusion), channel_id=1, source_target_pairs={{0,2},{1,3},{2,0},{3,1},{4,6},{5,7},{6,4},{7,5},{8,10},{9,11},{10,... | collective-permute-start | bytes 884744 | tf_op jit(solution)/shard_map/ppermute | solution.py:539
  21.9 13.5 %collective-permute-start.4 = (f32[8,8,2304]{2,1,0:T(8,128)S(1)}, f32[8,8,2304]{2,1,0:T(8,128)S(1)}, u32[]{:S(2)}, u32[]{:S(2)}) collective-permute-start(f32[8,8,2304]{2,1,0:T(8,128)S(1)} %constant_dynamic-update-slice_fusion), channel_id=1, source_target_pairs={{0,16},{1,17},{2,18},{3,19},{4,20},{5,21},{6,22},{7,23},{8,24},{9,... | collective-permute-start | bytes 1769480 | tf_op jit(solution)/shard_map/ppermute | solution.py:539
  23.5 25.4 %collective-permute-start.6 = (f32[8,8,2304]{2,1,0:T(8,128)S(1)}, f32[8,8,2304]{2,1,0:T(8,128)S(1)}, u32[]{:S(2)}, u32[]{:S(2)}) collective-permute-start(f32[8,8,2304]{2,1,0:T(8,128)S(1)} %constant_dynamic-update-slice_fusion), channel_id=1, source_target_pairs={{0,1},{1,0},{2,3},{3,2},{4,5},{5,4},{6,7},{7,6},{8,9},{9,8},{10,11... | collective-permute-start | bytes 1769480 | tf_op jit(solution)/shard_map/ppermute | solution.py:539
  35.4 27.2 %collective-permute-start.5 = (f32[8,8,2304]{2,1,0:T(8,128)S(1)}, f32[8,8,2304]{2,1,0:T(8,128)S(1)}, u32[]{:S(2)}, u32[]{:S(2)}) collective-permute-start(f32[8,8,2304]{2,1,0:T(8,128)S(1)} %collective-permute-done.4.points_ref), channel_id=1, source_target_pairs={{0,1},{1,0},{2,3},{3,2},{4,5},{5,4},{6,7},{7,6},{8,9},{9,8},{10,11... | collective-permute-start | bytes 1769480 | tf_op jit(solution)/shard_map/ppermute | solution.py:539
  62.5 13.6 %copy-start = (bf16[512,1536]{1,0:T(8,128)(2,1)S(1)}, bf16[512,1536]{1,0:T(8,128)(2,1)}, u32[]{:S(2)}) copy-start(bf16[512,1536]{1,0:T(8,128)(2,1)} %constant.74.clone.refs_7_) | copy-start | bytes 4718596
  62.5 13.6 %copy-start.1 = (bf16[512,1536]{1,0:T(8,128)(2,1)S(1)}, bf16[512,1536]{1,0:T(8,128)(2,1)}, u32[]{:S(2)}) copy-start(bf16[512,1536]{1,0:T(8,128)(2,1)} %constant.76.clone.refs_9_) | copy-start | bytes 4718596
  62.6 13.6 %copy-start.2 = (bf16[2,256,768]{2,1,0:T(8,128)(2,1)S(1)}, bf16[2,256,768]{2,1,0:T(8,128)(2,1)}, u32[]{:S(2)}) copy-start(bf16[2,256,768]{2,1,0:T(8,128)(2,1)} %constant.73.clone.refs_6_) | copy-start | bytes 2359300
  62.6 13.6 %copy-start.3 = (bf16[2,256,768]{2,1,0:T(8,128)(2,1)S(1)}, bf16[2,256,768]{2,1,0:T(8,128)(2,1)}, u32[]{:S(2)}) copy-start(bf16[2,256,768]{2,1,0:T(8,128)(2,1)} %constant.75.clone.refs_8_) | copy-start | bytes 2359300
  100.5 11.7 %collective-permute-start.7 = (f32[8,3,2048]{2,1,0:T(4,128)S(1)}, f32[8,3,2048]{2,1,0:T(4,128)S(1)}, u32[]{:S(2)}, u32[]{:S(2)}) collective-permute-start(f32[8,3,2048]{2,1,0:T(4,128)S(1)} %interpolate.7), channel_id=1, source_target_pairs={{0,1},{1,0},{2,3},{3,2},{4,5},{5,4},{6,7},{7,6},{8,9},{9,8},{10,11... | collective-permute-start | bytes 589832 | tf_op jit(solution)/shard_map/ppermute | solution.py:539
  112.3 12.7 %collective-permute-start.8 = (f32[8,3,2048]{2,1,0:T(4,128)S(1)}, f32[8,3,2048]{2,1,0:T(4,128)S(1)}, u32[]{:S(2)}, u32[]{:S(2)}) collective-permute-start(f32[8,3,2048]{2,1,0:T(4,128)S(1)} %add.61), channel_id=1, source_target_pairs={{0,16},{1,17},{2,18},{3,19},{4,20},{5,21},{6,22},{7,23},{8,24},{9,... | collective-permute-start | bytes 589832 | tf_op jit(solution)/shard_map/ppermute | solution.py:539
  125.0 5.9 %collective-permute-start.9 = (f32[8,3,2048]{2,1,0:T(4,128)S(1)}, f32[8,3,2048]{2,1,0:T(4,128)S(1)}, u32[]{:S(2)}, u32[]{:S(2)}) collective-permute-start(f32[8,3,2048]{2,1,0:T(4,128)S(1)} %interpolate.9), channel_id=1, source_target_pairs={{0,1},{1,0},{2,3},{3,2},{4,5},{5,4},{6,7},{7,6},{8,9},{9,8},{10,11... | collective-permute-start | bytes 589832 | tf_op jit(solution)/shard_map/ppermute | solution.py:539
  131.1 6.0 %collective-permute-start.10 = (f32[4,3,2048]{2,1,0:T(4,128)S(1)}, f32[4,3,2048]{2,1,0:T(4,128)S(1)}, u32[]{:S(2)}, u32[]{:S(2)}) collective-permute-start(f32[4,3,2048]{2,1,0:T(4,128)S(1)} %slice_add_fusion.1), channel_id=1, source_target_pairs={{0,2},{1,3},{2,0},{3,1},{4,6},{5,7},{6,4},{7,5},{8,10},{9,11},{10,... | collective-permute-start | bytes 294920 | tf_op jit(solution)/shard_map/ppermute | solution.py:539
  137.1 3.4 %copy-start.5 = (f32[1,8,2304]{2,1,0:T(8,128)S(1)}, f32[1,8,2304]{2,1,0:T(8,128)}, u32[]{:S(2)}) copy-start(f32[1,8,2304]{2,1,0:T(8,128)} %pack.1.points_ref) | copy-start | bytes 221188
  137.1 6.1 %collective-permute-start.11 = (f32[2,3,2048]{2,1,0:T(4,128)S(1)}, f32[2,3,2048]{2,1,0:T(4,128)S(1)}, u32[]{:S(2)}, u32[]{:S(2)}) collective-permute-start(f32[2,3,2048]{2,1,0:T(4,128)S(1)} %slice_add_fusion.2), channel_id=1, source_target_pairs={{0,8},{1,9},{2,10},{3,11},{4,12},{5,13},{6,14},{7,15},{8,0},{9,1},... | collective-permute-start | bytes 147464 | tf_op jit(solution)/shard_map/ppermute | solution.py:539
  140.5 4.5 %copy-start.6 = (f32[3,2048]{1,0:T(4,128)S(1)}, f32[3,2048]{1,0:T(4,128)}, u32[]{:S(2)}) copy-start(f32[3,2048]{1,0:T(4,128)} %forces_ref.2) | copy-start | bytes 73732
  140.5 4.5 %copy-start.7 = (s32[3,2048]{1,0:T(4,128)S(1)}, s32[3,2048]{1,0:T(4,128)}, u32[]{:S(2)}) copy-start(s32[3,2048]{1,0:T(4,128)} %start_ref.3) | copy-start | bytes 73732
  140.5 4.4 %copy-start.8 = (f32[3,2048]{1,0:T(4,128)S(1)}, f32[3,2048]{1,0:T(4,128)}, u32[]{:S(2)}) copy-start(f32[3,2048]{1,0:T(4,128)} %fraction_ref.3) | copy-start | bytes 73732
  143.3 9.0 %collective-permute-start.12 = (f32[1,3,2048]{2,1,0:T(4,128)S(1)}, f32[1,3,2048]{2,1,0:T(4,128)S(1)}, u32[]{:S(2)}, u32[]{:S(2)}) collective-permute-start(f32[1,3,2048]{2,1,0:T(4,128)S(1)} %fusion), channel_id=1, source_target_pairs={{0,4},{1,5},{2,6},{3,7},{4,0},{5,1},{6,2},{7,3},{8,12},{9,13},{10,... | collective-permute-start | bytes 73736 | tf_op jit(solution)/shard_map/ppermute | solution.py:539

commit v2 on v1

--- a/solution.py
+++ b/solution.py
@@ -407,12 +407,12 @@
     plane[LANES:] = low
     main, last = unpack(points_ref[0])
     count = main.shape[1]
-    chunk = count // 4
+    chunk = count // 2
     if kept:
         own_y = basis_refs[0].shape[1] // 2 - KZ
     else:
         modes_y, modes_z = [[ref[i] for i in range(7)] for ref in basis_refs]
-    for index in range(4):
+    for index in range(2):
         at = slice(index * chunk, (index + 1) * chunk)
         if kept:
             rows_y = [basis_refs[0][0, i * own_y : (i + 1) * own_y, at] for i in range(2)]
@@ -557,7 +557,12 @@
     modes_y, modes_z, waves = far_tables(device, devices)
     tables = [jnp.asarray(table) for table in line_tables()]
     keep = keeps(own, modes_y)
-    spreads = [spread(points, modes_y, modes_z, rows, keep) for points in parts]
+    spreads = []
+    modes = modes_y
+    for points in parts:
+        result = spread(points, modes, modes_z, rows, keep)
+        piece, modes = lax.optimization_barrier((result[0], modes_y))
+        spreads.append([piece, *result[1:]])
     pieces = [result[0] for result in spreads]
     lines = solve(pieces, ids, waves, tables, planes, rows)
     firsts = np.cumsum([0] + [points.shape[0] for points in parts])

time: 155 us -> 148 us (0.955)
  the two profiles are of different devices: /device:TPU:2 before, /device:TPU:0 now
where the time goes in v2:
time: 148 us
  Pallas kernels  122 us (82%)
  starting transfers between devices  15.4 us (10%)
  local copies, waits for them, and re-layouts  4.39 us (3%)
  waiting for transfers between devices  3.22 us (2%)
  other arithmetic  1.58 us (1%)
    pallas_call x6, Pallas kernels, spread(): pl.pallas_call(functools.partial(spread_kernel, rows), grid=(blocks,), in...  54.4 us
    pallas_call x7, Pallas kernels, gather(): pl.pallas_call(functools.partial(gather_kernel, planes, rows, before, kep...  43.8 us
    ppermute x13, starting transfers between devices, from_flipped(): return lax.ppermute(values, ('group', 'dev'), pairs)  15.4 us
    pallas_call x1, Pallas kernels, solve(): pl.pallas_call(functools.partial(solve_kernel, planes, rows, len(pieces))...  12.9 us
    pallas_call x1, Pallas kernels, near_field(): pl.pallas_call(near_kernel, in_specs=[smem, smem, vmem, vmem, vmem], out_...  9.69 us
    ppermute x13, waiting for transfers between devices, from_flipped(): return lax.ppermute(values, ('group', 'dev'), pairs)  3.22 us
  transfers between devices with their start and end apart: 13, of which 3 were waited for; matrix products, arithmetic and copies ran while one was open for 3% of the time, Pallas kernels for 56%

profile of v2, /device:TPU:0, one launch (start us, length us, event | category | flops | bytes accessed | tf_op | source)
XLA Modules:
  0.0 148.0 jit_solution(6329968871724087065)
XLA Ops:
  0.0 1.4 pack.1.points_ref
  1.5 3.0 %collective-permute-start = (f32[1,8,2304]{2,1,0:T(8,128)}, f32[1,8,2304]{2,1,0:T(8,128)S(1)}, u32[]{:S(2)}, u32[]{:S(2)}) collective-permute-start(f32[1,8,2304]{2,1,0:T(8,128)} %pack.1.points_ref), channel_id=1, source_target_pairs={{0,4},{1,5},{2,6},{3,7},{4,0},{5,1},{6,2},{7,3},{8,12},{9,13},{10,... | collective-permute-start | bytes 221192 | tf_op jit(solution)/shard_map/ppermute | solution.py:539
  4.5 2.6 %collective-permute-start.1 = (f32[1,8,2304]{2,1,0:T(8,128)}, f32[1,8,2304]{2,1,0:T(8,128)S(1)}, u32[]{:S(2)}, u32[]{:S(2)}) collective-permute-start(f32[1,8,2304]{2,1,0:T(8,128)} %pack.1.points_ref), channel_id=1, source_target_pairs={{0,8},{1,9},{2,10},{3,11},{4,12},{5,13},{6,14},{7,15},{8,0},{9,1},... | collective-permute-start | bytes 221192 | tf_op jit(solution)/shard_map/ppermute | solution.py:539
  11.1 1.7 %spread.6 = (f32[1,120,512]{2,1,0:T(8,128)S(1)}, f32[1,48,2048]{2,1,0:T(8,128)S(1)}) custom-call(f32[1,8,2304]{2,1,0:T(8,128)S(1)} %copy-done.4, f32[7,8,128]{2,1,0:T(8,128)S(1)} %broadcast.5.modes_y_ref, f32[7,16,128]{2,1,0:T(8,128)S(1)} %broadcast.7.modes_z_ref), custom_call_target="tpu_custom_call" | custom-call | flops 1879048192 | bytes 319488 | tf_op jit(solution)/shard_map/spread/pallas_call | solution.py:256
  14.4 1.7 %collective-permute-start.3 = (f32[4,8,2304]{2,1,0:T(8,128)S(1)}, f32[4,8,2304]{2,1,0:T(8,128)S(1)}, u32[]{:S(2)}, u32[]{:S(2)}) collective-permute-start(f32[4,8,2304]{2,1,0:T(8,128)S(1)} %pad_maximum_fusion), channel_id=1, source_target_pairs={{0,2},{1,3},{2,0},{3,1},{4,6},{5,7},{6,4},{7,5},{8,10},{9,11},{10,... | collective-permute-start | bytes 884744 | tf_op jit(solution)/shard_map/ppermute | solution.py:539
  16.2 5.3 %spread.7 = (f32[3,120,512]{2,1,0:T(8,128)S(1)}, f32[3,48,2048]{2,1,0:T(8,128)S(1)}) custom-call(f32[3,8,2304]{2,1,0:T(8,128)S(1)} %get-tuple-element.93.points_ref, f32[7,8,128]{2,1,0:T(8,128)S(1)} %broadcast.5.modes_y_ref, f32[7,16,128]{2,1,0:T(8,128)S(1)} %broadcast.7.modes_z_ref), custom_call_target="tpu_custom_call" | custom-call | flops 5637144576 | bytes 958464 | tf_op jit(solution)/shard_map/spread/pallas_call | solution.py:256
  22.7 1.6 %collective-permute-start.4 = (f32[8,8,2304]{2,1,0:T(8,128)S(1)}, f32[8,8,2304]{2,1,0:T(8,128)S(1)}, u32[]{:S(2)}, u32[]{:S(2)}) collective-permute-start(f32[8,8,2304]{2,1,0:T(8,128)S(1)} %constant_dynamic-update-slice_fusion), channel_id=1, source_target_pairs={{0,16},{1,17},{2,18},{3,19},{4,20},{5,21},{6,22},{7,23},{8,24},{9,... | collective-permute-start | bytes 1769480 | tf_op jit(solution)/shard_map/ppermute | solution.py:539
  24.3 6.8 %spread.8 = (f32[4,120,512]{2,1,0:T(8,128)S(1)}, f32[4,48,2048]{2,1,0:T(8,128)S(1)}) custom-call(f32[4,8,2304]{2,1,0:T(8,128)S(1)} %collective-permute-done.3.points_ref, f32[7,8,128]{2,1,0:T(8,128)S(1)} %broadcast.5.modes_y_ref, f32[7,16,128]{2,1,0:T(8,128)S(1)} %broadcast.7.modes_z_ref), custom_call_target="tpu_custom_call" | custom-call | flops 7516192768 | bytes 1277952 | tf_op jit(solution)/shard_map/spread/pallas_call | solution.py:256
  31.1 13.6 %spread.9 = (f32[8,120,512]{2,1,0:T(8,128)S(1)}, f32[8,48,2048]{2,1,0:T(8,128)S(1)}) custom-call(f32[8,8,2304]{2,1,0:T(8,128)S(1)} %collective-permute-done.6.points_ref, f32[7,8,128]{2,1,0:T(8,128)S(1)} %broadcast.5.modes_y_ref, f32[7,16,128]{2,1,0:T(8,128)S(1)} %broadcast.7.modes_z_ref), custom_call_target="tpu_custom_call" | custom-call | flops 15032385536 | bytes 2555904 | tf_op jit(solution)/shard_map/spread/pallas_call | solution.py:256
  45.3 13.5 %spread.10 = (f32[8,120,512]{2,1,0:T(8,128)S(1)}, f32[8,48,2048]{2,1,0:T(8,128)S(1)}) custom-call(f32[8,8,2304]{2,1,0:T(8,128)S(1)} %collective-permute-done.4.points_ref, f32[7,8,128]{2,1,0:T(8,128)S(1)} %broadcast.5.modes_y_ref, f32[7,16,128]{2,1,0:T(8,128)S(1)} %broadcast.7.modes_z_ref), custom_call_target="tpu_custom_call" | custom-call | flops 15032385536 | bytes 2555904 | tf_op jit(solution)/shard_map/spread/pallas_call | solution.py:256
  58.9 13.6 %spread.11 = (f32[8,120,512]{2,1,0:T(8,128)S(1)}, f32[8,48,2048]{2,1,0:T(8,128)S(1)}) custom-call(f32[8,8,2304]{2,1,0:T(8,128)S(1)} %collective-permute-done.5.points_ref, f32[7,8,128]{2,1,0:T(8,128)S(1)} %broadcast.5.modes_y_ref, f32[7,16,128]{2,1,0:T(8,128)S(1)} %broadcast.7.modes_z_ref), custom_call_target="tpu_custom_call" | custom-call | flops 15032385536 | bytes 2555904 | tf_op jit(solution)/shard_map/spread/pallas_call | solution.py:256
  72.5 12.9 %solve.1.refs_1_ = f32[3,1032,512]{2,1,0:T(8,128)S(1)} custom-call(s32[32]{0:T(128)S(1)} %broadcast_xor_fusion.ids_ref, f32[1,120,512]{2,1,0:T(8,128)S(1)} %get-tuple-element.60.refs_0_, f32[3,120,512]{2,1,0:T(8,128)S(1)} %get-tuple-element.61.refs_1_, f32[4,120,512]{2,1,0:T(8,128)S(1)} %get-tuple-element.62.refs_2_, ...), custom_call_target="tpu_custom_call" | custom-call | flops 3623878656 | bytes 12582912 | tf_op jit(solution)/shard_map/solve/pallas_call | solution.py:379
  85.4 10.8 %interpolate.7 = f32[8,3,2048]{2,1,0:T(4,128)S(1)} custom-call(s32[32]{0:T(128)S(1)} %broadcast_xor_fusion.ids_ref, f32[8,8,2304]{2,1,0:T(8,128)S(1)} %collective-permute-done.5.points_ref, f32[8,48,2048]{2,1,0:T(8,128)S(1)} %get-tuple-element.59.refs_0_, f32[3,1032,512]{2,1,0:T(8,128)S(1)} %solve.1.refs_1_), custom_call_target="tpu_custom_call" | custom-call | flops 15032385536 | bytes 786432 | tf_op jit(solution)/shard_map/interpolate/pallas_call | solution.py:449
  96.3 10.5 %interpolate.8 = f32[8,3,2048]{2,1,0:T(4,128)S(1)} custom-call(s32[32]{0:T(128)S(1)} %broadcast_xor_fusion.ids_ref, f32[8,8,2304]{2,1,0:T(8,128)S(1)} %collective-permute-done.4.points_ref, f32[8,48,2048]{2,1,0:T(8,128)S(1)} %get-tuple-element.68.refs_0_, f32[3,1032,512]{2,1,0:T(8,128)S(1)} %solve.1.refs_1_), custom_call_target="tpu_custom_call" | custom-call | flops 15032385536 | bytes 786432 | tf_op jit(solution)/shard_map/interpolate/pallas_call | solution.py:449
  107.5 10.5 %interpolate.9 = f32[8,3,2048]{2,1,0:T(4,128)S(1)} custom-call(s32[32]{0:T(128)S(1)} %broadcast_xor_fusion.ids_ref, f32[8,8,2304]{2,1,0:T(8,128)S(1)} %collective-permute-done.6.points_ref, f32[8,48,2048]{2,1,0:T(8,128)S(1)} %get-tuple-element.72.refs_0_, f32[3,1032,512]{2,1,0:T(8,128)S(1)} %solve.1.refs_1_), custom_call_target="tpu_custom_call" | custom-call | flops 15032385536 | bytes 786432 | tf_op jit(solution)/shard_map/interpolate/pallas_call | solution.py:449
  118.3 5.5 %interpolate.10 = f32[4,3,2048]{2,1,0:T(4,128)S(1)} custom-call(s32[32]{0:T(128)S(1)} %broadcast_xor_fusion.ids_ref, f32[4,8,2304]{2,1,0:T(8,128)S(1)} %collective-permute-done.3.points_ref, f32[4,48,2048]{2,1,0:T(8,128)S(1)} %get-tuple-element.75.refs_0_, f32[3,1032,512]{2,1,0:T(8,128)S(1)} %solve.1.refs_1_), custom_call_target="tpu_custom_call" | custom-call | flops 7516192768 | bytes 393216 | tf_op jit(solution)/shard_map/interpolate/pallas_call | solution.py:449
  124.0 1.5 %collective-permute-start.10 = (f32[4,3,2048]{2,1,0:T(4,128)S(1)}, f32[4,3,2048]{2,1,0:T(4,128)S(1)}, u32[]{:S(2)}, u32[]{:S(2)}) collective-permute-start(f32[4,3,2048]{2,1,0:T(4,128)S(1)} %slice_add_fusion.1), channel_id=1, source_target_pairs={{0,2},{1,3},{2,0},{3,1},{4,6},{5,7},{6,4},{7,5},{8,10},{9,11},{10,... | collective-permute-start | bytes 294920 | tf_op jit(solution)/shard_map/ppermute | solution.py:539
  125.5 3.0 %interpolate.11 = f32[2,3,2048]{2,1,0:T(4,128)S(1)} custom-call(s32[32]{0:T(128)S(1)} %broadcast_xor_fusion.ids_ref, f32[3,8,2304]{2,1,0:T(8,128)S(1)} %get-tuple-element.93.points_ref, f32[3,48,2048]{2,1,0:T(8,128)S(1)} %get-tuple-element.81.refs_0_, f32[3,1032,512]{2,1,0:T(8,128)S(1)} %solve.1.refs_1_), custom_call_target="tpu_custom_call" | custom-call | flops 3758096384 | bytes 196608 | tf_op jit(solution)/shard_map/interpolate/pallas_call | solution.py:449
  128.5 1.2 collective-permute-done.10
  129.8 1.7 %collective-permute-start.11 = (f32[2,3,2048]{2,1,0:T(4,128)S(1)}, f32[2,3,2048]{2,1,0:T(4,128)S(1)}, u32[]{:S(2)}, u32[]{:S(2)}) collective-permute-start(f32[2,3,2048]{2,1,0:T(4,128)S(1)} %slice_add_fusion.2), channel_id=1, source_target_pairs={{0,8},{1,9},{2,10},{3,11},{4,12},{5,13},{6,14},{7,15},{8,0},{9,1},... | collective-permute-start | bytes 147464 | tf_op jit(solution)/shard_map/ppermute | solution.py:539
  131.5 1.8 %interpolate.12 = f32[1,3,2048]{2,1,0:T(4,128)S(1)} custom-call(s32[32]{0:T(128)S(1)} %broadcast_xor_fusion.ids_ref, f32[3,8,2304]{2,1,0:T(8,128)S(1)} %get-tuple-element.93.points_ref, f32[3,48,2048]{2,1,0:T(8,128)S(1)} %get-tuple-element.81.refs_0_, f32[3,1032,512]{2,1,0:T(8,128)S(1)} %solve.1.refs_1_), custom_call_target="tpu_custom_call" | custom-call | flops 1879048192 | bytes 98304 | tf_op jit(solution)/shard_map/interpolate/pallas_call | solution.py:449
  133.3 1.8 %interpolate.13 = f32[1,3,2048]{2,1,0:T(4,128)S(1)} custom-call(s32[32]{0:T(128)S(1)} %broadcast_xor_fusion.ids_ref, f32[1,8,2304]{2,1,0:T(8,128)S(1)} %copy-done.5, f32[1,48,2048]{2,1,0:T(8,128)S(1)} %get-tuple-element.86.refs_0_, f32[3,1032,512]{2,1,0:T(8,128)S(1)} %solve.1.refs_1_), custom_call_target="tpu_custom_call" | custom-call | flops 1879048192 | bytes 98304 | tf_op jit(solution)/shard_map/interpolate/pallas_call | solution.py:449
  135.8 1.8 %collective-permute-start.12 = (f32[1,3,2048]{2,1,0:T(4,128)S(1)}, f32[1,3,2048]{2,1,0:T(4,128)S(1)}, u32[]{:S(2)}, u32[]{:S(2)}) collective-permute-start(f32[1,3,2048]{2,1,0:T(4,128)S(1)} %fusion), channel_id=1, source_target_pairs={{0,4},{1,5},{2,6},{3,7},{4,0},{5,1},{6,2},{7,3},{8,12},{9,13},{10,... | collective-permute-start | bytes 73736 | tf_op jit(solution)/shard_map/ppermute | solution.py:539
  137.6 9.7 %near.1 = f32[3,2048]{1,0:T(4,128)S(1)} custom-call(s32[96]{0:T(128)S(1)} %reshape.8.pairs_ref, s32[1]{0:T(128)S(6)} %copy.22.count_ref, f32[3,2048]{1,0:T(4,128)S(1)} %copy-done.6, s32[3,2048]{1,0:T(4,128)S(1)} %copy-done.7, f32[3,2048]{1,0:T(4,128)S(1)} %copy-done.8), custom_call_target="tpu_custom_call" | custom-call | flops 4718592000 | bytes 98304 | tf_op jit(solution)/shard_map/near/pallas_call | solution.py:82
  (59 shorter events, 9.5 us)
Async XLA Ops:
  1.5 12.9 %collective-permute-start = (f32[1,8,2304]{2,1,0:T(8,128)}, f32[1,8,2304]{2,1,0:T(8,128)S(1)}, u32[]{:S(2)}, u32[]{:S(2)}) collective-permute-start(f32[1,8,2304]{2,1,0:T(8,128)} %pack.1.points_ref), channel_id=1, source_target_pairs={{0,4},{1,5},{2,6},{3,7},{4,0},{5,1},{6,2},{7,3},{8,12},{9,13},{10,... | collective-permute-start | bytes 221192 | tf_op jit(solution)/shard_map/ppermute | solution.py:539
  4.5 9.9 %collective-permute-start.1 = (f32[1,8,2304]{2,1,0:T(8,128)}, f32[1,8,2304]{2,1,0:T(8,128)S(1)}, u32[]{:S(2)}, u32[]{:S(2)}) collective-permute-start(f32[1,8,2304]{2,1,0:T(8,128)} %pack.1.points_ref), channel_id=1, source_target_pairs={{0,8},{1,9},{2,10},{3,11},{4,12},{5,13},{6,14},{7,15},{8,0},{9,1},... | collective-permute-start | bytes 221192 | tf_op jit(solution)/shard_map/ppermute | solution.py:539
  7.1 7.3 %collective-permute-start.2 = (f32[1,8,2304]{2,1,0:T(8,128)}, f32[1,8,2304]{2,1,0:T(8,128)S(1)}, u32[]{:S(2)}, u32[]{:S(2)}) collective-permute-start(f32[1,8,2304]{2,1,0:T(8,128)} %pack.1.points_ref), channel_id=1, source_target_pairs={{0,12},{1,13},{2,14},{3,15},{4,8},{5,9},{6,10},{7,11},{8,4},{9,5},... | collective-permute-start | bytes 221192 | tf_op jit(solution)/shard_map/ppermute | solution.py:539
  10.2 0.9 copy-start.4
  11.1 1.7 %copy-start.9 = (s32[48,2]{0,1:T(2,128)S(1)}, s32[48,2]{0,1:T(2,128)}, u32[]{:S(2)}) copy-start(s32[48,2]{0,1:T(2,128)} %param.16) | copy-start | bytes 1156
  11.1 3.3 %copy-start.5 = (f32[1,8,2304]{2,1,0:T(8,128)S(1)}, f32[1,8,2304]{2,1,0:T(8,128)}, u32[]{:S(2)}) copy-start(f32[1,8,2304]{2,1,0:T(8,128)} %pack.1.points_ref) | copy-start | bytes 221188
  14.4 8.3 %collective-permute-start.3 = (f32[4,8,2304]{2,1,0:T(8,128)S(1)}, f32[4,8,2304]{2,1,0:T(8,128)S(1)}, u32[]{:S(2)}, u32[]{:S(2)}) collective-permute-start(f32[4,8,2304]{2,1,0:T(8,128)S(1)} %pad_maximum_fusion), channel_id=1, source_target_pairs={{0,2},{1,3},{2,0},{3,1},{4,6},{5,7},{6,4},{7,5},{8,10},{9,11},{10,... | collective-permute-start | bytes 884744 | tf_op jit(solution)/shard_map/ppermute | solution.py:539
  22.7 22.0 %collective-permute-start.4 = (f32[8,8,2304]{2,1,0:T(8,128)S(1)}, f32[8,8,2304]{2,1,0:T(8,128)S(1)}, u32[]{:S(2)}, u32[]{:S(2)}) collective-permute-start(f32[8,8,2304]{2,1,0:T(8,128)S(1)} %constant_dynamic-update-slice_fusion), channel_id=1, source_target_pairs={{0,16},{1,17},{2,18},{3,19},{4,20},{5,21},{6,22},{7,23},{8,24},{9,... | collective-permute-start | bytes 1769480 | tf_op jit(solution)/shard_map/ppermute | solution.py:539
  24.3 6.8 %collective-permute-start.6 = (f32[8,8,2304]{2,1,0:T(8,128)S(1)}, f32[8,8,2304]{2,1,0:T(8,128)S(1)}, u32[]{:S(2)}, u32[]{:S(2)}) collective-permute-start(f32[8,8,2304]{2,1,0:T(8,128)S(1)} %constant_dynamic-update-slice_fusion), channel_id=1, source_target_pairs={{0,1},{1,0},{2,3},{3,2},{4,5},{5,4},{6,7},{7,6},{8,9},{9,8},{10,11... | collective-permute-start | bytes 1769480 | tf_op jit(solution)/shard_map/ppermute | solution.py:539
  44.7 14.2 %collective-permute-start.5 = (f32[8,8,2304]{2,1,0:T(8,128)S(1)}, f32[8,8,2304]{2,1,0:T(8,128)S(1)}, u32[]{:S(2)}, u32[]{:S(2)}) collective-permute-start(f32[8,8,2304]{2,1,0:T(8,128)S(1)} %collective-permute-done.4.points_ref), channel_id=1, source_target_pairs={{0,1},{1,0},{2,3},{3,2},{4,5},{5,4},{6,7},{7,6},{8,9},{9,8},{10,11... | collective-permute-start | bytes 1769480 | tf_op jit(solution)/shard_map/ppermute | solution.py:539
  58.8 13.6 %copy-start = (bf16[512,1536]{1,0:T(8,128)(2,1)S(1)}, bf16[512,1536]{1,0:T(8,128)(2,1)}, u32[]{:S(2)}) copy-start(bf16[512,1536]{1,0:T(8,128)(2,1)} %constant.74.clone.refs_7_) | copy-start | bytes 4718596
  58.8 13.6 %copy-start.1 = (bf16[512,1536]{1,0:T(8,128)(2,1)S(1)}, bf16[512,1536]{1,0:T(8,128)(2,1)}, u32[]{:S(2)}) copy-start(bf16[512,1536]{1,0:T(8,128)(2,1)} %constant.76.clone.refs_9_) | copy-start | bytes 4718596
  58.8 13.6 %copy-start.2 = (bf16[2,256,768]{2,1,0:T(8,128)(2,1)S(1)}, bf16[2,256,768]{2,1,0:T(8,128)(2,1)}, u32[]{:S(2)}) copy-start(bf16[2,256,768]{2,1,0:T(8,128)(2,1)} %constant.73.clone.refs_6_) | copy-start | bytes 2359300
  58.8 13.6 %copy-start.3 = (bf16[2,256,768]{2,1,0:T(8,128)(2,1)S(1)}, bf16[2,256,768]{2,1,0:T(8,128)(2,1)}, u32[]{:S(2)}) copy-start(bf16[2,256,768]{2,1,0:T(8,128)(2,1)} %constant.75.clone.refs_8_) | copy-start | bytes 2359300
  96.2 10.6 %collective-permute-start.7 = (f32[8,3,2048]{2,1,0:T(4,128)S(1)}, f32[8,3,2048]{2,1,0:T(4,128)S(1)}, u32[]{:S(2)}, u32[]{:S(2)}) collective-permute-start(f32[8,3,2048]{2,1,0:T(4,128)S(1)} %interpolate.7), channel_id=1, source_target_pairs={{0,1},{1,0},{2,3},{3,2},{4,5},{5,4},{6,7},{7,6},{8,9},{9,8},{10,11... | collective-permute-start | bytes 589832 | tf_op jit(solution)/shard_map/ppermute | solution.py:539
  106.9 11.1 %collective-permute-start.8 = (f32[8,3,2048]{2,1,0:T(4,128)S(1)}, f32[8,3,2048]{2,1,0:T(4,128)S(1)}, u32[]{:S(2)}, u32[]{:S(2)}) collective-permute-start(f32[8,3,2048]{2,1,0:T(4,128)S(1)} %add.61), channel_id=1, source_target_pairs={{0,16},{1,17},{2,18},{3,19},{4,20},{5,21},{6,22},{7,23},{8,24},{9,... | collective-permute-start | bytes 589832 | tf_op jit(solution)/shard_map/ppermute | solution.py:539
  118.0 5.8 %collective-permute-start.9 = (f32[8,3,2048]{2,1,0:T(4,128)S(1)}, f32[8,3,2048]{2,1,0:T(4,128)S(1)}, u32[]{:S(2)}, u32[]{:S(2)}) collective-permute-start(f32[8,3,2048]{2,1,0:T(4,128)S(1)} %interpolate.9), channel_id=1, source_target_pairs={{0,1},{1,0},{2,3},{3,2},{4,5},{5,4},{6,7},{7,6},{8,9},{9,8},{10,11... | collective-permute-start | bytes 589832 | tf_op jit(solution)/shard_map/ppermute | solution.py:539
  124.0 5.8 %collective-permute-start.10 = (f32[4,3,2048]{2,1,0:T(4,128)S(1)}, f32[4,3,2048]{2,1,0:T(4,128)S(1)}, u32[]{:S(2)}, u32[]{:S(2)}) collective-permute-start(f32[4,3,2048]{2,1,0:T(4,128)S(1)} %slice_add_fusion.1), channel_id=1, source_target_pairs={{0,2},{1,3},{2,0},{3,1},{4,6},{5,7},{6,4},{7,5},{8,10},{9,11},{10,... | collective-permute-start | bytes 294920 | tf_op jit(solution)/shard_map/ppermute | solution.py:539
  129.8 6.0 %collective-permute-start.11 = (f32[2,3,2048]{2,1,0:T(4,128)S(1)}, f32[2,3,2048]{2,1,0:T(4,128)S(1)}, u32[]{:S(2)}, u32[]{:S(2)}) collective-permute-start(f32[2,3,2048]{2,1,0:T(4,128)S(1)} %slice_add_fusion.2), channel_id=1, source_target_pairs={{0,8},{1,9},{2,10},{3,11},{4,12},{5,13},{6,14},{7,15},{8,0},{9,1},... | collective-permute-start | bytes 147464 | tf_op jit(solution)/shard_map/ppermute | solution.py:539
  133.2 4.4 %copy-start.6 = (f32[3,2048]{1,0:T(4,128)S(1)}, f32[3,2048]{1,0:T(4,128)}, u32[]{:S(2)}) copy-start(f32[3,2048]{1,0:T(4,128)} %forces_ref.2) | copy-start | bytes 73732
  133.2 4.4 %copy-start.7 = (s32[3,2048]{1,0:T(4,128)S(1)}, s32[3,2048]{1,0:T(4,128)}, u32[]{:S(2)}) copy-start(s32[3,2048]{1,0:T(4,128)} %start_ref.3) | copy-start | bytes 73732
  133.2 4.4 %copy-start.8 = (f32[3,2048]{1,0:T(4,128)S(1)}, f32[3,2048]{1,0:T(4,128)}, u32[]{:S(2)}) copy-start(f32[3,2048]{1,0:T(4,128)} %fraction_ref.3) | copy-start | bytes 73732
  135.8 11.5 %collective-permute-start.12 = (f32[1,3,2048]{2,1,0:T(4,128)S(1)}, f32[1,3,2048]{2,1,0:T(4,128)S(1)}, u32[]{:S(2)}, u32[]{:S(2)}) collective-permute-start(f32[1,3,2048]{2,1,0:T(4,128)S(1)} %fusion), channel_id=1, source_target_pairs={{0,4},{1,5},{2,6},{3,7},{4,0},{5,1},{6,2},{7,3},{8,12},{9,13},{10,... | collective-permute-start | bytes 73736 | tf_op jit(solution)/shard_map/ppermute | solution.py:539

commit v3 on v2

--- a/solution.py
+++ b/solution.py
@@ -20,8 +20,9 @@
 
 LANES = 128
 SPREAD_LIMIT = 24 * 2**20
-SOLVE_LIMIT = 20 * 2**20
+SOLVE_LIMIT = 15 * 2**20
 GATHER_LIMIT = 20 * 2**20
+WIDE_PART = 3
 KEEP_BYTES = 32 * 2**20
 KZ = 16
 BF16 = jnp.bfloat16
@@ -33,36 +34,37 @@
     return jnp.where(gap < -length / 2, gap + length, gap)
 
 
-def near_kernel(pairs_ref, count_ref, forces_ref, start_ref, fraction_ref, out_ref, columns):
-    tiles = out_ref.shape[1] // LANES
+def tile_rows(own_ref, tile, points):
+    per = points // 8 // LANES
+    at = pl.ds(pl.multiple_of(tile * LANES, LANES), LANES)
+    last_at = pl.ds(pl.multiple_of(points + lax.rem(tile, per) * LANES, LANES), LANES)
+    pieces = own_ref[0, :, last_at]
+    here = lax.broadcasted_iota(jnp.int32, pieces.shape, 0) == lax.div(tile, per)
+    return own_ref[0, :, at], jnp.sum(jnp.where(here, pieces, 0.0), axis=0, keepdims=True)
+
+
+def near_kernel(pairs_ref, count_ref, own_ref, wide_ref, out_ref):
+    points = out_ref.shape[1]
     out_ref[...] = jnp.zeros_like(out_ref)
-
-    @pl.loop(0, tiles)
-    def _(tile):
-        at = pl.ds(pl.multiple_of(tile * LANES, LANES), LANES)
-        nine = jnp.concatenate(
-            [start_ref[:, at].astype(F32), fraction_ref[:, at], forces_ref[:, at]], axis=0
-        )
-        for value in range(9):
-            wide = jnp.broadcast_to(nine[value : value + 1], (LANES, LANES))
-            columns[value, at] = wide.T
 
     @pl.loop(0, count_ref[0])
     def _(slot):
-        target = pl.ds(pl.multiple_of(pairs_ref[2 * slot] * LANES, LANES), LANES)
+        tile = pairs_ref[2 * slot]
+        target = pl.ds(pl.multiple_of(tile * LANES, LANES), LANES)
         base = pl.multiple_of(pairs_ref[2 * slot + 1] * LANES, LANES)
-        start = start_ref[:, target].astype(F32)
-        fraction = fraction_ref[:, target]
+        main, last = tile_rows(own_ref, tile, points)
+        start = [main[3 + axis : 4 + axis] for axis in range(3)]
+        fraction = [main[6:7], main[7:8], last]
         sums = [jnp.zeros((8, LANES), F32) for _ in range(3)]
         for row in range(0, LANES, 8):
-            source = [columns[value, pl.ds(base + row, 8)] for value in range(9)]
+            source = [wide_ref[value, pl.ds(base + row, 8)] for value in range(9)]
             gaps = []
             for axis, length in enumerate((None, NY, NZ)):
-                gap = start[axis : axis + 1] - source[axis]
+                gap = start[axis] - source[3 + axis]
                 if length is not None:
                     gap = wrapped(gap, float(length))
-                gaps.append(gap + (fraction[axis : axis + 1] - source[3 + axis]))
-            pulled = source[6:9]
+                gaps.append(gap + (fraction[axis] - source[6 + axis]))
+            pulled = source[0:3]
             distance = gaps[0] * gaps[0] + gaps[1] * gaps[1] + gaps[2] * gaps[2]
             inverse = lax.rsqrt(distance + EPS_SQ)
             fall = NEAR_SCALE * jnp.exp(distance * (-1.0 / RANGE_SQ)) * (inverse * inverse * inverse)
@@ -74,23 +76,22 @@
         )
 
 
-def near_field(forces, stencil_start, fraction, tile_pairs, pair_count):
+def near_field(own, wide, tile_pairs, pair_count):
     smem = pl.BlockSpec(memory_space=pltpu.SMEM)
     vmem = pl.BlockSpec(memory_space=pltpu.VMEM)
-    points = forces.shape[1]
+    points = wide.shape[1]
     slots = tile_pairs.shape[0]
     return pl.pallas_call(
         near_kernel,
-        in_specs=[smem, smem, vmem, vmem, vmem],
+        in_specs=[smem, smem, vmem, vmem],
         out_specs=vmem,
         out_shape=jax.ShapeDtypeStruct((3, points), F32),
-        scratch_shapes=[pltpu.VMEM((9, points, LANES), F32)],
         compiler_params=pltpu.CompilerParams(vmem_limit_bytes=16 * 2**20),
         cost_estimate=pl.CostEstimate(
             flops=slots * LANES * LANES * 6000, bytes_accessed=points * 48, transcendentals=0
         ),
         name="near",
-    )(tile_pairs.reshape(-1), pair_count, forces, stencil_start, fraction)
+    )(tile_pairs.reshape(-1), pair_count, own, wide)
 
 
 def pack_kernel(first_ref, forces_ref, start_ref, fraction_ref, out_ref):
@@ -117,8 +118,12 @@
     )(first, forces, stencil_start, fraction)
 
 
+def unpacked(width):
+    return width // 9 * 8
+
+
 def unpack(values):
-    points = values.shape[1] // 9 * 8
+    points = unpacked(values.shape[1])
     pieces = [values[row : row + 1, points:] for row in range(8)]
     return values[:, :points], jnp.concatenate(pieces, axis=1)
 
@@ -210,7 +215,19 @@
     return lax.div(block, joined) * (joined * planes)
 
 
-def spread_kernel(rows, points_ref, modes_y_ref, modes_z_ref, out_ref, *kept_refs):
+def spread_kernel(rows, tiles, points_ref, modes_y_ref, modes_z_ref, *refs):
+    if tiles:
+        own_ref, out_ref, *kept_refs, wide_ref = refs
+        last_tile = unpacked(own_ref.shape[2]) // LANES - 1
+        for index in range(tiles):
+            tile = jnp.minimum(pl.program_id(0) * tiles + index, last_tile)
+            eight, ninth = tile_rows(own_ref, tile, unpacked(own_ref.shape[2]))
+            nine = jnp.concatenate([eight, ninth], axis=0)
+            for value in range(9):
+                wide = jnp.broadcast_to(nine[value : value + 1], (LANES, LANES))
+                wide_ref[value, index * LANES : (index + 1) * LANES] = wide.T
+    else:
+        out_ref, *kept_refs = refs
     main, last = unpack(points_ref[0])
     count = main.shape[1]
     modes_y = [modes_y_ref[i] for i in range(7)]
@@ -242,7 +259,7 @@
     ) * 4 <= KEEP_BYTES
 
 
-def spread(points, modes_y, modes_z, rows, keep):
+def spread(points, modes_y, modes_z, rows, keep, own=None):
     blocks, _, width = points.shape
     count = width // 9 * 8
     own_y = modes_y.shape[1]
@@ -253,14 +270,26 @@
     if keep:
         out_specs.append(pl.BlockSpec((1, kept, count), lambda i: (i, 0, 0)))
         out_shape.append(jax.ShapeDtypeStruct((blocks, kept, count), F32))
+    in_specs = [
+        pl.BlockSpec((1, 8, width), lambda i: (i, 0, 0)),
+        pl.BlockSpec(modes_y.shape, lambda i: (0, 0, 0)),
+        pl.BlockSpec(modes_z.shape, lambda i: (0, 0, 0)),
+    ]
+    operands = [points, modes_y, modes_z]
+    tiles = 0
+    if own is not None:
+        tiles = max(1, count // LANES // blocks)
+        last = count // LANES // tiles - 1
+        in_specs.append(pl.BlockSpec((1, 8, width), lambda i: (0, 0, 0)))
+        operands.append(own)
+        out_specs.append(
+            pl.BlockSpec((9, tiles * LANES, LANES), lambda i: (0, jnp.minimum(i, last), 0))
+        )
+        out_shape.append(jax.ShapeDtypeStruct((9, count, LANES), F32))
     return pl.pallas_call(
-        functools.partial(spread_kernel, rows),
+        functools.partial(spread_kernel, rows, tiles),
         grid=(blocks,),
-        in_specs=[
-            pl.BlockSpec((1, 8, width), lambda i: (i, 0, 0)),
-            pl.BlockSpec(modes_y.shape, lambda i: (0, 0, 0)),
-            pl.BlockSpec(modes_z.shape, lambda i: (0, 0, 0)),
-        ],
+        in_specs=in_specs,
         out_specs=out_specs,
         out_shape=out_shape,
         compiler_params=pltpu.CompilerParams(vmem_limit_bytes=SPREAD_LIMIT),
@@ -270,7 +299,7 @@
             transcendentals=0,
         ),
         name="spread",
-    )(points, modes_y, modes_z)
+    )(*operands)
 
 
 def solve_kernel(planes, rows, parts, ids_ref, *refs):
@@ -559,8 +588,11 @@
     keep = keeps(own, modes_y)
     spreads = []
     modes = modes_y
-    for points in parts:
-        result = spread(points, modes, modes_z, rows, keep)
+    for part, points in enumerate(parts):
+        wide_own = own if part == len(parts) - WIDE_PART else None
+        result = spread(points, modes, modes_z, rows, keep, wide_own)
+        if wide_own is not None:
+            *result, wide = result
         piece, modes = lax.optimization_barrier((result[0], modes_y))
         spreads.append([piece, *result[1:]])
     pieces = [result[0] for result in spreads]
@@ -605,8 +637,8 @@
     (far_pair, last, far), after = then((far_pair, last, far))
     last = last + total[1:2] + far_pair[1:]
     far = far + total[:1] + far_pair[:1]
-    forces, count_late, last = lax.optimization_barrier((forces, pair_count, last))
-    near = near_field(forces, stencil_start, fraction, tile_pairs, count_late)
+    count_late, last = lax.optimization_barrier((pair_count, last))
+    near = near_field(own, wide, tile_pairs, count_late)
     return far[0] + from_flipped(last, 4)[0] + near
 
 

time: 148 us -> 148 us (level); the launches traced: 148 us -> 145 us
  Pallas kernels: 122 us -> 114 us
  waiting for transfers between devices: 3.22 us -> 6.86 us
  local copies, waits for them, and re-layouts: 4.39 us -> 6.64 us
    pallas_call x7, Pallas kernels: 64.1 us -> 55.8 us  [the longest x6 54.5 us: spread(): pl.pallas_call(functools.partial(spread_kernel, rows, tiles), grid=(block...]
    ppermute x13, waiting for transfers between devices: 3.22 us -> 6.86 us  [from_flipped(): return lax.ppermute(values, ('group', 'dev'), pairs)]
    unnamed x24 -> x20, local copies, waits for them, and re-layouts: 2.02 us -> 4.26 us
  transfers between devices with their start and end apart: 13 -> 13, of which waited for: 3 -> 4; matrix products, arithmetic and copies ran while one was open for 3% -> 3% of each run, Pallas kernels for 56% -> 51%
where the time goes in v3:
time: 148 us; the launch traced here: 145 us
  Pallas kernels  114 us (77%)
  starting transfers between devices  14.9 us (10%)
  waiting for transfers between devices  6.86 us (5%)
  local copies, waits for them, and re-layouts  6.64 us (4%)
  other arithmetic  1.57 us (1%)
    pallas_call x6, Pallas kernels, spread(): pl.pallas_call(functools.partial(spread_kernel, rows, tiles), grid=(block...  54.5 us
    pallas_call x7, Pallas kernels, gather(): pl.pallas_call(functools.partial(gather_kernel, planes, rows, before, kep...  43.6 us
    ppermute x13, starting transfers between devices, from_flipped(): return lax.ppermute(values, ('group', 'dev'), pairs)  14.9 us
    pallas_call x1, Pallas kernels, solve(): pl.pallas_call(functools.partial(solve_kernel, planes, rows, len(pieces))...  12.9 us
    ppermute x13, waiting for transfers between devices, from_flipped(): return lax.ppermute(values, ('group', 'dev'), pairs)  6.86 us
    unnamed x20, local copies, waits for them, and re-layouts  4.26 us
  transfers between devices with their start and end apart: 13, of which 4 were waited for; matrix products, arithmetic and copies ran while one was open for 3% of the time, Pallas kernels for 51%

profile of v3, /device:TPU:0, one launch (start us, length us, event | category | flops | bytes accessed | tf_op | source)
XLA Modules:
  0.0 144.8 jit_solution(1335997788505789176)
XLA Ops:
  0.0 1.4 pack.1.points_ref.refs_0_.own_ref
  1.4 5.0 %collective-permute-start.2 = (f32[1,8,2304]{2,1,0:T(8,128)}, f32[1,8,2304]{2,1,0:T(8,128)S(1)}, u32[]{:S(2)}, u32[]{:S(2)}) collective-permute-start(f32[1,8,2304]{2,1,0:T(8,128)} %pack.1.points_ref.refs_0_.own_ref), channel_id=1, source_target_pairs={{0,12},{1,13},{2,14},{3,15},{4,8},{5,9},{6,10},{7,11},{8,4},{9,5},... | collective-permute-start | bytes 221192 | tf_op jit(solution)/shard_map/ppermute | solution.py:568
  12.6 1.7 %spread.6 = (f32[1,120,512]{2,1,0:T(8,128)S(1)}, f32[1,48,2048]{2,1,0:T(8,128)S(1)}) custom-call(f32[1,8,2304]{2,1,0:T(8,128)S(1)} %copy-done.4, f32[7,8,128]{2,1,0:T(8,128)S(1)} %broadcast.5.modes_y_ref, f32[7,16,128]{2,1,0:T(8,128)S(1)} %broadcast.7.modes_z_ref), custom_call_target="tpu_custom_call" | custom-call | flops 1879048192 | bytes 319488 | tf_op jit(solution)/shard_map/spread/pallas_call | solution.py:289
  15.1 1.8 %collective-permute-start.3 = (f32[4,8,2304]{2,1,0:T(8,128)S(1)}, f32[4,8,2304]{2,1,0:T(8,128)S(1)}, u32[]{:S(2)}, u32[]{:S(2)}) collective-permute-start(f32[4,8,2304]{2,1,0:T(8,128)S(1)} %pad_maximum_fusion), channel_id=1, source_target_pairs={{0,2},{1,3},{2,0},{3,1},{4,6},{5,7},{6,4},{7,5},{8,10},{9,11},{10,... | collective-permute-start | bytes 884744 | tf_op jit(solution)/shard_map/ppermute | solution.py:568
  16.9 5.1 %spread.7 = (f32[3,120,512]{2,1,0:T(8,128)S(1)}, f32[3,48,2048]{2,1,0:T(8,128)S(1)}) custom-call(f32[3,8,2304]{2,1,0:T(8,128)S(1)} %get-tuple-element.93.points_ref, f32[7,8,128]{2,1,0:T(8,128)S(1)} %broadcast.5.modes_y_ref, f32[7,16,128]{2,1,0:T(8,128)S(1)} %broadcast.7.modes_z_ref), custom_call_target="tpu_custom_call" | custom-call | flops 5637144576 | bytes 958464 | tf_op jit(solution)/shard_map/spread/pallas_call | solution.py:289
  23.4 1.6 %collective-permute-start.4 = (f32[8,8,2304]{2,1,0:T(8,128)S(1)}, f32[8,8,2304]{2,1,0:T(8,128)S(1)}, u32[]{:S(2)}, u32[]{:S(2)}) collective-permute-start(f32[8,8,2304]{2,1,0:T(8,128)S(1)} %constant_dynamic-update-slice_fusion), channel_id=1, source_target_pairs={{0,16},{1,17},{2,18},{3,19},{4,20},{5,21},{6,22},{7,23},{8,24},{9,... | collective-permute-start | bytes 1769480 | tf_op jit(solution)/shard_map/ppermute | solution.py:568
  25.0 6.8 %spread.8 = (f32[4,120,512]{2,1,0:T(8,128)S(1)}, f32[4,48,2048]{2,1,0:T(8,128)S(1)}) custom-call(f32[4,8,2304]{2,1,0:T(8,128)S(1)} %collective-permute-done.3.points_ref, f32[7,8,128]{2,1,0:T(8,128)S(1)} %broadcast.5.modes_y_ref, f32[7,16,128]{2,1,0:T(8,128)S(1)} %broadcast.7.modes_z_ref), custom_call_target="tpu_custom_call" | custom-call | flops 7516192768 | bytes 1277952 | tf_op jit(solution)/shard_map/spread/pallas_call | solution.py:289
  31.9 13.8 %spread.9 = (f32[8,120,512]{2,1,0:T(8,128)S(1)}, f32[8,48,2048]{2,1,0:T(8,128)S(1)}, f32[9,2048,128]{2,1,0:T(8,128)S(1)}) custom-call(f32[8,8,2304]{2,1,0:T(8,128)S(1)} %collective-permute-done.6.points_ref, f32[7,8,128]{2,1,0:T(8,128)S(1)} %broadcast.5.modes_y_ref, f32[7,16,128]{2,1,0:T(8,128)S(1)} %broadcast.7.modes_z_ref, f32[1,8,2304]{2,1,0:T(8,128)S(1)} %copy-done.5), custom_call_target="tpu_custom_call" | custom-call | flops 15032385536 | bytes 2555904 | tf_op jit(solution)/shard_map/spread/pallas_call | solution.py:289
  45.9 13.6 %spread.10 = (f32[8,120,512]{2,1,0:T(8,128)S(1)}, f32[8,48,2048]{2,1,0:T(8,128)S(1)}) custom-call(f32[8,8,2304]{2,1,0:T(8,128)S(1)} %collective-permute-done.4.points_ref, f32[7,8,128]{2,1,0:T(8,128)S(1)} %broadcast.5.modes_y_ref, f32[7,16,128]{2,1,0:T(8,128)S(1)} %broadcast.7.modes_z_ref), custom_call_target="tpu_custom_call" | custom-call | flops 15032385536 | bytes 2555904 | tf_op jit(solution)/shard_map/spread/pallas_call | solution.py:289
  59.6 13.5 %spread.11 = (f32[8,120,512]{2,1,0:T(8,128)S(1)}, f32[8,48,2048]{2,1,0:T(8,128)S(1)}) custom-call(f32[8,8,2304]{2,1,0:T(8,128)S(1)} %collective-permute-done.5.points_ref, f32[7,8,128]{2,1,0:T(8,128)S(1)} %broadcast.5.modes_y_ref, f32[7,16,128]{2,1,0:T(8,128)S(1)} %broadcast.7.modes_z_ref), custom_call_target="tpu_custom_call" | custom-call | flops 15032385536 | bytes 2555904 | tf_op jit(solution)/shard_map/spread/pallas_call | solution.py:289
  73.1 1.6 %copy-done.6 = f32[8,48,2048]{2,1,0:T(8,128)} copy-done((f32[8,48,2048]{2,1,0:T(8,128)}, f32[8,48,2048]{2,1,0:T(8,128)S(1)}, u32[]{:S(2)}) %copy-start.6) | copy-done | bytes 3145752
  74.8 12.9 %solve.1.refs_1_ = f32[3,1032,512]{2,1,0:T(8,128)S(1)} custom-call(s32[32]{0:T(128)S(1)} %broadcast_xor_fusion.ids_ref, f32[1,120,512]{2,1,0:T(8,128)S(1)} %get-tuple-element.60.refs_0_, f32[3,120,512]{2,1,0:T(8,128)S(1)} %get-tuple-element.61.refs_1_, f32[4,120,512]{2,1,0:T(8,128)S(1)} %get-tuple-element.62.refs_2_, ...), custom_call_target="tpu_custom_call" | custom-call | flops 3623878656 | bytes 12582912 | tf_op jit(solution)/shard_map/solve/pallas_call | solution.py:408
  87.7 10.5 %interpolate.7 = f32[8,3,2048]{2,1,0:T(4,128)S(1)} custom-call(s32[32]{0:T(128)S(1)} %broadcast_xor_fusion.ids_ref, f32[8,8,2304]{2,1,0:T(8,128)S(1)} %collective-permute-done.5.points_ref, f32[8,48,2048]{2,1,0:T(8,128)S(1)} %copy-done.7, f32[3,1032,512]{2,1,0:T(8,128)S(1)} %solve.1.refs_1_), custom_call_target="tpu_custom_call" | custom-call | flops 15032385536 | bytes 786432 | tf_op jit(solution)/shard_map/interpolate/pallas_call | solution.py:478
  98.7 10.5 %interpolate.8 = f32[8,3,2048]{2,1,0:T(4,128)S(1)} custom-call(s32[32]{0:T(128)S(1)} %broadcast_xor_fusion.ids_ref, f32[8,8,2304]{2,1,0:T(8,128)S(1)} %collective-permute-done.4.points_ref, f32[8,48,2048]{2,1,0:T(8,128)S(1)} %get-tuple-element.68.refs_0_, f32[3,1032,512]{2,1,0:T(8,128)S(1)} %solve.1.refs_1_), custom_call_target="tpu_custom_call" | custom-call | flops 15032385536 | bytes 786432 | tf_op jit(solution)/shard_map/interpolate/pallas_call | solution.py:478
  109.8 10.5 %interpolate.9 = f32[8,3,2048]{2,1,0:T(4,128)S(1)} custom-call(s32[32]{0:T(128)S(1)} %broadcast_xor_fusion.ids_ref, f32[8,8,2304]{2,1,0:T(8,128)S(1)} %collective-permute-done.6.points_ref, f32[8,48,2048]{2,1,0:T(8,128)S(1)} %get-tuple-element.72.refs_0_, f32[3,1032,512]{2,1,0:T(8,128)S(1)} %solve.1.refs_1_), custom_call_target="tpu_custom_call" | custom-call | flops 15032385536 | bytes 786432 | tf_op jit(solution)/shard_map/interpolate/pallas_call | solution.py:478
  120.4 5.5 %interpolate.10 = f32[4,3,2048]{2,1,0:T(4,128)S(1)} custom-call(s32[32]{0:T(128)S(1)} %broadcast_xor_fusion.ids_ref, f32[4,8,2304]{2,1,0:T(8,128)S(1)} %collective-permute-done.3.points_ref, f32[4,48,2048]{2,1,0:T(8,128)S(1)} %get-tuple-element.75.refs_0_, f32[3,1032,512]{2,1,0:T(8,128)S(1)} %solve.1.refs_1_), custom_call_target="tpu_custom_call" | custom-call | flops 7516192768 | bytes 393216 | tf_op jit(solution)/shard_map/interpolate/pallas_call | solution.py:478
  126.1 1.6 %collective-permute-start.10 = (f32[4,3,2048]{2,1,0:T(4,128)S(1)}, f32[4,3,2048]{2,1,0:T(4,128)S(1)}, u32[]{:S(2)}, u32[]{:S(2)}) collective-permute-start(f32[4,3,2048]{2,1,0:T(4,128)S(1)} %slice_add_fusion.1), channel_id=1, source_target_pairs={{0,2},{1,3},{2,0},{3,1},{4,6},{5,7},{6,4},{7,5},{8,10},{9,11},{10,... | collective-permute-start | bytes 294920 | tf_op jit(solution)/shard_map/ppermute | solution.py:568
  127.7 3.0 %interpolate.11 = f32[2,3,2048]{2,1,0:T(4,128)S(1)} custom-call(s32[32]{0:T(128)S(1)} %broadcast_xor_fusion.ids_ref, f32[3,8,2304]{2,1,0:T(8,128)S(1)} %get-tuple-element.93.points_ref, f32[3,48,2048]{2,1,0:T(8,128)S(1)} %get-tuple-element.81.refs_0_, f32[3,1032,512]{2,1,0:T(8,128)S(1)} %solve.1.refs_1_), custom_call_target="tpu_custom_call" | custom-call | flops 3758096384 | bytes 196608 | tf_op jit(solution)/shard_map/interpolate/pallas_call | solution.py:478
  130.7 1.4 collective-permute-done.10
  132.1 1.8 %interpolate.12 = f32[1,3,2048]{2,1,0:T(4,128)S(1)} custom-call(s32[32]{0:T(128)S(1)} %broadcast_xor_fusion.ids_ref, f32[3,8,2304]{2,1,0:T(8,128)S(1)} %get-tuple-element.93.points_ref, f32[3,48,2048]{2,1,0:T(8,128)S(1)} %get-tuple-element.81.refs_0_, f32[3,1032,512]{2,1,0:T(8,128)S(1)} %solve.1.refs_1_), custom_call_target="tpu_custom_call" | custom-call | flops 1879048192 | bytes 98304 | tf_op jit(solution)/shard_map/interpolate/pallas_call | solution.py:478
  133.9 2.5 %collective-permute-start.11 = (f32[2,3,2048]{2,1,0:T(4,128)S(1)}, f32[2,3,2048]{2,1,0:T(4,128)S(1)}, u32[]{:S(2)}, u32[]{:S(2)}) collective-permute-start(f32[2,3,2048]{2,1,0:T(4,128)S(1)} %slice_add_fusion.2), channel_id=1, source_target_pairs={{0,8},{1,9},{2,10},{3,11},{4,12},{5,13},{6,14},{7,15},{8,0},{9,1},... | collective-permute-start | bytes 147464 | tf_op jit(solution)/shard_map/ppermute | solution.py:568
  136.4 1.8 %interpolate.13 = f32[1,3,2048]{2,1,0:T(4,128)S(1)} custom-call(s32[32]{0:T(128)S(1)} %broadcast_xor_fusion.ids_ref, f32[1,8,2304]{2,1,0:T(8,128)S(1)} %copy-done.5, f32[1,48,2048]{2,1,0:T(8,128)S(1)} %get-tuple-element.86.refs_0_, f32[3,1032,512]{2,1,0:T(8,128)S(1)} %solve.1.refs_1_), custom_call_target="tpu_custom_call" | custom-call | flops 1879048192 | bytes 98304 | tf_op jit(solution)/shard_map/interpolate/pallas_call | solution.py:478
  138.1 2.0 %collective-permute-done.11 = f32[2,3,2048]{2,1,0:T(4,128)S(1)} collective-permute-done((f32[2,3,2048]{2,1,0:T(4,128)S(1)}, f32[2,3,2048]{2,1,0:T(4,128)S(1)}, u32[]{:S(2)}, u32[]{:S(2)}) %collective-permute-start.11) | collective-permute-done | bytes 49184 | tf_op jit(solution)/shard_map/ppermute | solution.py:568
  142.1 2.1 %collective-permute-done.12 = f32[1,3,2048]{2,1,0:T(4,128)S(1)} collective-permute-done((f32[1,3,2048]{2,1,0:T(4,128)S(1)}, f32[1,3,2048]{2,1,0:T(4,128)S(1)}, u32[]{:S(2)}, u32[]{:S(2)}) %collective-permute-start.12) | collective-permute-done | bytes 24608 | tf_op jit(solution)/shard_map/ppermute | solution.py:568
  (55 shorter events, 11.7 us)
Async XLA Ops:
  1.4 13.6 %collective-permute-start.2 = (f32[1,8,2304]{2,1,0:T(8,128)}, f32[1,8,2304]{2,1,0:T(8,128)S(1)}, u32[]{:S(2)}, u32[]{:S(2)}) collective-permute-start(f32[1,8,2304]{2,1,0:T(8,128)} %pack.1.points_ref.refs_0_.own_ref), channel_id=1, source_target_pairs={{0,12},{1,13},{2,14},{3,15},{4,8},{5,9},{6,10},{7,11},{8,4},{9,5},... | collective-permute-start | bytes 221192 | tf_op jit(solution)/shard_map/ppermute | solution.py:568
  6.5 8.5 %collective-permute-start.1 = (f32[1,8,2304]{2,1,0:T(8,128)}, f32[1,8,2304]{2,1,0:T(8,128)S(1)}, u32[]{:S(2)}, u32[]{:S(2)}) collective-permute-start(f32[1,8,2304]{2,1,0:T(8,128)} %pack.1.points_ref.refs_0_.own_ref), channel_id=1, source_target_pairs={{0,8},{1,9},{2,10},{3,11},{4,12},{5,13},{6,14},{7,15},{8,0},{9,1},... | collective-permute-start | bytes 221192 | tf_op jit(solution)/shard_map/ppermute | solution.py:568
  6.5 8.5 %collective-permute-start = (f32[1,8,2304]{2,1,0:T(8,128)}, f32[1,8,2304]{2,1,0:T(8,128)S(1)}, u32[]{:S(2)}, u32[]{:S(2)}) collective-permute-start(f32[1,8,2304]{2,1,0:T(8,128)} %pack.1.points_ref.refs_0_.own_ref), channel_id=1, source_target_pairs={{0,4},{1,5},{2,6},{3,7},{4,0},{5,1},{6,2},{7,3},{8,12},{9,13},{10,... | collective-permute-start | bytes 221192 | tf_op jit(solution)/shard_map/ppermute | solution.py:568
  11.7 0.9 copy-start.4
  15.1 8.3 %collective-permute-start.3 = (f32[4,8,2304]{2,1,0:T(8,128)S(1)}, f32[4,8,2304]{2,1,0:T(8,128)S(1)}, u32[]{:S(2)}, u32[]{:S(2)}) collective-permute-start(f32[4,8,2304]{2,1,0:T(8,128)S(1)} %pad_maximum_fusion), channel_id=1, source_target_pairs={{0,2},{1,3},{2,0},{3,1},{4,6},{5,7},{6,4},{7,5},{8,10},{9,11},{10,... | collective-permute-start | bytes 884744 | tf_op jit(solution)/shard_map/ppermute | solution.py:568
  23.3 8.5 %copy-start.5 = (f32[1,8,2304]{2,1,0:T(8,128)S(1)}, f32[1,8,2304]{2,1,0:T(8,128)}, u32[]{:S(2)}) copy-start(f32[1,8,2304]{2,1,0:T(8,128)} %pack.1.points_ref.refs_0_.own_ref) | copy-start | bytes 221188
  23.3 8.5 %collective-permute-start.6 = (f32[8,8,2304]{2,1,0:T(8,128)S(1)}, f32[8,8,2304]{2,1,0:T(8,128)S(1)}, u32[]{:S(2)}, u32[]{:S(2)}) collective-permute-start(f32[8,8,2304]{2,1,0:T(8,128)S(1)} %constant_dynamic-update-slice_fusion), channel_id=1, source_target_pairs={{0,1},{1,0},{2,3},{3,2},{4,5},{5,4},{6,7},{7,6},{8,9},{9,8},{10,11... | collective-permute-start | bytes 1769480 | tf_op jit(solution)/shard_map/ppermute | solution.py:568
  23.4 22.2 %collective-permute-start.4 = (f32[8,8,2304]{2,1,0:T(8,128)S(1)}, f32[8,8,2304]{2,1,0:T(8,128)S(1)}, u32[]{:S(2)}, u32[]{:S(2)}) collective-permute-start(f32[8,8,2304]{2,1,0:T(8,128)S(1)} %constant_dynamic-update-slice_fusion), channel_id=1, source_target_pairs={{0,16},{1,17},{2,18},{3,19},{4,20},{5,21},{6,22},{7,23},{8,24},{9,... | collective-permute-start | bytes 1769480 | tf_op jit(solution)/shard_map/ppermute | solution.py:568
  45.7 13.9 %collective-permute-start.5 = (f32[8,8,2304]{2,1,0:T(8,128)S(1)}, f32[8,8,2304]{2,1,0:T(8,128)S(1)}, u32[]{:S(2)}, u32[]{:S(2)}) collective-permute-start(f32[8,8,2304]{2,1,0:T(8,128)S(1)} %collective-permute-done.4.points_ref), channel_id=1, source_target_pairs={{0,1},{1,0},{2,3},{3,2},{4,5},{5,4},{6,7},{7,6},{8,9},{9,8},{10,11... | collective-permute-start | bytes 1769480 | tf_op jit(solution)/shard_map/ppermute | solution.py:568
  59.5 15.2 %copy-start = (bf16[512,1536]{1,0:T(8,128)(2,1)S(1)}, bf16[512,1536]{1,0:T(8,128)(2,1)}, u32[]{:S(2)}) copy-start(bf16[512,1536]{1,0:T(8,128)(2,1)} %constant.76.clone.refs_9_) | copy-start | bytes 4718596
  59.5 15.2 %copy-start.1 = (bf16[512,1536]{1,0:T(8,128)(2,1)S(1)}, bf16[512,1536]{1,0:T(8,128)(2,1)}, u32[]{:S(2)}) copy-start(bf16[512,1536]{1,0:T(8,128)(2,1)} %constant.74.clone.refs_7_) | copy-start | bytes 4718596
  59.6 15.2 %copy-start.2 = (bf16[2,256,768]{2,1,0:T(8,128)(2,1)S(1)}, bf16[2,256,768]{2,1,0:T(8,128)(2,1)}, u32[]{:S(2)}) copy-start(bf16[2,256,768]{2,1,0:T(8,128)(2,1)} %constant.75.clone.refs_8_) | copy-start | bytes 2359300
  59.6 15.2 %copy-start.3 = (bf16[2,256,768]{2,1,0:T(8,128)(2,1)S(1)}, bf16[2,256,768]{2,1,0:T(8,128)(2,1)}, u32[]{:S(2)}) copy-start(bf16[2,256,768]{2,1,0:T(8,128)(2,1)} %constant.73.clone.refs_6_) | copy-start | bytes 2359300
  73.1 1.6 %copy-start.6 = (f32[8,48,2048]{2,1,0:T(8,128)}, f32[8,48,2048]{2,1,0:T(8,128)S(1)}, u32[]{:S(2)}) copy-start(f32[8,48,2048]{2,1,0:T(8,128)S(1)} %get-tuple-element.59.refs_0_) | copy-start | bytes 9437188
  74.8 13.0 %copy-start.7 = (f32[8,48,2048]{2,1,0:T(8,128)S(1)}, f32[8,48,2048]{2,1,0:T(8,128)}, u32[]{:S(2)}) copy-start(f32[8,48,2048]{2,1,0:T(8,128)} %copy-done.6) | copy-start | bytes 9437188
  98.3 10.9 %collective-permute-start.7 = (f32[8,3,2048]{2,1,0:T(4,128)S(1)}, f32[8,3,2048]{2,1,0:T(4,128)S(1)}, u32[]{:S(2)}, u32[]{:S(2)}) collective-permute-start(f32[8,3,2048]{2,1,0:T(4,128)S(1)} %interpolate.7), channel_id=1, source_target_pairs={{0,1},{1,0},{2,3},{3,2},{4,5},{5,4},{6,7},{7,6},{8,9},{9,8},{10,11... | collective-permute-start | bytes 589832 | tf_op jit(solution)/shard_map/ppermute | solution.py:568
  109.2 11.1 %collective-permute-start.8 = (f32[8,3,2048]{2,1,0:T(4,128)S(1)}, f32[8,3,2048]{2,1,0:T(4,128)S(1)}, u32[]{:S(2)}, u32[]{:S(2)}) collective-permute-start(f32[8,3,2048]{2,1,0:T(4,128)S(1)} %add.61), channel_id=1, source_target_pairs={{0,16},{1,17},{2,18},{3,19},{4,20},{5,21},{6,22},{7,23},{8,24},{9,... | collective-permute-start | bytes 589832 | tf_op jit(solution)/shard_map/ppermute | solution.py:568
  120.4 5.6 %collective-permute-start.9 = (f32[8,3,2048]{2,1,0:T(4,128)S(1)}, f32[8,3,2048]{2,1,0:T(4,128)S(1)}, u32[]{:S(2)}, u32[]{:S(2)}) collective-permute-start(f32[8,3,2048]{2,1,0:T(4,128)S(1)} %interpolate.9), channel_id=1, source_target_pairs={{0,1},{1,0},{2,3},{3,2},{4,5},{5,4},{6,7},{7,6},{8,9},{9,8},{10,11... | collective-permute-start | bytes 589832 | tf_op jit(solution)/shard_map/ppermute | solution.py:568
  126.1 5.9 %collective-permute-start.10 = (f32[4,3,2048]{2,1,0:T(4,128)S(1)}, f32[4,3,2048]{2,1,0:T(4,128)S(1)}, u32[]{:S(2)}, u32[]{:S(2)}) collective-permute-start(f32[4,3,2048]{2,1,0:T(4,128)S(1)} %slice_add_fusion.1), channel_id=1, source_target_pairs={{0,2},{1,3},{2,0},{3,1},{4,6},{5,7},{6,4},{7,5},{8,10},{9,11},{10,... | collective-permute-start | bytes 294920 | tf_op jit(solution)/shard_map/ppermute | solution.py:568
  133.9 6.3 %collective-permute-start.11 = (f32[2,3,2048]{2,1,0:T(4,128)S(1)}, f32[2,3,2048]{2,1,0:T(4,128)S(1)}, u32[]{:S(2)}, u32[]{:S(2)}) collective-permute-start(f32[2,3,2048]{2,1,0:T(4,128)S(1)} %slice_add_fusion.2), channel_id=1, source_target_pairs={{0,8},{1,9},{2,10},{3,11},{4,12},{5,13},{6,14},{7,15},{8,0},{9,1},... | collective-permute-start | bytes 147464 | tf_op jit(solution)/shard_map/ppermute | solution.py:568
  140.2 4.0 %collective-permute-start.12 = (f32[1,3,2048]{2,1,0:T(4,128)S(1)}, f32[1,3,2048]{2,1,0:T(4,128)S(1)}, u32[]{:S(2)}, u32[]{:S(2)}) collective-permute-start(f32[1,3,2048]{2,1,0:T(4,128)S(1)} %fusion), channel_id=1, source_target_pairs={{0,4},{1,5},{2,6},{3,7},{4,0},{5,1},{6,2},{7,3},{8,12},{9,13},{10,... | collective-permute-start | bytes 73736 | tf_op jit(solution)/shard_map/ppermute | solution.py:568

commit v4 on v3

--- a/solution.py
+++ b/solution.py
@@ -19,9 +19,9 @@
 NEAR_SCALE = 0.25
 
 LANES = 128
-SPREAD_LIMIT = 24 * 2**20
-SOLVE_LIMIT = 15 * 2**20
-GATHER_LIMIT = 20 * 2**20
+SPREAD_LIMIT = 16 * 2**20
+SOLVE_LIMIT = 8 * 2**20
+GATHER_LIMIT = 12 * 2**20
 WIDE_PART = 3
 KEEP_BYTES = 32 * 2**20
 KZ = 16
@@ -305,7 +305,7 @@
 def solve_kernel(planes, rows, parts, ids_ref, *refs):
     piece_refs = refs[:parts]
     forward_half_ref, forward_ref, back_half_ref, back_ref = refs[parts : parts + 4]
-    waves_ref, out_ref, modes, stacked = refs[parts + 4 :]
+    waves_ref, out_ref, stacked = refs[parts + 4 :]
     extra = 8
     out_ref[...] = jnp.zeros_like(out_ref)
     before = 0
@@ -336,10 +336,15 @@
     def _(c):
         cuts = [out_ref[c, i * quarter : (i + 1) * quarter] for i in range(4)]
         first, second = cuts[0] + cuts[2], cuts[1] + cuts[3]
-        modes[c, 0:quarter] = transform(forward_half_ref[0], first + second)
-        modes[c, quarter : 2 * quarter] = transform(forward_half_ref[1], first - second)
         odd = jnp.concatenate([cuts[0] - cuts[2], cuts[1] - cuts[3]], axis=0)
-        modes[c, 2 * quarter :] = transform(forward_ref[...], odd)
+        odd = transform(forward_ref[...], odd)
+        results = [
+            transform(forward_half_ref[0], first + second),
+            transform(forward_half_ref[1], first - second),
+        ]
+        out_ref[c, 0:quarter] = results[0]
+        out_ref[c, quarter : 2 * quarter] = results[1]
+        out_ref[c, 2 * quarter : NX] = odd
 
     wave_y = waves_ref[0:1]
     wave_z = waves_ref[1:2]
@@ -370,7 +375,7 @@
                 return tuple(1 - t if i == axis else t for i, t in enumerate(state))
 
             states = [(a, b, d) for a in range(2) for b in range(2) for d in range(2)]
-            values = {(c,) + state: modes[place(c, state)] for c in range(3) for state in states}
+            values = {(c,) + state: out_ref[place(c, state)] for c in range(3) for state in states}
             divergence = {}
             for state in states:
                 total = None
@@ -385,18 +390,14 @@
                     term = waves[axis] * divergence[flip(state, axis)]
                     value = values[(axis,) + state]
                     value = value - term if state[axis] else value + term
-                    modes[place(axis, state)] = value * factor
+                    out_ref[place(axis, state)] = value * factor
 
     @pl.loop(0, 3)
     def _(c):
-        even = transform(back_half_ref[0], modes[c, 0:quarter])
-        out_ref[c, 0:quarter] = even
-        even = transform(back_half_ref[1], modes[c, quarter : 2 * quarter])
-        first = out_ref[c, 0:quarter]
-        out_ref[c, 0:quarter] = first + even
-        out_ref[c, quarter : 2 * quarter] = first - even
-        odd = transform(back_ref[...], modes[c, 2 * quarter :])
-        even = out_ref[c, 0 : 2 * quarter]
+        first = transform(back_half_ref[0], out_ref[c, 0:quarter])
+        second = transform(back_half_ref[1], out_ref[c, quarter : 2 * quarter])
+        odd = transform(back_ref[...], out_ref[c, 2 * quarter : NX])
+        even = jnp.concatenate([first + second, first - second], axis=0)
         out_ref[c, 0 : 2 * quarter] = even + odd
         out_ref[c, 2 * quarter : NX] = even - odd
         out_ref[c, NX : NX + extra] = out_ref[c, 0:extra]
@@ -411,7 +412,6 @@
         out_specs=full,
         out_shape=jax.ShapeDtypeStruct((3, NX + 8, cols), F32),
         scratch_shapes=[
-            pltpu.VMEM((3, NX, cols), F32),
             pltpu.VMEM((3 * NX // 2, cols), BF16),
         ],
         compiler_params=pltpu.CompilerParams(vmem_limit_bytes=SOLVE_LIMIT),
@@ -489,7 +489,7 @@
         scratch_shapes=[pltpu.VMEM((2 * LANES, cols), BF16)],
         compiler_params=pltpu.CompilerParams(vmem_limit_bytes=GATHER_LIMIT),
         cost_estimate=pl.CostEstimate(
-            flops=blocks * count * cols * LANES * 14,
+            flops=blocks * count * cols * LANES * 5,
             bytes_accessed=blocks * 12 * count * 4,
             transcendentals=0,
         ),

time: 148 us -> 147 us (level); the launches traced: 145 us -> 148 us
  Pallas kernels: 114 us -> 121 us
  waiting for transfers between devices: 6.86 us -> 4.66 us
  local copies, waits for them, and re-layouts: 6.64 us -> 5.01 us
    pallas_call x1, Pallas kernels: 1.27 us -> 7.49 us  [near_field(): pl.pallas_call(near_kernel, in_specs=[smem, smem, vmem, vmem], out_specs=...]
    ppermute x13, waiting for transfers between devices: 6.86 us -> 4.66 us  [from_flipped(): return lax.ppermute(values, ('group', 'dev'), pairs)]
    unnamed x20 -> x16, local copies, waits for them, and re-layouts: 4.26 us -> 2.64 us
  transfers between devices with their start and end apart: 13 -> 13, of which waited for: 4 -> 3; matrix products, arithmetic and copies ran while one was open for 3% -> 3% of each run, Pallas kernels for 51% -> 54%
where the time goes in v4:
time: 147 us; the launch traced here: 148 us
  Pallas kernels  121 us (82%)
  starting transfers between devices  15 us (10%)
  local copies, waits for them, and re-layouts  5.01 us (3%)
  waiting for transfers between devices  4.66 us (3%)
  other arithmetic  1.58 us (1%)
    pallas_call x6, Pallas kernels, spread(): pl.pallas_call(functools.partial(spread_kernel, rows, tiles), grid=(block...  54.7 us
    pallas_call x7, Pallas kernels, gather(): pl.pallas_call(functools.partial(gather_kernel, planes, rows, before, kep...  43.8 us
    ppermute x13, starting transfers between devices, from_flipped(): return lax.ppermute(values, ('group', 'dev'), pairs)  15 us
    pallas_call x1, Pallas kernels, solve(): pl.pallas_call(functools.partial(solve_kernel, planes, rows, len(pieces))...  13.1 us
    pallas_call x1, Pallas kernels, near_field(): pl.pallas_call(near_kernel, in_specs=[smem, smem, vmem, vmem], out_specs=...  7.49 us
    ppermute x13, waiting for transfers between devices, from_flipped(): return lax.ppermute(values, ('group', 'dev'), pairs)  4.66 us
  transfers between devices with their start and end apart: 13, of which 3 were waited for; matrix products, arithmetic and copies ran while one was open for 3% of the time, Pallas kernels for 54%

profile of v4, /device:TPU:0, one launch (start us, length us, event | category | flops | bytes accessed | tf_op | source)
XLA Modules:
  0.0 147.7 jit_solution(16048771936760454446)
XLA Ops:
  0.0 1.4 pack.1.points_ref.refs_0_.own_ref
  1.4 5.0 %collective-permute-start.2 = (f32[1,8,2304]{2,1,0:T(8,128)}, f32[1,8,2304]{2,1,0:T(8,128)S(1)}, u32[]{:S(2)}, u32[]{:S(2)}) collective-permute-start(f32[1,8,2304]{2,1,0:T(8,128)} %pack.1.points_ref.refs_0_.own_ref), channel_id=1, source_target_pairs={{0,12},{1,13},{2,14},{3,15},{4,8},{5,9},{6,10},{7,11},{8,4},{9,5},... | collective-permute-start | bytes 221192 | tf_op jit(solution)/shard_map/ppermute | solution.py:568
  12.6 1.7 %spread.6 = (f32[1,120,512]{2,1,0:T(8,128)S(1)}, f32[1,48,2048]{2,1,0:T(8,128)S(1)}) custom-call(f32[1,8,2304]{2,1,0:T(8,128)S(1)} %copy-done.2, f32[7,8,128]{2,1,0:T(8,128)S(1)} %broadcast.5.modes_y_ref, f32[7,16,128]{2,1,0:T(8,128)S(1)} %broadcast.7.modes_z_ref), custom_call_target="tpu_custom_call" | custom-call | flops 1879048192 | bytes 319488 | tf_op jit(solution)/shard_map/spread/pallas_call | solution.py:289
  15.0 1.8 %collective-permute-start.3 = (f32[4,8,2304]{2,1,0:T(8,128)S(1)}, f32[4,8,2304]{2,1,0:T(8,128)S(1)}, u32[]{:S(2)}, u32[]{:S(2)}) collective-permute-start(f32[4,8,2304]{2,1,0:T(8,128)S(1)} %pad_maximum_fusion), channel_id=1, source_target_pairs={{0,2},{1,3},{2,0},{3,1},{4,6},{5,7},{6,4},{7,5},{8,10},{9,11},{10,... | collective-permute-start | bytes 884744 | tf_op jit(solution)/shard_map/ppermute | solution.py:568
  16.9 5.1 %spread.7 = (f32[3,120,512]{2,1,0:T(8,128)S(1)}, f32[3,48,2048]{2,1,0:T(8,128)S(1)}) custom-call(f32[3,8,2304]{2,1,0:T(8,128)S(1)} %get-tuple-element.93.points_ref, f32[7,8,128]{2,1,0:T(8,128)S(1)} %broadcast.5.modes_y_ref, f32[7,16,128]{2,1,0:T(8,128)S(1)} %broadcast.7.modes_z_ref), custom_call_target="tpu_custom_call" | custom-call | flops 5637144576 | bytes 958464 | tf_op jit(solution)/shard_map/spread/pallas_call | solution.py:289
  22.0 1.3 collective-permute-done.3.points_ref
  23.4 1.6 %collective-permute-start.4 = (f32[8,8,2304]{2,1,0:T(8,128)S(1)}, f32[8,8,2304]{2,1,0:T(8,128)S(1)}, u32[]{:S(2)}, u32[]{:S(2)}) collective-permute-start(f32[8,8,2304]{2,1,0:T(8,128)S(1)} %constant_dynamic-update-slice_fusion), channel_id=1, source_target_pairs={{0,16},{1,17},{2,18},{3,19},{4,20},{5,21},{6,22},{7,23},{8,24},{9,... | collective-permute-start | bytes 1769480 | tf_op jit(solution)/shard_map/ppermute | solution.py:568
  25.0 6.8 %spread.8 = (f32[4,120,512]{2,1,0:T(8,128)S(1)}, f32[4,48,2048]{2,1,0:T(8,128)S(1)}) custom-call(f32[4,8,2304]{2,1,0:T(8,128)S(1)} %collective-permute-done.3.points_ref, f32[7,8,128]{2,1,0:T(8,128)S(1)} %broadcast.5.modes_y_ref, f32[7,16,128]{2,1,0:T(8,128)S(1)} %broadcast.7.modes_z_ref), custom_call_target="tpu_custom_call" | custom-call | flops 7516192768 | bytes 1277952 | tf_op jit(solution)/shard_map/spread/pallas_call | solution.py:289
  31.8 13.8 %spread.9 = (f32[8,120,512]{2,1,0:T(8,128)S(1)}, f32[8,48,2048]{2,1,0:T(8,128)S(1)}, f32[9,2048,128]{2,1,0:T(8,128)S(1)}) custom-call(f32[8,8,2304]{2,1,0:T(8,128)S(1)} %collective-permute-done.6.points_ref, f32[7,8,128]{2,1,0:T(8,128)S(1)} %broadcast.5.modes_y_ref, f32[7,16,128]{2,1,0:T(8,128)S(1)} %broadcast.7.modes_z_ref, f32[1,8,2304]{2,1,0:T(8,128)S(1)} %copy-done.3), custom_call_target="tpu_custom_call" | custom-call | flops 15032385536 | bytes 2555904 | tf_op jit(solution)/shard_map/spread/pallas_call | solution.py:289
  45.9 13.6 %spread.10 = (f32[8,120,512]{2,1,0:T(8,128)S(1)}, f32[8,48,2048]{2,1,0:T(8,128)S(1)}) custom-call(f32[8,8,2304]{2,1,0:T(8,128)S(1)} %collective-permute-done.4.points_ref, f32[7,8,128]{2,1,0:T(8,128)S(1)} %broadcast.5.modes_y_ref, f32[7,16,128]{2,1,0:T(8,128)S(1)} %broadcast.7.modes_z_ref), custom_call_target="tpu_custom_call" | custom-call | flops 15032385536 | bytes 2555904 | tf_op jit(solution)/shard_map/spread/pallas_call | solution.py:289
  59.6 13.6 %spread.11 = (f32[8,120,512]{2,1,0:T(8,128)S(1)}, f32[8,48,2048]{2,1,0:T(8,128)S(1)}) custom-call(f32[8,8,2304]{2,1,0:T(8,128)S(1)} %collective-permute-done.5.points_ref, f32[7,8,128]{2,1,0:T(8,128)S(1)} %broadcast.5.modes_y_ref, f32[7,16,128]{2,1,0:T(8,128)S(1)} %broadcast.7.modes_z_ref), custom_call_target="tpu_custom_call" | custom-call | flops 15032385536 | bytes 2555904 | tf_op jit(solution)/shard_map/spread/pallas_call | solution.py:289
  73.2 13.1 %solve.1.refs_1_ = f32[3,1032,512]{2,1,0:T(8,128)S(1)} custom-call(s32[32]{0:T(128)S(1)} %broadcast_xor_fusion.ids_ref, f32[1,120,512]{2,1,0:T(8,128)S(1)} %get-tuple-element.60.refs_0_, f32[3,120,512]{2,1,0:T(8,128)S(1)} %get-tuple-element.61.refs_1_, f32[4,120,512]{2,1,0:T(8,128)S(1)} %get-tuple-element.62.refs_2_, ...), custom_call_target="tpu_custom_call" | custom-call | flops 3623878656 | bytes 12582912 | tf_op jit(solution)/shard_map/solve/pallas_call | solution.py:409
  86.3 10.7 %interpolate.7 = f32[8,3,2048]{2,1,0:T(4,128)S(1)} custom-call(s32[32]{0:T(128)S(1)} %broadcast_xor_fusion.ids_ref, f32[8,8,2304]{2,1,0:T(8,128)S(1)} %collective-permute-done.5.points_ref, f32[8,48,2048]{2,1,0:T(8,128)S(1)} %get-tuple-element.59.refs_0_, f32[3,1032,512]{2,1,0:T(8,128)S(1)} %solve.1.refs_1_), custom_call_target="tpu_custom_call" | custom-call | flops 5368709120 | bytes 786432 | tf_op jit(solution)/shard_map/interpolate/pallas_call | solution.py:478
  97.4 10.5 %interpolate.8 = f32[8,3,2048]{2,1,0:T(4,128)S(1)} custom-call(s32[32]{0:T(128)S(1)} %broadcast_xor_fusion.ids_ref, f32[8,8,2304]{2,1,0:T(8,128)S(1)} %collective-permute-done.4.points_ref, f32[8,48,2048]{2,1,0:T(8,128)S(1)} %get-tuple-element.68.refs_0_, f32[3,1032,512]{2,1,0:T(8,128)S(1)} %solve.1.refs_1_), custom_call_target="tpu_custom_call" | custom-call | flops 5368709120 | bytes 786432 | tf_op jit(solution)/shard_map/interpolate/pallas_call | solution.py:478
  108.6 10.5 %interpolate.9 = f32[8,3,2048]{2,1,0:T(4,128)S(1)} custom-call(s32[32]{0:T(128)S(1)} %broadcast_xor_fusion.ids_ref, f32[8,8,2304]{2,1,0:T(8,128)S(1)} %collective-permute-done.6.points_ref, f32[8,48,2048]{2,1,0:T(8,128)S(1)} %get-tuple-element.72.refs_0_, f32[3,1032,512]{2,1,0:T(8,128)S(1)} %solve.1.refs_1_), custom_call_target="tpu_custom_call" | custom-call | flops 5368709120 | bytes 786432 | tf_op jit(solution)/shard_map/interpolate/pallas_call | solution.py:478
  119.2 5.5 %interpolate.10 = f32[4,3,2048]{2,1,0:T(4,128)S(1)} custom-call(s32[32]{0:T(128)S(1)} %broadcast_xor_fusion.ids_ref, f32[4,8,2304]{2,1,0:T(8,128)S(1)} %collective-permute-done.3.points_ref, f32[4,48,2048]{2,1,0:T(8,128)S(1)} %get-tuple-element.75.refs_0_, f32[3,1032,512]{2,1,0:T(8,128)S(1)} %solve.1.refs_1_), custom_call_target="tpu_custom_call" | custom-call | flops 2684354560 | bytes 393216 | tf_op jit(solution)/shard_map/interpolate/pallas_call | solution.py:478
  124.9 1.6 %collective-permute-start.10 = (f32[4,3,2048]{2,1,0:T(4,128)S(1)}, f32[4,3,2048]{2,1,0:T(4,128)S(1)}, u32[]{:S(2)}, u32[]{:S(2)}) collective-permute-start(f32[4,3,2048]{2,1,0:T(4,128)S(1)} %slice_add_fusion.1), channel_id=1, source_target_pairs={{0,2},{1,3},{2,0},{3,1},{4,6},{5,7},{6,4},{7,5},{8,10},{9,11},{10,... | collective-permute-start | bytes 294920 | tf_op jit(solution)/shard_map/ppermute | solution.py:568
  126.5 3.0 %interpolate.11 = f32[2,3,2048]{2,1,0:T(4,128)S(1)} custom-call(s32[32]{0:T(128)S(1)} %broadcast_xor_fusion.ids_ref, f32[3,8,2304]{2,1,0:T(8,128)S(1)} %get-tuple-element.93.points_ref, f32[3,48,2048]{2,1,0:T(8,128)S(1)} %get-tuple-element.81.refs_0_, f32[3,1032,512]{2,1,0:T(8,128)S(1)} %solve.1.refs_1_), custom_call_target="tpu_custom_call" | custom-call | flops 1342177280 | bytes 196608 | tf_op jit(solution)/shard_map/interpolate/pallas_call | solution.py:478
  129.5 1.3 collective-permute-done.10
  130.9 1.8 %interpolate.12 = f32[1,3,2048]{2,1,0:T(4,128)S(1)} custom-call(s32[32]{0:T(128)S(1)} %broadcast_xor_fusion.ids_ref, f32[3,8,2304]{2,1,0:T(8,128)S(1)} %get-tuple-element.93.points_ref, f32[3,48,2048]{2,1,0:T(8,128)S(1)} %get-tuple-element.81.refs_0_, f32[3,1032,512]{2,1,0:T(8,128)S(1)} %solve.1.refs_1_), custom_call_target="tpu_custom_call" | custom-call | flops 671088640 | bytes 98304 | tf_op jit(solution)/shard_map/interpolate/pallas_call | solution.py:478
  132.7 2.5 %collective-permute-start.11 = (f32[2,3,2048]{2,1,0:T(4,128)S(1)}, f32[2,3,2048]{2,1,0:T(4,128)S(1)}, u32[]{:S(2)}, u32[]{:S(2)}) collective-permute-start(f32[2,3,2048]{2,1,0:T(4,128)S(1)} %slice_add_fusion.2), channel_id=1, source_target_pairs={{0,8},{1,9},{2,10},{3,11},{4,12},{5,13},{6,14},{7,15},{8,0},{9,1},... | collective-permute-start | bytes 147464 | tf_op jit(solution)/shard_map/ppermute | solution.py:568
  135.2 1.8 %interpolate.13 = f32[1,3,2048]{2,1,0:T(4,128)S(1)} custom-call(s32[32]{0:T(128)S(1)} %broadcast_xor_fusion.ids_ref, f32[1,8,2304]{2,1,0:T(8,128)S(1)} %copy-done.3, f32[1,48,2048]{2,1,0:T(8,128)S(1)} %get-tuple-element.86.refs_0_, f32[3,1032,512]{2,1,0:T(8,128)S(1)} %solve.1.refs_1_), custom_call_target="tpu_custom_call" | custom-call | flops 671088640 | bytes 98304 | tf_op jit(solution)/shard_map/interpolate/pallas_call | solution.py:478
  136.9 2.0 %collective-permute-done.11 = f32[2,3,2048]{2,1,0:T(4,128)S(1)} collective-permute-done((f32[2,3,2048]{2,1,0:T(4,128)S(1)}, f32[2,3,2048]{2,1,0:T(4,128)S(1)}, u32[]{:S(2)}, u32[]{:S(2)}) %collective-permute-start.11) | collective-permute-done | bytes 49184 | tf_op jit(solution)/shard_map/ppermute | solution.py:568
  139.6 7.5 %near.1 = f32[3,2048]{1,0:T(4,128)S(1)} custom-call(s32[96]{0:T(128)S(1)} %reshape.8.pairs_ref, s32[1]{0:T(128)S(6)} %copy.22.count_ref, f32[1,8,2304]{2,1,0:T(8,128)S(1)} %copy-done.3, f32[9,2048,128]{2,1,0:T(8,128)S(1)} %get-tuple-element.92.wide_ref), custom_call_target="tpu_custom_call" | custom-call | flops 4718592000 | bytes 98304 | tf_op jit(solution)/shard_map/near/pallas_call | solution.py:84
  (51 shorter events, 9.1 us)
Async XLA Ops:
  1.4 13.6 %collective-permute-start.2 = (f32[1,8,2304]{2,1,0:T(8,128)}, f32[1,8,2304]{2,1,0:T(8,128)S(1)}, u32[]{:S(2)}, u32[]{:S(2)}) collective-permute-start(f32[1,8,2304]{2,1,0:T(8,128)} %pack.1.points_ref.refs_0_.own_ref), channel_id=1, source_target_pairs={{0,12},{1,13},{2,14},{3,15},{4,8},{5,9},{6,10},{7,11},{8,4},{9,5},... | collective-permute-start | bytes 221192 | tf_op jit(solution)/shard_map/ppermute | solution.py:568
  6.5 8.5 %collective-permute-start.1 = (f32[1,8,2304]{2,1,0:T(8,128)}, f32[1,8,2304]{2,1,0:T(8,128)S(1)}, u32[]{:S(2)}, u32[]{:S(2)}) collective-permute-start(f32[1,8,2304]{2,1,0:T(8,128)} %pack.1.points_ref.refs_0_.own_ref), channel_id=1, source_target_pairs={{0,8},{1,9},{2,10},{3,11},{4,12},{5,13},{6,14},{7,15},{8,0},{9,1},... | collective-permute-start | bytes 221192 | tf_op jit(solution)/shard_map/ppermute | solution.py:568
  6.5 8.5 %collective-permute-start = (f32[1,8,2304]{2,1,0:T(8,128)}, f32[1,8,2304]{2,1,0:T(8,128)S(1)}, u32[]{:S(2)}, u32[]{:S(2)}) collective-permute-start(f32[1,8,2304]{2,1,0:T(8,128)} %pack.1.points_ref.refs_0_.own_ref), channel_id=1, source_target_pairs={{0,4},{1,5},{2,6},{3,7},{4,0},{5,1},{6,2},{7,3},{8,12},{9,13},{10,... | collective-permute-start | bytes 221192 | tf_op jit(solution)/shard_map/ppermute | solution.py:568
  11.7 0.9 copy-start.2
  15.0 8.3 %collective-permute-start.3 = (f32[4,8,2304]{2,1,0:T(8,128)S(1)}, f32[4,8,2304]{2,1,0:T(8,128)S(1)}, u32[]{:S(2)}, u32[]{:S(2)}) collective-permute-start(f32[4,8,2304]{2,1,0:T(8,128)S(1)} %pad_maximum_fusion), channel_id=1, source_target_pairs={{0,2},{1,3},{2,0},{3,1},{4,6},{5,7},{6,4},{7,5},{8,10},{9,11},{10,... | collective-permute-start | bytes 884744 | tf_op jit(solution)/shard_map/ppermute | solution.py:568
  23.3 8.5 %copy-start.3 = (f32[1,8,2304]{2,1,0:T(8,128)S(1)}, f32[1,8,2304]{2,1,0:T(8,128)}, u32[]{:S(2)}) copy-start(f32[1,8,2304]{2,1,0:T(8,128)} %pack.1.points_ref.refs_0_.own_ref) | copy-start | bytes 221188
  23.3 8.5 %collective-permute-start.6 = (f32[8,8,2304]{2,1,0:T(8,128)S(1)}, f32[8,8,2304]{2,1,0:T(8,128)S(1)}, u32[]{:S(2)}, u32[]{:S(2)}) collective-permute-start(f32[8,8,2304]{2,1,0:T(8,128)S(1)} %constant_dynamic-update-slice_fusion), channel_id=1, source_target_pairs={{0,1},{1,0},{2,3},{3,2},{4,5},{5,4},{6,7},{7,6},{8,9},{9,8},{10,11... | collective-permute-start | bytes 1769480 | tf_op jit(solution)/shard_map/ppermute | solution.py:568
  23.4 22.2 %collective-permute-start.4 = (f32[8,8,2304]{2,1,0:T(8,128)S(1)}, f32[8,8,2304]{2,1,0:T(8,128)S(1)}, u32[]{:S(2)}, u32[]{:S(2)}) collective-permute-start(f32[8,8,2304]{2,1,0:T(8,128)S(1)} %constant_dynamic-update-slice_fusion), channel_id=1, source_target_pairs={{0,16},{1,17},{2,18},{3,19},{4,20},{5,21},{6,22},{7,23},{8,24},{9,... | collective-permute-start | bytes 1769480 | tf_op jit(solution)/shard_map/ppermute | solution.py:568
  45.6 13.9 %collective-permute-start.5 = (f32[8,8,2304]{2,1,0:T(8,128)S(1)}, f32[8,8,2304]{2,1,0:T(8,128)S(1)}, u32[]{:S(2)}, u32[]{:S(2)}) collective-permute-start(f32[8,8,2304]{2,1,0:T(8,128)S(1)} %collective-permute-done.4.points_ref), channel_id=1, source_target_pairs={{0,1},{1,0},{2,3},{3,2},{4,5},{5,4},{6,7},{7,6},{8,9},{9,8},{10,11... | collective-permute-start | bytes 1769480 | tf_op jit(solution)/shard_map/ppermute | solution.py:568
  59.5 13.7 %copy-start = (bf16[512,1536]{1,0:T(8,128)(2,1)S(1)}, bf16[512,1536]{1,0:T(8,128)(2,1)}, u32[]{:S(2)}) copy-start(bf16[512,1536]{1,0:T(8,128)(2,1)} %constant.76.clone.refs_9_) | copy-start | bytes 4718596
  59.5 13.7 %copy-start.1 = (bf16[512,1536]{1,0:T(8,128)(2,1)S(1)}, bf16[512,1536]{1,0:T(8,128)(2,1)}, u32[]{:S(2)}) copy-start(bf16[512,1536]{1,0:T(8,128)(2,1)} %constant.74.clone.refs_7_) | copy-start | bytes 4718596
  59.5 13.7 %copy-start.4 = (bf16[2,256,768]{2,1,0:T(8,128)(2,1)S(1)}, bf16[2,256,768]{2,1,0:T(8,128)(2,1)}, u32[]{:S(2)}) copy-start(bf16[2,256,768]{2,1,0:T(8,128)(2,1)} %constant.75.clone.refs_8_) | copy-start | bytes 2359300
  59.5 13.7 %copy-start.5 = (bf16[2,256,768]{2,1,0:T(8,128)(2,1)S(1)}, bf16[2,256,768]{2,1,0:T(8,128)(2,1)}, u32[]{:S(2)}) copy-start(bf16[2,256,768]{2,1,0:T(8,128)(2,1)} %constant.73.clone.refs_6_) | copy-start | bytes 2359300
  97.0 10.9 %collective-permute-start.7 = (f32[8,3,2048]{2,1,0:T(4,128)S(1)}, f32[8,3,2048]{2,1,0:T(4,128)S(1)}, u32[]{:S(2)}, u32[]{:S(2)}) collective-permute-start(f32[8,3,2048]{2,1,0:T(4,128)S(1)} %interpolate.7), channel_id=1, source_target_pairs={{0,1},{1,0},{2,3},{3,2},{4,5},{5,4},{6,7},{7,6},{8,9},{9,8},{10,11... | collective-permute-start | bytes 589832 | tf_op jit(solution)/shard_map/ppermute | solution.py:568
  108.0 11.1 %collective-permute-start.8 = (f32[8,3,2048]{2,1,0:T(4,128)S(1)}, f32[8,3,2048]{2,1,0:T(4,128)S(1)}, u32[]{:S(2)}, u32[]{:S(2)}) collective-permute-start(f32[8,3,2048]{2,1,0:T(4,128)S(1)} %add.61), channel_id=1, source_target_pairs={{0,16},{1,17},{2,18},{3,19},{4,20},{5,21},{6,22},{7,23},{8,24},{9,... | collective-permute-start | bytes 589832 | tf_op jit(solution)/shard_map/ppermute | solution.py:568
  119.2 5.6 %collective-permute-start.9 = (f32[8,3,2048]{2,1,0:T(4,128)S(1)}, f32[8,3,2048]{2,1,0:T(4,128)S(1)}, u32[]{:S(2)}, u32[]{:S(2)}) collective-permute-start(f32[8,3,2048]{2,1,0:T(4,128)S(1)} %interpolate.9), channel_id=1, source_target_pairs={{0,1},{1,0},{2,3},{3,2},{4,5},{5,4},{6,7},{7,6},{8,9},{9,8},{10,11... | collective-permute-start | bytes 589832 | tf_op jit(solution)/shard_map/ppermute | solution.py:568
  124.9 5.9 %collective-permute-start.10 = (f32[4,3,2048]{2,1,0:T(4,128)S(1)}, f32[4,3,2048]{2,1,0:T(4,128)S(1)}, u32[]{:S(2)}, u32[]{:S(2)}) collective-permute-start(f32[4,3,2048]{2,1,0:T(4,128)S(1)} %slice_add_fusion.1), channel_id=1, source_target_pairs={{0,2},{1,3},{2,0},{3,1},{4,6},{5,7},{6,4},{7,5},{8,10},{9,11},{10,... | collective-permute-start | bytes 294920 | tf_op jit(solution)/shard_map/ppermute | solution.py:568
  132.7 6.3 %collective-permute-start.11 = (f32[2,3,2048]{2,1,0:T(4,128)S(1)}, f32[2,3,2048]{2,1,0:T(4,128)S(1)}, u32[]{:S(2)}, u32[]{:S(2)}) collective-permute-start(f32[2,3,2048]{2,1,0:T(4,128)S(1)} %slice_add_fusion.2), channel_id=1, source_target_pairs={{0,8},{1,9},{2,10},{3,11},{4,12},{5,13},{6,14},{7,15},{8,0},{9,1},... | collective-permute-start | bytes 147464 | tf_op jit(solution)/shard_map/ppermute | solution.py:568
  139.0 8.1 %collective-permute-start.12 = (f32[1,3,2048]{2,1,0:T(4,128)S(1)}, f32[1,3,2048]{2,1,0:T(4,128)S(1)}, u32[]{:S(2)}, u32[]{:S(2)}) collective-permute-start(f32[1,3,2048]{2,1,0:T(4,128)S(1)} %fusion), channel_id=1, source_target_pairs={{0,4},{1,5},{2,6},{3,7},{4,0},{5,1},{6,2},{7,3},{8,12},{9,13},{10,... | collective-permute-start | bytes 73736 | tf_op jit(solution)/shard_map/ppermute | solution.py:568

commit v5 on v4

--- a/solution.py
+++ b/solution.py
@@ -489,7 +489,7 @@
         scratch_shapes=[pltpu.VMEM((2 * LANES, cols), BF16)],
         compiler_params=pltpu.CompilerParams(vmem_limit_bytes=GATHER_LIMIT),
         cost_estimate=pl.CostEstimate(
-            flops=blocks * count * cols * LANES * 5,
+            flops=blocks * count * cols * LANES * (14 if blocks > 1 else 2),
             bytes_accessed=blocks * 12 * count * 4,
             transcendentals=0,
         ),

time: 147 us -> 145 us (0.986)
  the two profiles are of different devices: /device:TPU:0 before, /device:TPU:20 now
where the time goes in v5:
time: 145 us
  Pallas kernels  120 us (83%)
  starting transfers between devices  12.8 us (9%)
  local copies, waits for them, and re-layouts  5.04 us (3%)
  waiting for transfers between devices  4.16 us (3%)
  other arithmetic  1.58 us (1%)
    pallas_call x6, Pallas kernels, spread(): pl.pallas_call(functools.partial(spread_kernel, rows, tiles), grid=(block...  54.7 us
    pallas_call x7, Pallas kernels, gather(): pl.pallas_call(functools.partial(gather_kernel, planes, rows, before, kep...  43.8 us
    pallas_call x1, Pallas kernels, solve(): pl.pallas_call(functools.partial(solve_kernel, planes, rows, len(pieces))...  12.9 us
    ppermute x13, starting transfers between devices, from_flipped(): return lax.ppermute(values, ('group', 'dev'), pairs)  12.8 us
    pallas_call x1, Pallas kernels, near_field(): pl.pallas_call(near_kernel, in_specs=[smem, smem, vmem, vmem], out_specs=...  7.49 us
    ppermute x13, waiting for transfers between devices, from_flipped(): return lax.ppermute(values, ('group', 'dev'), pairs)  4.16 us
  transfers between devices with their start and end apart: 13, of which 3 were waited for; matrix products, arithmetic and copies ran while one was open for 3% of the time, Pallas kernels for 56%

profile of v5, /device:TPU:20, one launch (start us, length us, event | category | flops | bytes accessed | tf_op | source)
XLA Modules:
  0.0 144.9 jit_solution(7658870227441174492)
XLA Ops:
  0.0 1.4 pack.1.points_ref.refs_0_.own_ref
  1.9 3.5 %collective-permute-start.1 = (f32[1,8,2304]{2,1,0:T(8,128)}, f32[1,8,2304]{2,1,0:T(8,128)S(1)}, u32[]{:S(2)}, u32[]{:S(2)}) collective-permute-start(f32[1,8,2304]{2,1,0:T(8,128)} %pack.1.points_ref.refs_0_.own_ref), channel_id=1, source_target_pairs={{0,8},{1,9},{2,10},{3,11},{4,12},{5,13},{6,14},{7,15},{8,0},{9,1},... | collective-permute-start | bytes 221192 | tf_op jit(solution)/shard_map/ppermute | solution.py:568
  11.0 1.7 %spread.6 = (f32[1,120,512]{2,1,0:T(8,128)S(1)}, f32[1,48,2048]{2,1,0:T(8,128)S(1)}) custom-call(f32[1,8,2304]{2,1,0:T(8,128)S(1)} %copy-done.2, f32[7,8,128]{2,1,0:T(8,128)S(1)} %broadcast.5.modes_y_ref, f32[7,16,128]{2,1,0:T(8,128)S(1)} %broadcast.7.modes_z_ref), custom_call_target="tpu_custom_call" | custom-call | flops 1879048192 | bytes 319488 | tf_op jit(solution)/shard_map/spread/pallas_call | solution.py:289
  13.4 1.6 %collective-permute-start.3 = (f32[4,8,2304]{2,1,0:T(8,128)S(1)}, f32[4,8,2304]{2,1,0:T(8,128)S(1)}, u32[]{:S(2)}, u32[]{:S(2)}) collective-permute-start(f32[4,8,2304]{2,1,0:T(8,128)S(1)} %pad_maximum_fusion), channel_id=1, source_target_pairs={{0,2},{1,3},{2,0},{3,1},{4,6},{5,7},{6,4},{7,5},{8,10},{9,11},{10,... | collective-permute-start | bytes 884744 | tf_op jit(solution)/shard_map/ppermute | solution.py:568
  15.0 5.1 %spread.7 = (f32[3,120,512]{2,1,0:T(8,128)S(1)}, f32[3,48,2048]{2,1,0:T(8,128)S(1)}) custom-call(f32[3,8,2304]{2,1,0:T(8,128)S(1)} %get-tuple-element.93.points_ref, f32[7,8,128]{2,1,0:T(8,128)S(1)} %broadcast.5.modes_y_ref, f32[7,16,128]{2,1,0:T(8,128)S(1)} %broadcast.7.modes_z_ref), custom_call_target="tpu_custom_call" | custom-call | flops 5637144576 | bytes 958464 | tf_op jit(solution)/shard_map/spread/pallas_call | solution.py:289
  20.1 1.5 %collective-permute-done.3.points_ref = f32[4,8,2304]{2,1,0:T(8,128)S(1)} collective-permute-done((f32[4,8,2304]{2,1,0:T(8,128)S(1)}, f32[4,8,2304]{2,1,0:T(8,128)S(1)}, u32[]{:S(2)}, u32[]{:S(2)}) %collective-permute-start.3) | collective-permute-done | bytes 294944 | tf_op jit(solution)/shard_map/ppermute | solution.py:568
  22.3 6.8 %spread.8 = (f32[4,120,512]{2,1,0:T(8,128)S(1)}, f32[4,48,2048]{2,1,0:T(8,128)S(1)}) custom-call(f32[4,8,2304]{2,1,0:T(8,128)S(1)} %collective-permute-done.3.points_ref, f32[7,8,128]{2,1,0:T(8,128)S(1)} %broadcast.5.modes_y_ref, f32[7,16,128]{2,1,0:T(8,128)S(1)} %broadcast.7.modes_z_ref), custom_call_target="tpu_custom_call" | custom-call | flops 7516192768 | bytes 1277952 | tf_op jit(solution)/shard_map/spread/pallas_call | solution.py:289
  29.2 13.8 %spread.9 = (f32[8,120,512]{2,1,0:T(8,128)S(1)}, f32[8,48,2048]{2,1,0:T(8,128)S(1)}, f32[9,2048,128]{2,1,0:T(8,128)S(1)}) custom-call(f32[8,8,2304]{2,1,0:T(8,128)S(1)} %collective-permute-done.6.points_ref, f32[7,8,128]{2,1,0:T(8,128)S(1)} %broadcast.5.modes_y_ref, f32[7,16,128]{2,1,0:T(8,128)S(1)} %broadcast.7.modes_z_ref, f32[1,8,2304]{2,1,0:T(8,128)S(1)} %copy-done.3), custom_call_target="tpu_custom_call" | custom-call | flops 15032385536 | bytes 2555904 | tf_op jit(solution)/shard_map/spread/pallas_call | solution.py:289
  43.2 13.6 %spread.10 = (f32[8,120,512]{2,1,0:T(8,128)S(1)}, f32[8,48,2048]{2,1,0:T(8,128)S(1)}) custom-call(f32[8,8,2304]{2,1,0:T(8,128)S(1)} %collective-permute-done.4.points_ref, f32[7,8,128]{2,1,0:T(8,128)S(1)} %broadcast.5.modes_y_ref, f32[7,16,128]{2,1,0:T(8,128)S(1)} %broadcast.7.modes_z_ref), custom_call_target="tpu_custom_call" | custom-call | flops 15032385536 | bytes 2555904 | tf_op jit(solution)/shard_map/spread/pallas_call | solution.py:289
  56.9 13.7 %spread.11 = (f32[8,120,512]{2,1,0:T(8,128)S(1)}, f32[8,48,2048]{2,1,0:T(8,128)S(1)}) custom-call(f32[8,8,2304]{2,1,0:T(8,128)S(1)} %collective-permute-done.5.points_ref, f32[7,8,128]{2,1,0:T(8,128)S(1)} %broadcast.5.modes_y_ref, f32[7,16,128]{2,1,0:T(8,128)S(1)} %broadcast.7.modes_z_ref), custom_call_target="tpu_custom_call" | custom-call | flops 15032385536 | bytes 2555904 | tf_op jit(solution)/shard_map/spread/pallas_call | solution.py:289
  70.6 12.9 %solve.1.refs_1_ = f32[3,1032,512]{2,1,0:T(8,128)S(1)} custom-call(s32[32]{0:T(128)S(1)} %broadcast_xor_fusion.ids_ref, f32[1,120,512]{2,1,0:T(8,128)S(1)} %get-tuple-element.60.refs_0_, f32[3,120,512]{2,1,0:T(8,128)S(1)} %get-tuple-element.61.refs_1_, f32[4,120,512]{2,1,0:T(8,128)S(1)} %get-tuple-element.62.refs_2_, ...), custom_call_target="tpu_custom_call" | custom-call | flops 3623878656 | bytes 12582912 | tf_op jit(solution)/shard_map/solve/pallas_call | solution.py:409
  83.5 10.7 %interpolate.7 = f32[8,3,2048]{2,1,0:T(4,128)S(1)} custom-call(s32[32]{0:T(128)S(1)} %broadcast_xor_fusion.ids_ref, f32[8,8,2304]{2,1,0:T(8,128)S(1)} %collective-permute-done.5.points_ref, f32[8,48,2048]{2,1,0:T(8,128)S(1)} %get-tuple-element.59.refs_0_, f32[3,1032,512]{2,1,0:T(8,128)S(1)} %solve.1.refs_1_), custom_call_target="tpu_custom_call" | custom-call | flops 15032385536 | bytes 786432 | tf_op jit(solution)/shard_map/interpolate/pallas_call | solution.py:478
  94.7 10.5 %interpolate.8 = f32[8,3,2048]{2,1,0:T(4,128)S(1)} custom-call(s32[32]{0:T(128)S(1)} %broadcast_xor_fusion.ids_ref, f32[8,8,2304]{2,1,0:T(8,128)S(1)} %collective-permute-done.4.points_ref, f32[8,48,2048]{2,1,0:T(8,128)S(1)} %get-tuple-element.68.refs_0_, f32[3,1032,512]{2,1,0:T(8,128)S(1)} %solve.1.refs_1_), custom_call_target="tpu_custom_call" | custom-call | flops 15032385536 | bytes 786432 | tf_op jit(solution)/shard_map/interpolate/pallas_call | solution.py:478
  105.3 1.6 %collective-permute-start.8 = (f32[8,3,2048]{2,1,0:T(4,128)S(1)}, f32[8,3,2048]{2,1,0:T(4,128)S(1)}, u32[]{:S(2)}, u32[]{:S(2)}) collective-permute-start(f32[8,3,2048]{2,1,0:T(4,128)S(1)} %add.61), channel_id=1, source_target_pairs={{0,16},{1,17},{2,18},{3,19},{4,20},{5,21},{6,22},{7,23},{8,24},{9,... | collective-permute-start | bytes 589832 | tf_op jit(solution)/shard_map/ppermute | solution.py:568
  106.9 10.5 %interpolate.9 = f32[8,3,2048]{2,1,0:T(4,128)S(1)} custom-call(s32[32]{0:T(128)S(1)} %broadcast_xor_fusion.ids_ref, f32[8,8,2304]{2,1,0:T(8,128)S(1)} %collective-permute-done.6.points_ref, f32[8,48,2048]{2,1,0:T(8,128)S(1)} %get-tuple-element.72.refs_0_, f32[3,1032,512]{2,1,0:T(8,128)S(1)} %solve.1.refs_1_), custom_call_target="tpu_custom_call" | custom-call | flops 15032385536 | bytes 786432 | tf_op jit(solution)/shard_map/interpolate/pallas_call | solution.py:478
  117.5 5.5 %interpolate.10 = f32[4,3,2048]{2,1,0:T(4,128)S(1)} custom-call(s32[32]{0:T(128)S(1)} %broadcast_xor_fusion.ids_ref, f32[4,8,2304]{2,1,0:T(8,128)S(1)} %collective-permute-done.3.points_ref, f32[4,48,2048]{2,1,0:T(8,128)S(1)} %get-tuple-element.75.refs_0_, f32[3,1032,512]{2,1,0:T(8,128)S(1)} %solve.1.refs_1_), custom_call_target="tpu_custom_call" | custom-call | flops 7516192768 | bytes 393216 | tf_op jit(solution)/shard_map/interpolate/pallas_call | solution.py:478
  123.2 1.6 %collective-permute-start.10 = (f32[4,3,2048]{2,1,0:T(4,128)S(1)}, f32[4,3,2048]{2,1,0:T(4,128)S(1)}, u32[]{:S(2)}, u32[]{:S(2)}) collective-permute-start(f32[4,3,2048]{2,1,0:T(4,128)S(1)} %slice_add_fusion.1), channel_id=1, source_target_pairs={{0,2},{1,3},{2,0},{3,1},{4,6},{5,7},{6,4},{7,5},{8,10},{9,11},{10,... | collective-permute-start | bytes 294920 | tf_op jit(solution)/shard_map/ppermute | solution.py:568
  124.7 3.0 %interpolate.11 = f32[2,3,2048]{2,1,0:T(4,128)S(1)} custom-call(s32[32]{0:T(128)S(1)} %broadcast_xor_fusion.ids_ref, f32[3,8,2304]{2,1,0:T(8,128)S(1)} %get-tuple-element.93.points_ref, f32[3,48,2048]{2,1,0:T(8,128)S(1)} %get-tuple-element.81.refs_0_, f32[3,1032,512]{2,1,0:T(8,128)S(1)} %solve.1.refs_1_), custom_call_target="tpu_custom_call" | custom-call | flops 3758096384 | bytes 196608 | tf_op jit(solution)/shard_map/interpolate/pallas_call | solution.py:478
  127.7 1.4 collective-permute-done.10
  129.8 1.8 %interpolate.12 = f32[1,3,2048]{2,1,0:T(4,128)S(1)} custom-call(s32[32]{0:T(128)S(1)} %broadcast_xor_fusion.ids_ref, f32[3,8,2304]{2,1,0:T(8,128)S(1)} %get-tuple-element.93.points_ref, f32[3,48,2048]{2,1,0:T(8,128)S(1)} %get-tuple-element.81.refs_0_, f32[3,1032,512]{2,1,0:T(8,128)S(1)} %solve.1.refs_1_), custom_call_target="tpu_custom_call" | custom-call | flops 268435456 | bytes 98304 | tf_op jit(solution)/shard_map/interpolate/pallas_call | solution.py:478
  131.6 1.8 %interpolate.13 = f32[1,3,2048]{2,1,0:T(4,128)S(1)} custom-call(s32[32]{0:T(128)S(1)} %broadcast_xor_fusion.ids_ref, f32[1,8,2304]{2,1,0:T(8,128)S(1)} %copy-done.3, f32[1,48,2048]{2,1,0:T(8,128)S(1)} %get-tuple-element.86.refs_0_, f32[3,1032,512]{2,1,0:T(8,128)S(1)} %solve.1.refs_1_), custom_call_target="tpu_custom_call" | custom-call | flops 268435456 | bytes 98304 | tf_op jit(solution)/shard_map/interpolate/pallas_call | solution.py:478
  133.3 1.2 collective-permute-done.11
  134.5 2.3 %collective-permute-start.12 = (f32[1,3,2048]{2,1,0:T(4,128)S(1)}, f32[1,3,2048]{2,1,0:T(4,128)S(1)}, u32[]{:S(2)}, u32[]{:S(2)}) collective-permute-start(f32[1,3,2048]{2,1,0:T(4,128)S(1)} %fusion), channel_id=1, source_target_pairs={{0,4},{1,5},{2,6},{3,7},{4,0},{5,1},{6,2},{7,3},{8,12},{9,13},{10,... | collective-permute-start | bytes 73736 | tf_op jit(solution)/shard_map/ppermute | solution.py:568
  136.8 7.5 %near.1 = f32[3,2048]{1,0:T(4,128)S(1)} custom-call(s32[96]{0:T(128)S(1)} %reshape.8.pairs_ref, s32[1]{0:T(128)S(6)} %copy.22.count_ref, f32[1,8,2304]{2,1,0:T(8,128)S(1)} %copy-done.3, f32[9,2048,128]{2,1,0:T(8,128)S(1)} %get-tuple-element.92.wide_ref), custom_call_target="tpu_custom_call" | custom-call | flops 4718592000 | bytes 98304 | tf_op jit(solution)/shard_map/near/pallas_call | solution.py:84
  (51 shorter events, 9.1 us)
Async XLA Ops:
  1.4 11.9 %collective-permute-start.2 = (f32[1,8,2304]{2,1,0:T(8,128)}, f32[1,8,2304]{2,1,0:T(8,128)S(1)}, u32[]{:S(2)}, u32[]{:S(2)}) collective-permute-start(f32[1,8,2304]{2,1,0:T(8,128)} %pack.1.points_ref.refs_0_.own_ref), channel_id=1, source_target_pairs={{0,12},{1,13},{2,14},{3,15},{4,8},{5,9},{6,10},{7,11},{8,4},{9,5},... | collective-permute-start | bytes 221192 | tf_op jit(solution)/shard_map/ppermute | solution.py:568
  1.9 11.5 %collective-permute-start.1 = (f32[1,8,2304]{2,1,0:T(8,128)}, f32[1,8,2304]{2,1,0:T(8,128)S(1)}, u32[]{:S(2)}, u32[]{:S(2)}) collective-permute-start(f32[1,8,2304]{2,1,0:T(8,128)} %pack.1.points_ref.refs_0_.own_ref), channel_id=1, source_target_pairs={{0,8},{1,9},{2,10},{3,11},{4,12},{5,13},{6,14},{7,15},{8,0},{9,1},... | collective-permute-start | bytes 221192 | tf_op jit(solution)/shard_map/ppermute | solution.py:568
  5.4 8.0 %collective-permute-start = (f32[1,8,2304]{2,1,0:T(8,128)}, f32[1,8,2304]{2,1,0:T(8,128)S(1)}, u32[]{:S(2)}, u32[]{:S(2)}) collective-permute-start(f32[1,8,2304]{2,1,0:T(8,128)} %pack.1.points_ref.refs_0_.own_ref), channel_id=1, source_target_pairs={{0,4},{1,5},{2,6},{3,7},{4,0},{5,1},{6,2},{7,3},{8,12},{9,13},{10,... | collective-permute-start | bytes 221192 | tf_op jit(solution)/shard_map/ppermute | solution.py:568
  10.1 0.9 copy-start.2
  13.4 8.3 %collective-permute-start.3 = (f32[4,8,2304]{2,1,0:T(8,128)S(1)}, f32[4,8,2304]{2,1,0:T(8,128)S(1)}, u32[]{:S(2)}, u32[]{:S(2)}) collective-permute-start(f32[4,8,2304]{2,1,0:T(8,128)S(1)} %pad_maximum_fusion), channel_id=1, source_target_pairs={{0,2},{1,3},{2,0},{3,1},{4,6},{5,7},{6,4},{7,5},{8,10},{9,11},{10,... | collective-permute-start | bytes 884744 | tf_op jit(solution)/shard_map/ppermute | solution.py:568
  21.7 7.5 %copy-start.3 = (f32[1,8,2304]{2,1,0:T(8,128)S(1)}, f32[1,8,2304]{2,1,0:T(8,128)}, u32[]{:S(2)}) copy-start(f32[1,8,2304]{2,1,0:T(8,128)} %pack.1.points_ref.refs_0_.own_ref) | copy-start | bytes 221188
  21.7 7.5 %collective-permute-start.6 = (f32[8,8,2304]{2,1,0:T(8,128)S(1)}, f32[8,8,2304]{2,1,0:T(8,128)S(1)}, u32[]{:S(2)}, u32[]{:S(2)}) collective-permute-start(f32[8,8,2304]{2,1,0:T(8,128)S(1)} %constant_dynamic-update-slice_fusion), channel_id=1, source_target_pairs={{0,1},{1,0},{2,3},{3,2},{4,5},{5,4},{6,7},{7,6},{8,9},{9,8},{10,11... | collective-permute-start | bytes 1769480 | tf_op jit(solution)/shard_map/ppermute | solution.py:568
  21.8 21.2 %collective-permute-start.4 = (f32[8,8,2304]{2,1,0:T(8,128)S(1)}, f32[8,8,2304]{2,1,0:T(8,128)S(1)}, u32[]{:S(2)}, u32[]{:S(2)}) collective-permute-start(f32[8,8,2304]{2,1,0:T(8,128)S(1)} %constant_dynamic-update-slice_fusion), channel_id=1, source_target_pairs={{0,16},{1,17},{2,18},{3,19},{4,20},{5,21},{6,22},{7,23},{8,24},{9,... | collective-permute-start | bytes 1769480 | tf_op jit(solution)/shard_map/ppermute | solution.py:568
  43.0 13.9 %collective-permute-start.5 = (f32[8,8,2304]{2,1,0:T(8,128)S(1)}, f32[8,8,2304]{2,1,0:T(8,128)S(1)}, u32[]{:S(2)}, u32[]{:S(2)}) collective-permute-start(f32[8,8,2304]{2,1,0:T(8,128)S(1)} %collective-permute-done.4.points_ref), channel_id=1, source_target_pairs={{0,1},{1,0},{2,3},{3,2},{4,5},{5,4},{6,7},{7,6},{8,9},{9,8},{10,11... | collective-permute-start | bytes 1769480 | tf_op jit(solution)/shard_map/ppermute | solution.py:568
  56.9 13.7 %copy-start = (bf16[512,1536]{1,0:T(8,128)(2,1)S(1)}, bf16[512,1536]{1,0:T(8,128)(2,1)}, u32[]{:S(2)}) copy-start(bf16[512,1536]{1,0:T(8,128)(2,1)} %constant.76.clone.refs_9_) | copy-start | bytes 4718596
  56.9 13.7 %copy-start.1 = (bf16[512,1536]{1,0:T(8,128)(2,1)S(1)}, bf16[512,1536]{1,0:T(8,128)(2,1)}, u32[]{:S(2)}) copy-start(bf16[512,1536]{1,0:T(8,128)(2,1)} %constant.74.clone.refs_7_) | copy-start | bytes 4718596
  56.9 13.7 %copy-start.4 = (bf16[2,256,768]{2,1,0:T(8,128)(2,1)S(1)}, bf16[2,256,768]{2,1,0:T(8,128)(2,1)}, u32[]{:S(2)}) copy-start(bf16[2,256,768]{2,1,0:T(8,128)(2,1)} %constant.75.clone.refs_8_) | copy-start | bytes 2359300
  56.9 13.7 %copy-start.5 = (bf16[2,256,768]{2,1,0:T(8,128)(2,1)S(1)}, bf16[2,256,768]{2,1,0:T(8,128)(2,1)}, u32[]{:S(2)}) copy-start(bf16[2,256,768]{2,1,0:T(8,128)(2,1)} %constant.73.clone.refs_6_) | copy-start | bytes 2359300
  94.3 10.9 %collective-permute-start.7 = (f32[8,3,2048]{2,1,0:T(4,128)S(1)}, f32[8,3,2048]{2,1,0:T(4,128)S(1)}, u32[]{:S(2)}, u32[]{:S(2)}) collective-permute-start(f32[8,3,2048]{2,1,0:T(4,128)S(1)} %interpolate.7), channel_id=1, source_target_pairs={{0,1},{1,0},{2,3},{3,2},{4,5},{5,4},{6,7},{7,6},{8,9},{9,8},{10,11... | collective-permute-start | bytes 589832 | tf_op jit(solution)/shard_map/ppermute | solution.py:568
  105.3 12.1 %collective-permute-start.8 = (f32[8,3,2048]{2,1,0:T(4,128)S(1)}, f32[8,3,2048]{2,1,0:T(4,128)S(1)}, u32[]{:S(2)}, u32[]{:S(2)}) collective-permute-start(f32[8,3,2048]{2,1,0:T(4,128)S(1)} %add.61), channel_id=1, source_target_pairs={{0,16},{1,17},{2,18},{3,19},{4,20},{5,21},{6,22},{7,23},{8,24},{9,... | collective-permute-start | bytes 589832 | tf_op jit(solution)/shard_map/ppermute | solution.py:568
  117.4 5.6 %collective-permute-start.9 = (f32[8,3,2048]{2,1,0:T(4,128)S(1)}, f32[8,3,2048]{2,1,0:T(4,128)S(1)}, u32[]{:S(2)}, u32[]{:S(2)}) collective-permute-start(f32[8,3,2048]{2,1,0:T(4,128)S(1)} %interpolate.9), channel_id=1, source_target_pairs={{0,1},{1,0},{2,3},{3,2},{4,5},{5,4},{6,7},{7,6},{8,9},{9,8},{10,11... | collective-permute-start | bytes 589832 | tf_op jit(solution)/shard_map/ppermute | solution.py:568
  123.2 5.9 %collective-permute-start.10 = (f32[4,3,2048]{2,1,0:T(4,128)S(1)}, f32[4,3,2048]{2,1,0:T(4,128)S(1)}, u32[]{:S(2)}, u32[]{:S(2)}) collective-permute-start(f32[4,3,2048]{2,1,0:T(4,128)S(1)} %slice_add_fusion.1), channel_id=1, source_target_pairs={{0,2},{1,3},{2,0},{3,1},{4,6},{5,7},{6,4},{7,5},{8,10},{9,11},{10,... | collective-permute-start | bytes 294920 | tf_op jit(solution)/shard_map/ppermute | solution.py:568
  129.2 5.3 %collective-permute-start.11 = (f32[2,3,2048]{2,1,0:T(4,128)S(1)}, f32[2,3,2048]{2,1,0:T(4,128)S(1)}, u32[]{:S(2)}, u32[]{:S(2)}) collective-permute-start(f32[2,3,2048]{2,1,0:T(4,128)S(1)} %slice_add_fusion.2), channel_id=1, source_target_pairs={{0,8},{1,9},{2,10},{3,11},{4,12},{5,13},{6,14},{7,15},{8,0},{9,1},... | collective-permute-start | bytes 147464 | tf_op jit(solution)/shard_map/ppermute | solution.py:568
  134.5 9.8 %collective-permute-start.12 = (f32[1,3,2048]{2,1,0:T(4,128)S(1)}, f32[1,3,2048]{2,1,0:T(4,128)S(1)}, u32[]{:S(2)}, u32[]{:S(2)}) collective-permute-start(f32[1,3,2048]{2,1,0:T(4,128)S(1)} %fusion), channel_id=1, source_target_pairs={{0,4},{1,5},{2,6},{3,7},{4,0},{5,1},{6,2},{7,3},{8,12},{9,13},{10,... | collective-permute-start | bytes 73736 | tf_op jit(solution)/shard_map/ppermute | solution.py:568
